TPU v7x, 512 devices: a whole 4x8x8 slice. The times are simulated.
512 devices in a mesh: grp: 8 (over y), cent: 64 (over x, z, core).
Axes of the slice: x: 4, y: 8, z: 8, core: 2. Of those that a mesh axis runs over, the one named last changes fastest.
Arguments:
- vectors: bfloat16 [16384, 768], P(('grp', 'cent')), may hold values from -6 to 6
- centroids: bfloat16 [131072, 768], P('cent'), may hold values from -6 to 6
- postings: bfloat16 [256, 128, 768], P('cent'), may hold values from -6 to 6
- fill: int32 [256], P('cent'), may hold values from 32 to 64
- assign: int32 [16384], P(('grp', 'cent')), may hold values from 0 to 255, as said below
- split_posts: int32 [128], P('cent'), may hold values from -1 to 3, as said below
- split_members: int32 [128, 128], P('cent'), may hold values from 0 to 1
- neigh_post: int32 [32768], P(('grp', 'cent')), may hold values from 0 to 3
- neigh_row: int32 [32768], P(('grp', 'cent')), may hold values from 0 to 31
- neigh_split: int32 [32768], P(('grp', 'cent')), may hold values from 0 to 1, as said below
- neigh_dest: int32 [32768], P(('grp', 'cent')), may hold values from 0 to 63, as said below
Outputs:
- best_score: float32 [16384], P(('grp', 'cent'))
- postings_out: bfloat16 [256, 128, 768], P('cent')
- new_fill: int32 [256], P('cent')
- split_centers: float32 [128, 2, 768], P('cent')
- moved_rows: bfloat16 [65536, 768], P(('grp', 'cent'))
- moved_scores: bfloat16 [2, 65536], P(None, ('grp', 'cent'))
Inputs may be any that keep to these rules, and one draw needn't show every extreme that they name: `assign`: global posting ids. Among one device's new vectors each centroid shard (id // 4) is named 0 or exactly 2 times; among those of the 8 devices that share a cent index it is named exactly 4 times; among those of the devices that share a grp index it is named exactly 32 times; every posting is named exactly 64 times in all. `split_posts`: each shard's block of 2 slots holds 1 to 2 distinct local postings first and -1 after them; some shard's block is full. `neigh_split`: names a slot of the device's centroid shard that holds a posting. `neigh_dest`: among one device's neighbor vectors each destination shard is named 0 or exactly 2 times.
All inputs are finite; a program needn't handle non-finite values.
Results may differ from a plain program's by a relative error of at most 0.0022.
Values may be sent and summed in bfloat16 or wider, within the bound.
No kernel may reach another device: no remote copies, remote signals or barrier semaphores. Data moves between devices by JAX's collectives and lax.ppermute only.
A program may use at most 64 MiB of HBM per device.

v0:
```python
import jax
import jax.numpy as jnp
from jax import lax
from jax.sharding import PartitionSpec as P

D = 768
ROWS = 128
ITERS = 2
SEND_CAP = 2


def center_update(rows_f, row_mask, weights, prior):
    first = row_mask * weights
    second = row_mask * (1.0 - weights)
    both = jnp.stack([first, second])
    sums = jnp.dot(both, rows_f, precision=lax.Precision.HIGHEST)
    totals = jnp.sum(both, axis=1)
    return (sums + prior[None, :]) / (totals[:, None] + 1.0)


def two_means(rows_f, count, members, prior):
    row_mask = (jnp.arange(rows_f.shape[0], dtype=jnp.int32) < count).astype(rows_f.dtype)
    weights = members.astype(rows_f.dtype)
    centers = center_update(rows_f, row_mask, weights, prior)
    for turn in range(ITERS):
        far_two = jnp.sum(jnp.square(rows_f - centers[1][None, :]), axis=1)
        far_one = jnp.sum(jnp.square(rows_f - centers[0][None, :]), axis=1)
        weights = jax.nn.sigmoid(0.125 * (far_two - far_one))
        centers = center_update(rows_f, row_mask, weights, prior)
    return centers


def slot_table(targets, dest_count, capacity):
    matches = (targets[:, None] == jnp.arange(dest_count, dtype=jnp.int32)[None, :]).astype(
        jnp.int32
    )
    earlier = jnp.cumsum(matches, axis=0) - matches
    position = jnp.sum(earlier * matches, axis=1)
    slot_index = jnp.where(targets >= 0, targets * capacity + position, -1)
    return slot_index[None, :] == jnp.arange(dest_count * capacity, dtype=jnp.int32)[:, None]


def route_rows(vec_rows, id_rows, targets, dest_count, capacity):
    table = slot_table(targets, dest_count, capacity)
    placed = jnp.dot(
        table.astype(jnp.bfloat16), vec_rows, preferred_element_type=jnp.float32
    ).astype(jnp.bfloat16)
    filled = jnp.any(table, axis=1)
    picked = jnp.sum(table[None, :, :].astype(jnp.int32) * id_rows[:, None, :], axis=2)
    picked = jnp.where(filled[None, :], picked, -1)
    placed = placed.reshape(dest_count, capacity, vec_rows.shape[1])
    return (placed, picked.reshape(-1, dest_count, capacity).transpose(1, 0, 2))


def shards(
    vectors,
    centroids,
    postings,
    fill,
    assign,
    split_posts,
    split_members,
    neigh_post,
    neigh_row,
    neigh_split,
    neigh_dest,
):
    cent_count = lax.axis_size("cent")
    cent_index = lax.axis_index("cent")
    grp_index = lax.axis_index("grp")
    vec_count = vectors.shape[0]
    post_count = postings.shape[0]
    blocks = centroids.reshape(-1, 256, D)
    global_index = (grp_index * cent_count + cent_index) * vec_count + jnp.arange(
        vec_count, dtype=jnp.int32
    )
    id_pairs = jnp.stack([assign, global_index])
    piece = lax.all_gather(vectors, "cent", axis=0, tiled=True)

    def scan_step(running, block):
        scores = lax.dot_general(
            piece, block, (((1,), (1,)), ((), ())), preferred_element_type=jnp.float32
        )
        return (jnp.maximum(running, jnp.max(scores, axis=1)), None)

    initial = jnp.full((piece.shape[0],), -jnp.inf, jnp.float32)
    local_best = lax.scan(scan_step, initial, blocks)[0]
    whole_best = lax.pmax(local_best, "cent")
    best_score = lax.dynamic_slice_in_dim(whole_best, cent_index * vec_count, vec_count)
    all_vectors, all_ids = (
        lax.all_gather(vectors, "grp", axis=0, tiled=True),
        lax.all_gather(id_pairs, "grp", axis=1, tiled=True),
    )
    capacity = all_vectors.shape[0] // cent_count
    placed, placed_ids = route_rows(
        all_vectors, all_ids, all_ids[0] // post_count, cent_count, capacity
    )
    got_rows, got_ids = (
        lax.all_to_all(placed, "cent", split_axis=0, concat_axis=0, tiled=True),
        lax.all_to_all(placed_ids, "cent", split_axis=0, concat_axis=0, tiled=True),
    )
    arrived = got_rows.reshape(-1, D)
    arrived_ids = got_ids.transpose(1, 0, 2).reshape(2, -1)
    arrived_post = arrived_ids[0]
    arrived_order = arrived_ids[1]
    is_valid = arrived_post >= 0
    local_post = jnp.where(is_valid, arrived_post - cent_index * post_count, -1)
    same_post = (local_post[:, None] == local_post[None, :]) & is_valid[:, None] & is_valid[None, :]
    before = same_post & (arrived_order[None, :] < arrived_order[:, None])
    arrive_rank = jnp.sum(before.astype(jnp.int32), axis=1)
    post_match = (local_post[:, None] == jnp.arange(post_count, dtype=jnp.int32)[None, :]).astype(
        jnp.int32
    )
    arrive_counts = jnp.sum(post_match, axis=0)
    start_row = jnp.sum(post_match * fill[None, :], axis=1)
    target_row = jnp.where(is_valid, local_post * ROWS + start_row + arrive_rank, -1)
    write_table = jnp.arange(post_count * ROWS, dtype=jnp.int32)[:, None] == target_row[None, :]
    written = jnp.dot(
        write_table.astype(jnp.bfloat16), arrived, preferred_element_type=jnp.float32
    ).astype(jnp.bfloat16)
    was_hit = jnp.any(write_table, axis=1)
    flat_rows = jnp.where(was_hit[:, None], written, postings.reshape(-1, D))
    postings_out = flat_rows.reshape(post_count, ROWS, D)
    new_fill = fill + arrive_counts

    def split_one(post_local, members):
        alive = (post_local >= 0).astype(jnp.float32)
        chosen_post = jnp.maximum(post_local, 0)
        rows_f = postings_out[chosen_post].astype(jnp.float32)
        prior = centroids[chosen_post].astype(jnp.float32)
        return two_means(rows_f, new_fill[chosen_post], members, prior) * alive

    split_centers = jax.vmap(split_one)(split_posts, split_members)
    picked = flat_rows[neigh_post * ROWS + neigh_row]
    chosen_centers = split_centers[neigh_split]
    scores = jnp.einsum(
        "nkd,nd->nk", chosen_centers, picked.astype(jnp.float32), precision=lax.Precision.HIGHEST
    ).astype(jnp.bfloat16)
    send_table = slot_table(neigh_dest, cent_count, SEND_CAP)
    send_rows = jnp.dot(
        send_table.astype(jnp.bfloat16), picked, preferred_element_type=jnp.float32
    ).astype(jnp.bfloat16)
    send_scores = jnp.dot(
        send_table.astype(jnp.float32), scores.astype(jnp.float32), precision=lax.Precision.HIGHEST
    ).astype(jnp.bfloat16)
    send_rows = send_rows.reshape(cent_count, SEND_CAP, D)
    send_scores = send_scores.reshape(cent_count, SEND_CAP, 2).transpose(0, 2, 1)
    moved_in, scores_in = (
        lax.all_to_all(send_rows, "cent", split_axis=0, concat_axis=0, tiled=True),
        lax.all_to_all(send_scores, "cent", split_axis=0, concat_axis=0, tiled=True),
    )
    moved_rows = moved_in.reshape(-1, D)
    moved_scores = scores_in.transpose(1, 0, 2).reshape(2, -1)
    return (best_score, postings_out, new_fill, split_centers, moved_rows, moved_scores)


def solution(mesh):
    return jax.shard_map(
        shards,
        mesh=mesh,
        in_specs=(
            P(("grp", "cent"), None),
            P("cent", None),
            P("cent", None, None),
            P("cent"),
            P(("grp", "cent")),
            P("cent"),
            P("cent", None),
            P(("grp", "cent")),
            P(("grp", "cent")),
            P(("grp", "cent")),
            P(("grp", "cent")),
        ),
        out_specs=(
            P(("grp", "cent")),
            P("cent", None, None),
            P("cent"),
            P("cent", None, None),
            P(("grp", "cent"), None),
            P(None, ("grp", "cent")),
        ),
        check_vma=False,
    )
```

profile of v0, /device:TPU:1, one launch (start us, length us, event | category | flops | bytes accessed | tf_op | source)
XLA Modules:
  0.0 300.0 jit_solution(7349504109958238840)
XLA Ops:
  7.2 0.7 all-gather.3.cloned.1.call-update
  8.6 13.8 %all-gather = s32[8,32,2]{1,2,0:T(2,128)S(1)} all-gather(s32[1,32,2]{1,2,0:T(2,128)S(1)} %add_bitcast_fusion.1), channel_id=1, replica_groups=mesh['grp'=8,'cent'=64] {'grp'}, dimensions={0}, use_global_device_ids=true | all-gather | bytes 2304 | tf_op jit(solution)/shard_map/all_gather | solution.py:92
  24.1 0.7 copy.48
  24.7 17.8 %all-to-all-start = ((s32[64,2,4]{2,1,0:T(2,128)}), s32[64,2,4]{2,1,0:T(2,128)S(1)}, u32[]{:S(2)}, u32[]{:S(2)}) async-start(s32[64,2,4]{2,1,0:T(2,128)} %copy.48), calls=%async_computation | async-start | bytes 131072 | tf_op jit(solution)/shard_map/all_to_all | solution.py:100
  42.5 20.6 %all_gather.11 = bf16[256,768]{1,0:T(8,128)(2,1)S(1)} all-gather(bf16[32,768]{1,0:T(8,128)(2,1)} %param.13), channel_id=1, replica_groups=mesh['grp'=8,'cent'=64] {'grp'}, dimensions={0}, use_global_device_ids=true | all-gather | bytes 442368 | tf_op jit(solution)/shard_map/all_gather | solution.py:91
  64.7 0.7 compare_select_fusion.2
  65.4 0.7 fusion.29
  66.3 0.8 select_reduce_fusion
  67.1 0.7 compare_select_fusion.6
  68.4 0.8 reshape.426
  69.3 1.5 gather_fusion.2
  70.8 15.0 %all-to-all-start.1 = ((bf16[64,4,768]{2,1,0:T(4,128)(2,1)}), bf16[64,4,768]{2,1,0:T(4,128)(2,1)S(1)}, u32[]{:S(2)}, u32[]{:S(2)}) async-start(bf16[64,4,768]{2,1,0:T(4,128)(2,1)} %reshape.426), calls=%async_computation.1 | async-start | bytes 786432 | tf_op jit(solution)/shard_map/all_to_all | solution.py:99
  87.9 14.6 %all-to-all-done.1 = bf16[64,4,768]{2,1,0:T(4,128)(2,1)S(1)} async-done(((bf16[64,4,768]{2,1,0:T(4,128)(2,1)}), bf16[64,4,768]{2,1,0:T(4,128)(2,1)S(1)}, u32[]{:S(2)}, u32[]{:S(2)}) %all-to-all-start.1) | async-done | bytes 393248 | tf_op jit(solution)/shard_map/all_to_all | solution.py:99
  105.4 0.7 gather_fusion.3
  106.5 1.0 gather_fusion.4
  107.5 1.5 fusion.20
  109.9 6.5 %all-to-all-start.3 = ((bf16[64,2,2]{2,1,0:T(2,128)(2,1)}), bf16[64,2,2]{2,1,0:T(2,128)(2,1)S(1)}, u32[]{:S(2)}, u32[]{:S(2)}) async-start(bf16[64,2,2]{2,1,0:T(2,128)(2,1)} %copy.54), calls=%async_computation.3 | async-start | bytes 65536 | tf_op jit(solution)/shard_map/all_to_all | solution.py:150
  116.7 0.8 reshape.430
  117.4 8.3 %all-to-all-done.3 = bf16[64,2,2]{2,1,0:T(2,128)(2,1)S(1)} async-done(((bf16[64,2,2]{2,1,0:T(2,128)(2,1)}), bf16[64,2,2]{2,1,0:T(2,128)(2,1)S(1)}, u32[]{:S(2)}, u32[]{:S(2)}) %all-to-all-start.3) | async-done | bytes 544 | tf_op jit(solution)/shard_map/all_to_all | solution.py:150
  125.8 4.7 %all-to-all-start.2 = ((bf16[64,2,768]{2,1,0:T(2,128)(2,1)}), bf16[64,2,768]{2,1,0:T(2,128)(2,1)S(1)}, u32[]{:S(2)}, u32[]{:S(2)}) async-start(bf16[64,2,768]{2,1,0:T(2,128)(2,1)} %reshape.430), calls=%async_computation.2 | async-start | bytes 393216 | tf_op jit(solution)/shard_map/all_to_all | solution.py:149
  131.2 10.4 %all-to-all-done.2 = bf16[64,2,768]{2,1,0:T(2,128)(2,1)S(1)} async-done(((bf16[64,2,768]{2,1,0:T(2,128)(2,1)}), bf16[64,2,768]{2,1,0:T(2,128)(2,1)S(1)}, u32[]{:S(2)}, u32[]{:S(2)}) %all-to-all-start.2) | async-done | bytes 196640 | tf_op jit(solution)/shard_map/all_to_all | solution.py:149
  141.5 0.8 reshape.431
  142.3 24.7 %while.11 = (s32[]{:T(128)}, f32[2048]{0:T(1024)S(1)}, bf16[8,256,768]{2,1,0:T(8,128)(2,1)}, bf16[2048,768]{1,0:T(8,128)(2,1)}, s32[]{:T(128)}, /*index=5*/s32[]{:T(128)}) while((s32[]{:T(128)}, f32[2048]{0:T(1024)S(1)}, bf16[8,256,768]{2,1,0:T(8,128)(2,1)}, bf16[2048,768]{1,0:T(8,128)(2,1)}, s32[]{:T(128)}, ...), condition=%wide.region_2.3_spmd.clone, body=%wide.region_0.2_spmd.clone.sunk | while | flops 805832704 | bytes 3571803 | solution.py:87
  142.3 3.0 %convolution_reduce_fusion.2 = f32[2048]{0:T(1024)S(1)} fusion(bf16[2048,768]{1,0:T(8,128)(2,1)} %get-tuple-element.121, bf16[8,256,768]{2,1,0:T(8,128)(2,1)} %get-tuple-element.120, s32[]{:T(128)S(6)} %copy.78), kind=kOutput, calls=%fused_computation.5.clone.1 | convolution fusion | flops 805828608 | bytes 3547140 | tf_op jit(solution)/shard_map/while/body/eval_jaxpr/dot_general | solution.py:81
  145.4 3.0 %convolution_reduce_fusion.2 = f32[2048]{0:T(1024)S(1)} fusion(bf16[2048,768]{1,0:T(8,128)(2,1)} %get-tuple-element.121, bf16[8,256,768]{2,1,0:T(8,128)(2,1)} %get-tuple-element.120, s32[]{:T(128)S(6)} %copy.78), kind=kOutput, calls=%fused_computation.5.clone.1 | convolution fusion | flops 805828608 | bytes 3547140 | tf_op jit(solution)/shard_map/while/body/eval_jaxpr/dot_general | solution.py:81
  148.5 3.0 %convolution_reduce_fusion.2 = f32[2048]{0:T(1024)S(1)} fusion(bf16[2048,768]{1,0:T(8,128)(2,1)} %get-tuple-element.121, bf16[8,256,768]{2,1,0:T(8,128)(2,1)} %get-tuple-element.120, s32[]{:T(128)S(6)} %copy.78), kind=kOutput, calls=%fused_computation.5.clone.1 | convolution fusion | flops 805828608 | bytes 3547140 | tf_op jit(solution)/shard_map/while/body/eval_jaxpr/dot_general | solution.py:81
  151.6 3.0 %convolution_reduce_fusion.2 = f32[2048]{0:T(1024)S(1)} fusion(bf16[2048,768]{1,0:T(8,128)(2,1)} %get-tuple-element.121, bf16[8,256,768]{2,1,0:T(8,128)(2,1)} %get-tuple-element.120, s32[]{:T(128)S(6)} %copy.78), kind=kOutput, calls=%fused_computation.5.clone.1 | convolution fusion | flops 805828608 | bytes 3547140 | tf_op jit(solution)/shard_map/while/body/eval_jaxpr/dot_general | solution.py:81
  154.6 3.0 %convolution_reduce_fusion.2 = f32[2048]{0:T(1024)S(1)} fusion(bf16[2048,768]{1,0:T(8,128)(2,1)} %get-tuple-element.121, bf16[8,256,768]{2,1,0:T(8,128)(2,1)} %get-tuple-element.120, s32[]{:T(128)S(6)} %copy.78), kind=kOutput, calls=%fused_computation.5.clone.1 | convolution fusion | flops 805828608 | bytes 3547140 | tf_op jit(solution)/shard_map/while/body/eval_jaxpr/dot_general | solution.py:81
  157.7 3.0 %convolution_reduce_fusion.2 = f32[2048]{0:T(1024)S(1)} fusion(bf16[2048,768]{1,0:T(8,128)(2,1)} %get-tuple-element.121, bf16[8,256,768]{2,1,0:T(8,128)(2,1)} %get-tuple-element.120, s32[]{:T(128)S(6)} %copy.78), kind=kOutput, calls=%fused_computation.5.clone.1 | convolution fusion | flops 805828608 | bytes 3547140 | tf_op jit(solution)/shard_map/while/body/eval_jaxpr/dot_general | solution.py:81
  160.8 3.0 %convolution_reduce_fusion.2 = f32[2048]{0:T(1024)S(1)} fusion(bf16[2048,768]{1,0:T(8,128)(2,1)} %get-tuple-element.121, bf16[8,256,768]{2,1,0:T(8,128)(2,1)} %get-tuple-element.120, s32[]{:T(128)S(6)} %copy.78), kind=kOutput, calls=%fused_computation.5.clone.1 | convolution fusion | flops 805828608 | bytes 3547140 | tf_op jit(solution)/shard_map/while/body/eval_jaxpr/dot_general | solution.py:81
  163.9 3.0 %convolution_reduce_fusion.2 = f32[2048]{0:T(1024)S(1)} fusion(bf16[2048,768]{1,0:T(8,128)(2,1)} %get-tuple-element.121, bf16[8,256,768]{2,1,0:T(8,128)(2,1)} %get-tuple-element.120, s32[]{:T(128)S(6)} %copy.78), kind=kOutput, calls=%fused_computation.5.clone.1 | convolution fusion | flops 805828608 | bytes 3547140 | tf_op jit(solution)/shard_map/while/body/eval_jaxpr/dot_general | solution.py:81
  167.0 125.6 %pmax.7 = f32[2048]{0:T(1024)S(1)} all-reduce(f32[2048]{0:T(1024)S(1)} %get-tuple-element.28), channel_id=1, replica_groups=mesh['grp'=8,'cent'=64] {'cent'}, use_global_device_ids=true, to_apply=%region_3.4 | all-reduce | flops 2048 | bytes 16384 | tf_op jit(solution)/shard_map/pmax | solution.py:88
  (97 shorter events, 12.3 us)
Async XLA Ops:
  7.2 79.2 %copy-start.4 = (s32[4]{0:T(128)S(1)}, s32[4]{0:T(128)}, u32[]{:S(2)}) copy-start(s32[4]{0:T(128)} %param.16) | copy-start | bytes 52
  7.2 80.0 %copy-start.3 = (s32[2,128]{1,0:T(2,128)S(1)}, s32[2,128]{1,0:T(2,128)}, u32[]{:S(2)}) copy-start(s32[2,128]{1,0:T(2,128)} %param.19) | copy-start | bytes 3076
  7.2 95.4 %copy-start.5 = (bf16[4,128,768]{2,1,0:T(8,128)(2,1)S(1)}, bf16[4,128,768]{2,1,0:T(8,128)(2,1)}, u32[]{:S(2)}) copy-start(bf16[4,128,768]{2,1,0:T(8,128)(2,1)} %param.15) | copy-start | bytes 2359300
  7.2 135.1 %all-gather.3.cloned.1.call-start = ((), (), s32[]{:S(2)}) async-start(), calls=%async_computation.4 | async-start | bytes 3194880 | tf_op jit(solution)/shard_map/all_gather | solution.py:78
  24.7 46.0 %all-to-all-start = ((s32[64,2,4]{2,1,0:T(2,128)}), s32[64,2,4]{2,1,0:T(2,128)S(1)}, u32[]{:S(2)}, u32[]{:S(2)}) async-start(s32[64,2,4]{2,1,0:T(2,128)} %copy.48), calls=%async_computation | async-start | bytes 131072 | tf_op jit(solution)/shard_map/all_to_all | solution.py:100
  70.8 31.7 %all-to-all-start.1 = ((bf16[64,4,768]{2,1,0:T(4,128)(2,1)}), bf16[64,4,768]{2,1,0:T(4,128)(2,1)S(1)}, u32[]{:S(2)}, u32[]{:S(2)}) async-start(bf16[64,4,768]{2,1,0:T(4,128)(2,1)} %reshape.426), calls=%async_computation.1 | async-start | bytes 786432 | tf_op jit(solution)/shard_map/all_to_all | solution.py:99
  86.5 19.7 %copy-start = (s32[4]{0:T(128)}, s32[4]{0:T(128)S(1)}, u32[]{:S(2)}) copy-start(s32[4]{0:T(128)S(1)} %add.148) | copy-start | bytes 52
  103.0 7.0 %copy-start.2 = (bf16[512,768]{1,0:T(8,128)(2,1)}, bf16[512,768]{1,0:T(8,128)(2,1)S(1)}, u32[]{:S(2)}) copy-start(bf16[512,768]{1,0:T(8,128)(2,1)S(1)} %fusion.3) | copy-start | bytes 2359300
  106.5 35.8 %copy-start.1 = (f32[2,2,768]{2,1,0:T(2,128)}, f32[2,2,768]{2,1,0:T(2,128)S(1)}, u32[]{:S(2)}) copy-start(f32[2,2,768]{2,1,0:T(2,128)S(1)} %fusion.5) | copy-start | bytes 36868
  109.9 15.8 %all-to-all-start.3 = ((bf16[64,2,2]{2,1,0:T(2,128)(2,1)}), bf16[64,2,2]{2,1,0:T(2,128)(2,1)S(1)}, u32[]{:S(2)}, u32[]{:S(2)}) async-start(bf16[64,2,2]{2,1,0:T(2,128)(2,1)} %copy.54), calls=%async_computation.3 | async-start | bytes 65536 | tf_op jit(solution)/shard_map/all_to_all | solution.py:150
  125.8 15.8 %all-to-all-start.2 = ((bf16[64,2,768]{2,1,0:T(2,128)(2,1)}), bf16[64,2,768]{2,1,0:T(2,128)(2,1)S(1)}, u32[]{:S(2)}, u32[]{:S(2)}) async-start(bf16[64,2,768]{2,1,0:T(2,128)(2,1)} %reshape.430), calls=%async_computation.2 | async-start | bytes 393216 | tf_op jit(solution)/shard_map/all_to_all | solution.py:149
Sparse Core Ops, SparseCore 0:
  11.4 92.0 all-gather.2
where the time goes:
time: 301 us; the launch traced here: 300 us
  blocking collectives  160 us (53%)
  starting transfers between devices  44.1 us (15%)
  waiting for transfers between devices  34 us (11%)
  matrix products  27.6 us (9%)
  between operations  14.4 us (5%)
  local copies, waits for them, and re-layouts  10.7 us (4%)
  other arithmetic  8.92 us (3%)
    pmax x1, blocking collectives, shards(): whole_best = lax.pmax(local_best, 'cent')  126 us
    dot_general x8, matrix products, scan_step(): lax.dot_general(piece, block, (((1,), (1,)), ((), ())), preferred_element...  24.4 us
    all_gather x1, blocking collectives, shards(): lax.all_gather(vectors, 'grp', axis=0, tiled=True)  20.6 us
    all_to_all x1, starting transfers between devices, shards(): lax.all_to_all(placed_ids, 'cent', split_axis=0, concat_axis=0, tiled=True)  17.8 us
    all_to_all x1, starting transfers between devices, shards(): lax.all_to_all(placed, 'cent', split_axis=0, concat_axis=0, tiled=True)  15 us
    all_to_all x1, waiting for transfers between devices, shards(): lax.all_to_all(placed, 'cent', split_axis=0, concat_axis=0, tiled=True)  14.6 us
    all_gather x1, blocking collectives, shards(): lax.all_gather(id_pairs, 'grp', axis=1, tiled=True)  13.8 us
    all_to_all x1, waiting for transfers between devices, shards(): lax.all_to_all(send_rows, 'cent', split_axis=0, concat_axis=0, tiled=True)  10.4 us
  transfers between devices with their start and end apart: 5, of which 3 were waited for; matrix products, arithmetic and copies ran while one was open for 7% of the time, Pallas kernels for 0%

commit v1 on v0

v1 whole, which is shorter than its diff:
```python
import functools

import jax
import jax.numpy as jnp
from jax import lax
from jax.experimental import pallas as pl
from jax.experimental.pallas import tpu as pltpu
from jax.sharding import Mesh, PartitionSpec as P

D = 768
W = 896
ROWS = 128
HEAD = 32
ITERS = 2
NX, NY, NZ, NK = 4, 8, 8, 2
NC = NX * NZ * NK
V = 32
NB = 64
POSTS = 4
CENT = ("x", "z", "core")
LOW = -3.0e38
F32 = jnp.float32
BF = jnp.bfloat16
I32 = jnp.int32
VMEM_BYTES = 40 * 1024 * 1024


def iota(shape, dim):
    return lax.broadcasted_iota(I32, shape, dim)


def as_column(row):
    n = row.shape[1]
    eye = iota((n, n), 0) == iota((n, n), 1)
    return jnp.sum(jnp.where(eye, jnp.broadcast_to(row, (n, n)), 0), axis=1, keepdims=True)


def earlier_equal(row):
    n = row.shape[1]
    same = (as_column(row) == row) & (iota((n, n), 0) < iota((n, n), 1))
    return jnp.sum(same.astype(I32), axis=0, keepdims=True)


def one_hot(mask):
    return jnp.where(mask, 1.0, 0.0).astype(BF)


def dot(a, b):
    return jnp.dot(a, b, preferred_element_type=F32)


def dot_nt(a, b):
    return lax.dot_general(a, b, (((1,), (1,)), ((), ())), preferred_element_type=F32)


def pack_kernel(vec_ref, head_ref, assign_ref, npost_ref, nrow_ref, ndest_ref, out_ref):
    assign = assign_ref[...]
    dest = assign // POSTS
    place = earlier_equal(dest)
    slot = iota((NC * 8, V), 0)
    to, r = slot // 8, slot % 8
    col = iota((NC * 8, V), 1)
    share = (r < 4) & (col == ((to // (NZ * NK)) * NK + to % NK) * 4 + r)
    route = (dest == to) & (place == r - 4) & (r >= 4) & (r < 6)
    ndest = ndest_ref[...]
    nplace = earlier_equal(ndest)
    nslot = iota((NC * 8, NB), 0)
    chosen = one_hot((ndest == nslot // 8) & (nplace == nslot % 8 - 6) & (nslot % 8 >= 6))
    where_row = npost_ref[...] * HEAD + nrow_ref[...]
    picks = one_hot(where_row == iota((POSTS * HEAD, NB), 0))
    table = dot_nt(chosen, picks).astype(BF)
    head = head_ref[...].reshape(POSTS * HEAD, D)
    out_ref[:, :D] = (dot(one_hot(share | route), vec_ref[...]) + dot(table, head)).astype(BF)
    post = as_column(assign) % POSTS + 1
    mark = jnp.where(iota((V, 128), 1) == 0, post, 0).astype(F32).astype(BF)
    out_ref[:, D:] = dot(one_hot(route), mark).astype(BF)


def unpack_kernel(in_ref, share_ref, moved_ref, spread_ref):
    n = NC * 8
    p = iota((NC * 4, n), 1)
    i = iota((NC * 4, n), 0)
    rows = in_ref[:, :D]
    share_ref[...] = dot(one_hot(p == (i // 4) * 8 + i % 4), rows).astype(BF)
    p2, i2 = p[: NC * 2], i[: NC * 2]
    moved_ref[...] = dot(one_hot(p2 == (i2 // 2) * 8 + 6 + i2 % 2), rows).astype(BF)
    mark = dot_nt(one_hot(iota((8, 128), 1) == 0), in_ref[:, D:])
    upper = one_hot(iota((n, n), 0) < iota((n, n), 1))
    rank = dot(one_hot(mark > 0.5), upper)
    hit = (mark[:1] > 0.5) & (rank[:1].astype(I32) == iota((V, n), 0))
    compact = dot(one_hot(hit), in_ref[...]).astype(BF)
    for g in range(NY):
        spread_ref[g] = compact


def append_kernel(
    fill_ref, split_ref, got_ref, post_ref, prior_ref, member_ref, npost_ref, nrow_ref, nsplit_ref,
    ndest_ref, out_ref, count_ref, centers_ref, score_ref,
):
    n = NY * V
    mark = dot_nt(one_hot(iota((8, 128), 1) == 0), got_ref[:, D:]).astype(I32)
    match = mark == iota((8, n), 0) + 1
    upper = one_hot(iota((n, n), 0) < iota((n, n), 1))
    rank = dot(one_hot(match), upper).astype(I32)
    row = iota((ROWS, n), 0)
    line = iota((ROWS, 1), 0)
    got = got_ref[:, :D]
    for q in range(POSTS):
        mine = match[q : q + 1]
        count = jnp.sum(mine.astype(I32))
        first = fill_ref[q]
        table = one_hot(mine & (row == first + rank[q : q + 1]))
        written = dot(table, got)
        hit = (line >= first) & (line < first + count)
        out_ref[q] = jnp.where(hit, written, post_ref[q].astype(F32)).astype(BF)
        count_ref[q] = first + count

    head = post_ref[:, :HEAD, :].reshape(POSTS * HEAD, D).astype(F32)
    members = member_ref[...].astype(F32)
    eye = iota((ROWS, ROWS), 0) == iota((ROWS, ROWS), 1)
    lane = iota((POSTS * HEAD, 128), 1)
    ndest = ndest_ref[...]
    nplace = earlier_equal(ndest)
    nsplit = nsplit_ref[...]
    picks = one_hot(npost_ref[...] * HEAD + nrow_ref[...] == iota((POSTS * HEAD, NB), 0))
    to = iota((NC, NB), 0)
    sent = jnp.zeros((NC, 128), F32)
    for s in range(2):
        j = split_ref[s]
        alive = jnp.where(j >= 0, 1.0, 0.0).astype(F32)
        q = jnp.maximum(j, 0)
        x = out_ref[q].astype(F32)
        own = prior_ref[...].astype(F32)
        prior = jnp.sum(jnp.where(iota(own.shape, 0) == q, own, 0.0), axis=0, keepdims=True)
        mask = jnp.where(line < count_ref[q], 1.0, 0.0).astype(F32)
        weights = jnp.sum(jnp.where(eye, members[s : s + 1], 0.0), axis=1, keepdims=True)

        def update(weights):
            w1, w2 = mask * weights, mask * (1.0 - weights)
            s1 = jnp.sum(w1 * x, axis=0, keepdims=True) + prior
            s2 = jnp.sum(w2 * x, axis=0, keepdims=True) + prior
            t1 = jnp.sum(w1, axis=0, keepdims=True) + 1.0
            t2 = jnp.sum(w2, axis=0, keepdims=True) + 1.0
            return s1 / t1, s2 / t2

        a1, a2 = update(weights)
        for _ in range(ITERS):
            far = jnp.sum(jnp.square(x - a2), axis=1, keepdims=True) - jnp.sum(
                jnp.square(x - a1), axis=1, keepdims=True
            )
            a1, a2 = update(jax.nn.sigmoid(0.125 * far))
        a1, a2 = a1 * alive, a2 * alive
        centers_ref[s, 0:1, :] = a1
        centers_ref[s, 1:2, :] = a2
        c1 = jnp.sum(head * a1, axis=1, keepdims=True)
        c2 = jnp.sum(head * a2, axis=1, keepdims=True)
        for t in range(2):
            where_to = one_hot((ndest == to) & (nplace == t) & (nsplit == s))
            table = dot_nt(where_to, picks).astype(BF)
            values = jnp.where(lane == 32 + 2 * t, c1, jnp.where(lane == 33 + 2 * t, c2, 0.0))
            sent = sent + dot(table, values.astype(BF))
    score_ref[...] = sent


BLOCK = 1024
STEPS = 2048 // BLOCK


def best_kernel(place_ref, own_ref, mate_ref, v0_ref, v1_ref, v2_ref, v3_ref, score_ref, out_ref, acc_ref):
    step = pl.program_id(0)
    parts = (v0_ref, v1_ref, v2_ref, v3_ref)

    @pl.when(step == 0)
    def _():
        acc_ref[...] = jnp.full(acc_ref.shape, LOW, F32)

    def scan(block_ref):
        for a, part in enumerate(parts):
            scores = dot_nt(block_ref[...], part[...])
            top = jnp.max(scores.reshape(BLOCK // 8, 8, NC * 4), axis=0)
            acc_ref[a] = jnp.maximum(acc_ref[a], top)

    @pl.when(step < STEPS)
    def _():
        scan(own_ref)

    @pl.when(step >= STEPS)
    def _():
        scan(mate_ref)

    @pl.when(step == 2 * STEPS - 1)
    def _():
        x, core = place_ref[0], place_ref[1]
        wide = (NC, NC * 4)
        mine = iota(wide, 1) // 4 == iota(wide, 0)
        lane = iota((NC, 128), 1)
        best = jnp.full((NC, 128), LOW, F32)
        for a in range(NX):
            top = jnp.max(acc_ref[a], axis=0, keepdims=True)
            spread = jnp.where(mine, jnp.broadcast_to(top, wide), LOW)
            folded = jnp.maximum(spread[:, :128], spread[:, 128:])
            for shift in (64, 32, 16, 8, 4):
                folded = jnp.maximum(folded, pltpu.roll(folded, shift, 1))
            group = lax.rem(x + NX - a, NX) * NK + core
            best = jnp.where(lane // 4 == group, folded, best)
        out_ref[...] = jnp.where(lane < V, best, score_ref[...])


def final_kernel(in_ref, best_ref, score_ref):
    got = in_ref[...]
    best_ref[...] = jnp.max(got, axis=0, keepdims=True)[:, :V]
    lane = iota((NC, 128), 1)
    src = iota((NC, 128), 0)
    vals = jnp.where((lane >= 32) & (lane < 36), got, 0.0).astype(BF)
    total = jnp.zeros((8, 128), F32)
    pick = iota((8, 128), 0)
    at = iota((8, 128), 1)
    for t in range(2):
        chosen = one_hot(at == 32 + 2 * t + pick)
        rows = dot_nt(chosen, vals).astype(BF)
        total = total + dot(rows, one_hot(lane == src * 2 + t))
    score_ref[...] = total[:2].astype(BF)


def vm():
    return pl.BlockSpec(memory_space=pltpu.VMEM)


def sm():
    return pl.BlockSpec(memory_space=pltpu.SMEM)


def params(**kw):
    return pltpu.CompilerParams(vmem_limit_bytes=VMEM_BYTES, **kw)


def shards(
    vectors,
    centroids,
    postings,
    fill,
    assign,
    split_posts,
    split_members,
    neigh_post,
    neigh_row,
    neigh_split,
    neigh_dest,
):
    place = jnp.stack([lax.axis_index("x"), lax.axis_index("core")]).astype(I32)
    npost, nrow, nsplit, ndest = (
        a.reshape(1, NB) for a in (neigh_post, neigh_row, neigh_split, neigh_dest)
    )
    mate = lax.ppermute(centroids, "core", [(0, 1), (1, 0)])
    one = lambda *shape: pl.BlockSpec(shape, lambda i: (0,) * len(shape))
    packed = pl.pallas_call(
        pack_kernel,
        out_shape=jax.ShapeDtypeStruct((NC * 8, W), BF),
        grid=(1,),
        in_specs=[one(V, D), one(POSTS, HEAD, D), one(1, V), one(1, NB), one(1, NB), one(1, NB)],
        out_specs=one(NC * 8, W),
        compiler_params=params(),
        name="pack_rows",
    )(vectors, postings, assign.reshape(1, V), npost, nrow, ndest)
    got = lax.all_to_all(packed.reshape(NC, 8, W), CENT, 0, 0, tiled=True).reshape(NC * 8, W)
    share, moved_rows, spread = pl.pallas_call(
        unpack_kernel,
        out_shape=(
            jax.ShapeDtypeStruct((NC * 4, D), BF),
            jax.ShapeDtypeStruct((NC * 2, D), BF),
            jax.ShapeDtypeStruct((NY, V, W), BF),
        ),
        in_specs=[vm()],
        out_specs=(vm(), vm(), vm()),
        compiler_params=params(),
        name="unpack_rows",
    )(got)
    parts = [share] + [
        lax.ppermute(share, "x", [(i, (i + a) % NX) for i in range(NX)]) for a in range(1, NX)
    ]
    gathered = lax.all_to_all(spread, "y", 0, 0, tiled=True).reshape(NY * V, W)
    postings_out, new_fill, split_centers, scores = pl.pallas_call(
        append_kernel,
        out_shape=(
            jax.ShapeDtypeStruct((POSTS, ROWS, D), BF),
            jax.ShapeDtypeStruct((POSTS,), I32),
            jax.ShapeDtypeStruct((2, 2, D), F32),
            jax.ShapeDtypeStruct((NC, 128), F32),
        ),
        grid=(1,),
        in_specs=[
            sm(), sm(), one(NY * V, W), one(POSTS, ROWS, D), one(16, D), one(2, ROWS),
            one(1, NB), one(1, NB), one(1, NB), one(1, NB),
        ],
        out_specs=(one(POSTS, ROWS, D), sm(), one(2, 2, D), one(NC, 128)),
        compiler_params=params(),
        name="append_split",
    )(fill, split_posts, gathered, postings, centroids, split_members, npost, nrow, nsplit, ndest)
    whole = one(NC * 4, D)
    sending = pl.pallas_call(
        best_kernel,
        out_shape=jax.ShapeDtypeStruct((NC, 128), F32),
        grid=(2 * STEPS,),
        in_specs=[
            sm(),
            pl.BlockSpec((BLOCK, D), lambda i: (jnp.minimum(i, STEPS - 1), 0)),
            pl.BlockSpec((BLOCK, D), lambda i: (jnp.maximum(i - STEPS, 0), 0)),
            whole, whole, whole, whole,
            one(NC, 128),
        ],
        out_specs=one(NC, 128),
        scratch_shapes=[pltpu.VMEM((NX, 8, NC * 4), F32)],
        compiler_params=params(),
        name="best_scores",
    )(place, centroids, mate, *parts, scores)
    back = lax.all_to_all(sending.reshape(NC, 1, 128), CENT, 0, 0, tiled=True).reshape(NC, 128)
    best_score, moved_scores = pl.pallas_call(
        final_kernel,
        out_shape=(jax.ShapeDtypeStruct((1, V), F32), jax.ShapeDtypeStruct((2, 2 * NC), BF)),
        in_specs=[vm()],
        out_specs=(vm(), vm()),
        compiler_params=params(),
        name="last_step",
    )(back)
    return (
        best_score.reshape(V), postings_out, new_fill, split_centers, moved_rows, moved_scores
    )


def solution(mesh):
    fine = Mesh(mesh.devices.reshape(NY, NX, NZ, NK), ("y", "x", "z", "core"))
    both = ("y",) + CENT
    return jax.shard_map(
        shards,
        mesh=fine,
        in_specs=(
            P(both, None),
            P(CENT, None),
            P(CENT, None, None),
            P(CENT),
            P(both),
            P(CENT),
            P(CENT, None),
            P(both),
            P(both),
            P(both),
            P(both),
        ),
        out_specs=(
            P(both),
            P(CENT, None, None),
            P(CENT),
            P(CENT, None, None),
            P(both, None),
            P(None, both),
        ),
        check_vma=False,
    )
```

time: 301 us -> 109 us (0.36)
  blocking collectives: 160 us -> 46.9 us
  matrix products: 27.6 us -> 0 us
  waiting for transfers between devices: 34 us -> 10.7 us
  starting transfers between devices: 44.1 us -> 25.3 us
  Pallas kernels: 0 us -> 16 us
  between operations: 14.4 us -> 0.77 us
  other arithmetic: 8.92 us -> 0.64 us
    pmax x1 -> x0, blocking collectives: 126 us -> none  [shards(): whole_best = lax.pmax(local_best, 'cent')]
    all_to_all x0 -> x2, blocking collectives: none -> 46.9 us  [the longest x1 33.6 us: shards(): lax.all_to_all(packed.reshape(NC, 8, W), CENT, 0, 0, tiled=True)]
    all_to_all x4 -> x1, starting transfers between devices: 44 us -> 6.83 us  [shards(): gathered = lax.all_to_all(spread, 'y', 0, 0, tiled=True).reshape(NY * V, W)]
    all_gather x2 -> x0, blocking collectives: 34.4 us -> none  [the longest x1 20.6 us: shards(): lax.all_gather(vectors, 'grp', axis=0, tiled=True)]
    dot_general x16 -> x0, matrix products: 27.6 us -> none  [the longest x8 24.4 us: scan_step(): lax.dot_general(piece, block, (((1,), (1,)), ((), ())), preferred_element...]
    all_to_all x4 -> x1, waiting for transfers between devices: 33.3 us -> 6.57 us  [shards(): gathered = lax.all_to_all(spread, 'y', 0, 0, tiled=True).reshape(NY * V, W)]
    ppermute x0 -> x4, starting transfers between devices: none -> 18.5 us  [the longest x3 9.42 us: shards(): lax.ppermute(share, 'x', [(i, (i + a) % NX) for i in range(NX)])]
    pallas_call x0 -> x5, Pallas kernels: none -> 16 us  [the longest x1 9.58 us: shards(): pl.pallas_call(best_kernel, out_shape=jax.ShapeDtypeStruct((NC, 128), F32...]
  transfers between devices with their start and end apart: 5 -> 5, of which waited for: 3 -> 2; matrix products, arithmetic and copies ran while one was open for 7% -> 1% of each run, Pallas kernels for 0% -> 5%
where the time goes in v1:
time: 109 us
  blocking collectives  46.9 us (43%)
  starting transfers between devices  25.3 us (23%)
  Pallas kernels  16 us (15%)
  waiting for transfers between devices  10.7 us (10%)
  local copies, waits for them, and re-layouts  8.43 us (8%)
    all_to_all x1, blocking collectives, shards(): lax.all_to_all(packed.reshape(NC, 8, W), CENT, 0, 0, tiled=True)  33.6 us
    all_to_all x1, blocking collectives, shards(): lax.all_to_all(sending.reshape(NC, 1, 128), CENT, 0, 0, tiled=True)  13.3 us
    pallas_call x1, Pallas kernels, shards(): pl.pallas_call(best_kernel, out_shape=jax.ShapeDtypeStruct((NC, 128), F32...  9.58 us
    ppermute x3, starting transfers between devices, shards(): lax.ppermute(share, 'x', [(i, (i + a) % NX) for i in range(NX)])  9.42 us
    ppermute x1, starting transfers between devices, shards(): mate = lax.ppermute(centroids, 'core', [(0, 1), (1, 0)])  9.05 us
    unnamed x34, local copies, waits for them, and re-layouts  8.43 us
    all_to_all x1, starting transfers between devices, shards(): gathered = lax.all_to_all(spread, 'y', 0, 0, tiled=True).reshape(NY * V, W)  6.83 us
    all_to_all x1, waiting for transfers between devices, shards(): gathered = lax.all_to_all(spread, 'y', 0, 0, tiled=True).reshape(NY * V, W)  6.57 us
  transfers between devices with their start and end apart: 5, of which 2 were waited for; matrix products, arithmetic and copies ran while one was open for 1% of the time, Pallas kernels for 5%

profile of v1, /device:TPU:1, one launch (start us, length us, event | category | flops | bytes accessed | tf_op | source)
XLA Modules:
  0.0 108.8 jit_solution(1000059405226373791)
XLA Ops:
  0.6 0.0 copy-start
  0.6 9.1 %collective-permute-start = (bf16[2048,768]{1,0:T(8,128)(2,1)}, bf16[2048,768]{1,0:T(8,128)(2,1)}, u32[]{:S(2)}, u32[]{:S(2)}) collective-permute-start(bf16[2048,768]{1,0:T(8,128)(2,1)} %own_ref.1), channel_id=1, source_target_pairs={{0,1},{1,0},{2,3},{3,2},{4,5},{5,4},{6,7},{7,6},{8,9},{9,8},{10,11... | collective-permute-start | bytes 9437192 | tf_op jit(solution)/shard_map/ppermute | solution.py:254
  9.7 0.0 copy-start.1
  9.7 1.1 %copy-done.1 = bf16[4,128,768]{2,1,0:T(8,128)(2,1)S(1)} copy-done((bf16[4,128,768]{2,1,0:T(8,128)(2,1)S(1)}, bf16[4,128,768]{2,1,0:T(8,128)(2,1)}, u32[]{:S(2)}) %copy-start.1) | copy-done | bytes 786456
  10.8 0.8 copy-done.4
  11.6 0.7 copy-done.5
  12.3 0.7 copy-done.7
  13.0 0.7 copy-done.9
  13.6 0.7 copy-done.12
  14.3 0.9 pack_rows.1
  15.2 33.6 %all_to_all.15 = bf16[64,8,896]{2,1,0:T(8,128)(2,1)S(1)} all-to-all(bf16[64,8,896]{2,1,0:T(8,128)(2,1)S(1)} %bitcast.16), channel_id=1, replica_groups=mesh['y'=8,'x'=4,'z'=8,'core'=2] {'x','z','core'}, dimensions={0} | all-to-all | bytes 1835008 | tf_op jit(solution)/shard_map/all_to_all | solution.py:265
  48.8 1.2 %unpack_rows.1 = (bf16[256,768]{1,0:T(8,128)(2,1)S(1)}, bf16[128,768]{1,0:T(8,128)(2,1)}, bf16[8,32,896]{2,1,0:T(8,128)(2,1)S(1)}) custom-call(bf16[512,896]{1,0:T(8,128)(2,1)S(1)} %bitcast.15), custom_call_target="tpu_custom_call" | custom-call | tf_op jit(solution)/shard_map/unpack_rows/pallas_call | solution.py:266
  50.0 0.8 copy-done.3
  50.8 6.8 %all-to-all-start.1 = ((bf16[8,32,896]{2,1,0:T(8,128)(2,1)}), bf16[8,32,896]{2,1,0:T(8,128)(2,1)}, u32[]{:S(2)}, u32[]{:S(2)}) async-start(bf16[8,32,896]{2,1,0:T(8,128)(2,1)} %copy-done.3), calls=%async_computation.1 | async-start | bytes 917504 | tf_op jit(solution)/shard_map/all_to_all | solution.py:281
  57.6 4.6 %collective-permute-start.3 = (bf16[256,768]{1,0:T(8,128)(2,1)S(1)}, bf16[256,768]{1,0:T(8,128)(2,1)}, u32[]{:S(2)}, u32[]{:S(2)}) collective-permute-start(bf16[256,768]{1,0:T(8,128)(2,1)S(1)} %get-tuple-element.15.v0_ref), channel_id=1, source_target_pairs={{0,48},{16,0},{32,16},{48,32},{1,49},{17,1},{33,17},{49,33},{2,50}... | collective-permute-start | bytes 1179656 | tf_op jit(solution)/shard_map/ppermute | solution.py:279
  62.1 2.3 %collective-permute-start.2 = (bf16[256,768]{1,0:T(8,128)(2,1)S(1)}, bf16[256,768]{1,0:T(8,128)(2,1)}, u32[]{:S(2)}, u32[]{:S(2)}) collective-permute-start(bf16[256,768]{1,0:T(8,128)(2,1)S(1)} %get-tuple-element.15.v0_ref), channel_id=1, source_target_pairs={{0,32},{16,48},{32,0},{48,16},{1,33},{17,49},{33,1},{49,17},{2,34}... | collective-permute-start | bytes 1179656 | tf_op jit(solution)/shard_map/ppermute | solution.py:279
  64.4 2.6 %collective-permute-start.1 = (bf16[256,768]{1,0:T(8,128)(2,1)S(1)}, bf16[256,768]{1,0:T(8,128)(2,1)}, u32[]{:S(2)}, u32[]{:S(2)}) collective-permute-start(bf16[256,768]{1,0:T(8,128)(2,1)S(1)} %get-tuple-element.15.v0_ref), channel_id=1, source_target_pairs={{0,16},{16,32},{32,48},{48,0},{1,17},{17,33},{33,49},{49,1},{2,18}... | collective-permute-start | bytes 1179656 | tf_op jit(solution)/shard_map/ppermute | solution.py:279
  67.0 0.6 pad_add_fusion.place_ref
  67.7 6.6 %all-to-all-done.1 = bf16[8,32,896]{2,1,0:T(8,128)(2,1)} async-done(((bf16[8,32,896]{2,1,0:T(8,128)(2,1)}), bf16[8,32,896]{2,1,0:T(8,128)(2,1)}, u32[]{:S(2)}, u32[]{:S(2)}) %all-to-all-start.1) | async-done | bytes 458784 | tf_op jit(solution)/shard_map/all_to_all | solution.py:281
  74.3 0.0 copy-start.2
  74.3 1.1 %copy-done.2 = bf16[4,128,768]{2,1,0:T(8,128)(2,1)S(1)} copy-done((bf16[4,128,768]{2,1,0:T(8,128)(2,1)S(1)}, bf16[4,128,768]{2,1,0:T(8,128)(2,1)}, u32[]{:S(2)}) %copy-start.2) | copy-done | bytes 786456
  75.4 0.7 copy-done.13
  76.1 0.7 copy-done.14
  76.7 0.7 copy-done.15
  77.4 3.5 %append_split.1 = (bf16[4,128,768]{2,1,0:T(8,128)(2,1)}, s32[4]{0:T(128)}, f32[2,2,768]{2,1,0:T(2,128)}, f32[64,128]{1,0:T(8,128)S(1)}) custom-call(s32[4]{0:T(128)S(1)} %copy-done.13, s32[2]{0:T(128)S(1)} %copy-done.14, bf16[256,896]{1,0:T(8,128)(2,1)} %bitcast.8.got_ref, bf16[4,128,768]{2,1,0:T(8,128)(2,1)S(1)} %copy-done.2, ...), custom_call_target="tpu_custom_call" | custom-call | tf_op jit(solution)/shard_map/append_split/pallas_call | solution.py:282
  80.9 0.0 collective-permute-done.3.v3_ref
  80.9 0.0 collective-permute-done.2.v2_ref
  81.0 4.2 %collective-permute-done.1.v1_ref = bf16[256,768]{1,0:T(8,128)(2,1)} collective-permute-done((bf16[256,768]{1,0:T(8,128)(2,1)S(1)}, bf16[256,768]{1,0:T(8,128)(2,1)}, u32[]{:S(2)}, u32[]{:S(2)}) %collective-permute-start.1) | collective-permute-done | bytes 393248 | tf_op jit(solution)/shard_map/ppermute | solution.py:279
  85.1 0.0 collective-permute-done.mate_ref
  85.1 9.6 %best_scores.1 = f32[64,128]{1,0:T(8,128)S(1)} custom-call(s32[2]{0:T(128)S(1)} %copy-done.16, bf16[2048,768]{1,0:T(8,128)(2,1)S(1)} %copy-done, bf16[2048,768]{1,0:T(8,128)(2,1)} %collective-permute-done.mate_ref, bf16[256,768]{1,0:T(8,128)(2,1)S(1)} %get-tuple-element.15.v0_ref, bf16[256,768]{1,0:T(8,128)(2,1)} %collective-permute-done.1.v1_ref, ...), custom_call_target="tpu_custom_call" | custom-call | tf_op jit(solution)/shard_map/best_scores/pallas_call | solution.py:300
  94.7 13.3 %all_to_all.16 = f32[64,1,128]{2,1,0:T(1,128)S(1)} all-to-all(f32[64,1,128]{2,1,0:T(1,128)S(1)} %bitcast.17), channel_id=1, replica_groups=mesh['y'=8,'x'=4,'z'=8,'core'=2] {'x','z','core'}, dimensions={0} | all-to-all | bytes 65536 | tf_op jit(solution)/shard_map/all_to_all | solution.py:316
  108.0 0.8 last_step.1
  (20 shorter events, 0.0 us)
Async XLA Ops:
  0.6 73.6 %copy-start = (bf16[2048,768]{1,0:T(8,128)(2,1)S(1)}, bf16[2048,768]{1,0:T(8,128)(2,1)}, u32[]{:S(2)}) copy-start(bf16[2048,768]{1,0:T(8,128)(2,1)} %own_ref.1) | copy-start | bytes 9437188
  0.6 84.5 %collective-permute-start = (bf16[2048,768]{1,0:T(8,128)(2,1)}, bf16[2048,768]{1,0:T(8,128)(2,1)}, u32[]{:S(2)}, u32[]{:S(2)}) collective-permute-start(bf16[2048,768]{1,0:T(8,128)(2,1)} %own_ref.1), channel_id=1, source_target_pairs={{0,1},{1,0},{2,3},{3,2},{4,5},{5,4},{6,7},{7,6},{8,9},{9,8},{10,11... | collective-permute-start | bytes 9437192 | tf_op jit(solution)/shard_map/ppermute | solution.py:254
  9.7 1.1 %copy-start.1 = (bf16[4,128,768]{2,1,0:T(8,128)(2,1)S(1)}, bf16[4,128,768]{2,1,0:T(8,128)(2,1)}, u32[]{:S(2)}) copy-start(bf16[4,128,768]{2,1,0:T(8,128)(2,1)} %post_ref.1) | copy-start | bytes 2359300
  10.8 0.8 copy-start.4
  11.6 0.7 copy-start.5
  12.3 0.7 copy-start.7
  12.9 0.7 copy-start.9
  13.6 0.7 copy-start.12
  14.3 60.0 %copy-start.6 = (s32[64]{0:T(128)S(1)}, s32[64]{0:T(128)}, u32[]{:S(2)}) copy-start(s32[64]{0:T(128)} %param.18) | copy-start | bytes 772
  14.3 60.0 %copy-start.8 = (s32[64]{0:T(128)S(1)}, s32[64]{0:T(128)}, u32[]{:S(2)}) copy-start(s32[64]{0:T(128)} %param.19) | copy-start | bytes 772
  14.3 60.0 %copy-start.10 = (s32[64]{0:T(128)S(1)}, s32[64]{0:T(128)}, u32[]{:S(2)}) copy-start(s32[64]{0:T(128)} %param.21) | copy-start | bytes 772
  14.3 60.0 %copy-start.11 = (s32[2,128]{1,0:T(2,128)S(1)}, s32[2,128]{1,0:T(2,128)}, u32[]{:S(2)}) copy-start(s32[2,128]{1,0:T(2,128)} %member_ref.1) | copy-start | bytes 3076
  50.0 0.8 copy-start.3
  50.8 23.5 %all-to-all-start.1 = ((bf16[8,32,896]{2,1,0:T(8,128)(2,1)}), bf16[8,32,896]{2,1,0:T(8,128)(2,1)}, u32[]{:S(2)}, u32[]{:S(2)}) async-start(bf16[8,32,896]{2,1,0:T(8,128)(2,1)} %copy-done.3), calls=%async_computation.1 | async-start | bytes 917504 | tf_op jit(solution)/shard_map/all_to_all | solution.py:281
  57.6 23.4 %collective-permute-start.3 = (bf16[256,768]{1,0:T(8,128)(2,1)S(1)}, bf16[256,768]{1,0:T(8,128)(2,1)}, u32[]{:S(2)}, u32[]{:S(2)}) collective-permute-start(bf16[256,768]{1,0:T(8,128)(2,1)S(1)} %get-tuple-element.15.v0_ref), channel_id=1, source_target_pairs={{0,48},{16,0},{32,16},{48,32},{1,49},{17,1},{33,17},{49,33},{2,50}... | collective-permute-start | bytes 1179656 | tf_op jit(solution)/shard_map/ppermute | solution.py:279
  62.1 18.8 %collective-permute-start.2 = (bf16[256,768]{1,0:T(8,128)(2,1)S(1)}, bf16[256,768]{1,0:T(8,128)(2,1)}, u32[]{:S(2)}, u32[]{:S(2)}) collective-permute-start(bf16[256,768]{1,0:T(8,128)(2,1)S(1)} %get-tuple-element.15.v0_ref), channel_id=1, source_target_pairs={{0,32},{16,48},{32,0},{48,16},{1,33},{17,49},{33,1},{49,17},{2,34}... | collective-permute-start | bytes 1179656 | tf_op jit(solution)/shard_map/ppermute | solution.py:279
  64.4 20.7 %collective-permute-start.1 = (bf16[256,768]{1,0:T(8,128)(2,1)S(1)}, bf16[256,768]{1,0:T(8,128)(2,1)}, u32[]{:S(2)}, u32[]{:S(2)}) collective-permute-start(bf16[256,768]{1,0:T(8,128)(2,1)S(1)} %get-tuple-element.15.v0_ref), channel_id=1, source_target_pairs={{0,16},{16,32},{32,48},{48,0},{1,17},{17,33},{33,49},{49,1},{2,18}... | collective-permute-start | bytes 1179656 | tf_op jit(solution)/shard_map/ppermute | solution.py:279
  74.2 10.9 %copy-start.16 = (s32[2]{0:T(128)S(1)}, s32[2]{0:T(128)}, u32[]{:S(2)}) copy-start(s32[2]{0:T(128)} %pad_add_fusion.place_ref) | copy-start | bytes 28
  74.3 1.1 %copy-start.2 = (bf16[4,128,768]{2,1,0:T(8,128)(2,1)S(1)}, bf16[4,128,768]{2,1,0:T(8,128)(2,1)}, u32[]{:S(2)}) copy-start(bf16[4,128,768]{2,1,0:T(8,128)(2,1)} %post_ref.1) | copy-start | bytes 2359300
  75.4 0.7 copy-start.13
  76.1 0.7 copy-start.14
  76.7 0.7 copy-start.15

commit v2 on v1

v2 whole, which is shorter than its diff:
```python
import functools

import jax
import jax.numpy as jnp
from jax import lax
from jax.experimental import pallas as pl
from jax.experimental.pallas import tpu as pltpu
from jax.sharding import Mesh, PartitionSpec as P

D = 768
W = 896
ROWS = 128
HEAD = 32
ITERS = 2
NX, NY, NZ, NK = 4, 8, 8, 2
NC = NX * NZ * NK
V = 32
NB = 64
POSTS = 4
CENT = ("x", "z", "core")
LOW = -3.0e38
HALF = D // 2
P8 = HALF + 256
F32 = jnp.float32
BF = jnp.bfloat16
I32 = jnp.int32
MIB = 1024 * 1024


def iota(shape, dim):
    return lax.broadcasted_iota(I32, shape, dim)


def as_column(row):
    n = row.shape[1]
    eye = iota((n, n), 0) == iota((n, n), 1)
    return jnp.sum(jnp.where(eye, jnp.broadcast_to(row, (n, n)), 0), axis=1, keepdims=True)


def earlier_equal(row):
    n = row.shape[1]
    same = (as_column(row) == row) & (iota((n, n), 0) < iota((n, n), 1))
    return jnp.sum(same.astype(I32), axis=0, keepdims=True)


def one_hot(mask):
    return jnp.where(mask, 1.0, 0.0).astype(BF)


def dot(a, b):
    return jnp.dot(a, b, preferred_element_type=F32)


def dot_nt(a, b):
    return lax.dot_general(a, b, (((1,), (1,)), ((), ())), preferred_element_type=F32)


def pack_kernel(vec_ref, head_ref, assign_ref, npost_ref, nrow_ref, ndest_ref, out_ref, table_ref):
    n = NC * 8
    assign = assign_ref[...]
    dest = assign // POSTS
    zdest = (dest // NK) % NZ
    place = earlier_equal(dest)

    ones = jnp.ones((V, 128), BF)

    def routed(count, per):
        p = iota((count, V), 0)
        to, t = p // per, p % 4
        return (dest == to) & (place == t), (zdest != (to // NK) % NZ)

    named, other = routed(n, 8)
    small, _ = routed(NC * 4, 4)
    free = (1.0 - dot(one_hot(small), ones)).astype(BF)
    p, c = iota((n, NC * 4), 0), iota((n, NC * 4), 1)
    pd, cd = p // 8, c // 4
    slot = ((pd // (NZ * NK)) * NK + pd % NK) * 4 + p % 4
    cslot = ((cd // (NZ * NK)) * NK + cd % NK) * 4 + c % 4
    before = one_hot(((pd // NK) % NZ == (cd // NK) % NZ) & (cslot < slot))
    free_rank = dot(before, free)[:, :V]
    upper = one_hot(iota((V, V), 0) < iota((V, V), 1))
    rest_rank = dot(one_hot(other), upper)
    taken = dot(one_hot(named), ones)[:, :V]
    share = named | (other & (taken < 0.5) & (free_rank == rest_rank))
    low_half = iota((n, V), 0) % 8 < 4
    table = one_hot(share & low_half)
    table_ref[:, :V] = table
    out_ref[:, :HALF] = (
        dot(table, vec_ref[:, :HALF]) + dot(one_hot(share & ~low_half), vec_ref[:, HALF:])
    ).astype(BF)

    ndest = ndest_ref[...]
    nplace = earlier_equal(ndest)
    picks = one_hot(npost_ref[...] * HEAD + nrow_ref[...] == iota((POSTS * HEAD, NB), 0))
    head = head_ref[...].reshape(POSTS * HEAD, D)
    p, c = iota((n, 6 * NC), 0), iota((n, 6 * NC), 1)
    spread = one_hot((p // 8 == c % NC) & (p % 8 == c // NC))
    post = as_column(assign) % POSTS + 1
    mark = jnp.where(iota((V, 128), 1) == as_column(place), post, 0).astype(F32).astype(BF)
    sixth = one_hot((iota((n, V), 0) // 8 == dest) & (iota((n, V), 0) % 8 == 6))
    for t in range(2):
        chosen = one_hot((ndest == iota((NC, NB), 0)) & (nplace == t))
        rows = dot(dot_nt(chosen, picks).astype(BF), head).astype(BF)
        stack = jnp.concatenate([rows[:, 128 * k : 128 * k + 128] for k in range(6)], axis=0)
        tile = dot(spread, stack)
        if t == 0:
            tile = tile + dot(sixth, mark)
        out_ref[:, HALF + 128 * t : HALF + 128 * t + 128] = tile.astype(BF)


def share_kernel(in_ref, share_ref):
    n = NC * 8
    p, i = iota((NC * 4, n), 1), iota((NC * 4, n), 0)
    first = (i // 4) * 8 + i % 4
    rows = in_ref[:, :HALF]
    share_ref[:, :HALF] = dot(one_hot(p == first), rows).astype(BF)
    share_ref[:, HALF:] = dot(one_hot(p == first + 4), rows).astype(BF)


def moved_kernel(in_ref, moved_ref):
    n = NC * 8
    tiles = in_ref[:, HALF:]
    p, i = iota((NC * 2, n), 1), iota((NC * 2, n), 0)
    odd = iota((NC * 2, 128), 0) % 2 == 1
    for k in range(6):
        both = dot(one_hot(p == (i // 2) * 8 + k), tiles)
        moved_ref[:, 128 * k : 128 * k + 128] = jnp.where(odd, both[:, 128:], both[:, :128]).astype(BF)


def spread_kernel(in_ref, share_ref, out_ref, buf_ref, sems):
    n = NC * 8
    p, d = iota((NC, n), 1), iota((NC, n), 0)
    marks = dot(one_hot(p == d * 8 + 6), in_ref[:, HALF : HALF + 128]).astype(BF)
    first = dot_nt(one_hot(iota((8, 128), 1) == 0), marks)
    upper = one_hot(iota((NC, NC), 0) < iota((NC, NC), 1))
    valid = one_hot(first > 0.5)
    rank = dot(valid, upper).astype(BF)
    m = NC * 4
    widen = one_hot(iota((NC, m), 0) == iota((NC, m), 1) // 4)
    valid, rank = dot(valid, widen)[:1], dot(rank, widen)[:1].astype(I32)
    t = iota((V, m), 1) % 4
    hit = one_hot((valid > 0.5) & (t < 2) & (2 * rank + t == iota((V, m), 0)))
    tall = one_hot(iota((m, NC), 1) == iota((m, NC), 0) // 4)
    lane = iota((m, 128), 1)
    mine = jnp.where(lane == iota((m, 128), 0) % 4, dot(tall, marks), 0.0)
    post = jnp.sum(mine, axis=1, keepdims=True)
    buf_ref[:, :D] = dot(hit, share_ref[...]).astype(BF)
    buf_ref[:, D:] = dot(hit, jnp.where(lane == 0, post, 0.0).astype(BF)).astype(BF)
    copies = [pltpu.make_async_copy(buf_ref, out_ref.at[g], sems.at[g]) for g in range(NY)]
    for copy in copies:
        copy.start()
    for copy in copies:
        copy.wait()


def append_kernel(
    fill_ref, split_ref, got_ref, post_ref, prior_ref, member_ref, npost_ref, nrow_ref, nsplit_ref,
    ndest_ref, best_ref, out_ref, count_ref, centers_ref, send_ref,
):
    n = NY * V
    mark = dot_nt(one_hot(iota((8, 128), 1) == 0), got_ref[:, D:]).astype(I32)
    match = mark == iota((8, n), 0) + 1
    upper = one_hot(iota((n, n), 0) < iota((n, n), 1))
    rank = dot(one_hot(match), upper).astype(I32)
    row = iota((ROWS, n), 0)
    line = iota((ROWS, 1), 0)
    got = got_ref[:, :D]
    for q in range(POSTS):
        mine = match[q : q + 1]
        count = jnp.sum(mine.astype(I32))
        first = fill_ref[q]
        table = one_hot(mine & (row == first + rank[q : q + 1]))
        written = dot(table, got)
        hit = (line >= first) & (line < first + count)
        out_ref[q] = jnp.where(hit, written, post_ref[q].astype(F32)).astype(BF)
        count_ref[q] = first + count

    head = post_ref[:, :HEAD, :].reshape(POSTS * HEAD, D).astype(F32)
    members = member_ref[...].astype(F32)
    eye = iota((ROWS, ROWS), 0) == iota((ROWS, ROWS), 1)
    lane = iota((POSTS * HEAD, 128), 1)
    ndest = ndest_ref[...]
    nplace = earlier_equal(ndest)
    nsplit = nsplit_ref[...]
    picks = one_hot(npost_ref[...] * HEAD + nrow_ref[...] == iota((POSTS * HEAD, NB), 0))
    to = iota((NC, NB), 0)
    sent = jnp.zeros((NC, 128), F32)
    for s in range(2):
        j = split_ref[s]
        alive = jnp.where(j >= 0, 1.0, 0.0).astype(F32)
        q = jnp.maximum(j, 0)
        x = out_ref[q].astype(F32)
        own = prior_ref[...].astype(F32)
        prior = jnp.sum(jnp.where(iota(own.shape, 0) == q, own, 0.0), axis=0, keepdims=True)
        mask = jnp.where(line < count_ref[q], 1.0, 0.0).astype(F32)
        weights = jnp.sum(jnp.where(eye, members[s : s + 1], 0.0), axis=1, keepdims=True)

        def update(weights):
            w1, w2 = mask * weights, mask * (1.0 - weights)
            s1 = jnp.sum(w1 * x, axis=0, keepdims=True) + prior
            s2 = jnp.sum(w2 * x, axis=0, keepdims=True) + prior
            t1 = jnp.sum(w1, axis=0, keepdims=True) + 1.0
            t2 = jnp.sum(w2, axis=0, keepdims=True) + 1.0
            return s1 / t1, s2 / t2

        a1, a2 = update(weights)
        for _ in range(ITERS):
            far = jnp.sum(jnp.square(x - a2), axis=1, keepdims=True) - jnp.sum(
                jnp.square(x - a1), axis=1, keepdims=True
            )
            a1, a2 = update(jax.nn.sigmoid(0.125 * far))
        a1, a2 = a1 * alive, a2 * alive
        centers_ref[s, 0:1, :] = a1
        centers_ref[s, 1:2, :] = a2
        c1 = jnp.sum(head * a1, axis=1, keepdims=True)
        c2 = jnp.sum(head * a2, axis=1, keepdims=True)
        for t in range(2):
            where_to = one_hot((ndest == to) & (nplace == t) & (nsplit == s))
            table = dot_nt(where_to, picks).astype(BF)
            values = jnp.where(lane == 32 + 2 * t, c1, jnp.where(lane == 33 + 2 * t, c2, 0.0))
            sent = sent + dot(table, values.astype(BF))
    send_ref[...] = jnp.where(iota((NC, 128), 1) < V, best_ref[...], sent)


BLOCK = 1024


def scan_blocks(ref, part, best):
    for i in range(2048 // BLOCK):
        scores = dot_nt(ref[BLOCK * i : BLOCK * i + BLOCK, :], part)
        best = jnp.maximum(best, jnp.max(scores.reshape(BLOCK // 8, 8, NC * 4), axis=0))
    return best


def first_kernel(own_ref, mate_ref, v_ref, acc_ref, buf_ref, sem):
    copy = pltpu.make_async_copy(mate_ref, buf_ref, sem)
    copy.start()
    best = scan_blocks(own_ref, v_ref[...], jnp.full((8, NC * 4), LOW, F32))
    copy.wait()
    acc_ref[0] = scan_blocks(buf_ref, v_ref[...], best)


def best_kernel(
    place_ref, own_ref, mate_ref, v1_ref, v2_ref, v3_ref, acc0_ref, out_ref, acc_ref, part_ref, buf_ref, sems
):
    copies = [
        pltpu.make_async_copy(v, part_ref.at[a], sems.at[a])
        for a, v in enumerate((v1_ref, v2_ref, v3_ref))
    ] + [pltpu.make_async_copy(mate_ref, buf_ref, sems.at[NX - 1])]
    for copy in copies:
        copy.start()
    for a in range(NX - 1):
        copies[a].wait()
        acc_ref[a] = scan_blocks(own_ref, part_ref[a], jnp.full((8, NC * 4), LOW, F32))
    copies[NX - 1].wait()
    for a in range(NX - 1):
        acc_ref[a] = scan_blocks(buf_ref, part_ref[a], acc_ref[a])
    x, core = place_ref[0], place_ref[1]
    wide = (NC, NC * 4)
    mine = iota(wide, 1) // 4 == iota(wide, 0)
    lane = iota((NC, 128), 1)
    best = jnp.full((NC, 128), LOW, F32)
    for a in range(NX):
        acc = acc0_ref[0] if a == 0 else acc_ref[a - 1]
        top = jnp.max(acc, axis=0, keepdims=True)
        spread = jnp.where(mine, jnp.broadcast_to(top, wide), LOW)
        folded = jnp.maximum(spread[:, :128], spread[:, 128:])
        for shift in (64, 32, 16, 8, 4):
            folded = jnp.maximum(folded, pltpu.roll(folded, shift, 1))
        group = lax.rem(x + NX - a, NX) * NK + core
        best = jnp.where(lane // 4 == group, folded, best)
    out_ref[...] = best


def final_kernel(in_ref, table_ref, best_ref, score_ref):
    got = in_ref[...]
    lane = iota((NC, 128), 1)
    src = iota((NC, 128), 0)
    n = NZ * NK
    pair = jnp.maximum(
        jnp.maximum(got[:n], got[n : 2 * n]), jnp.maximum(got[2 * n : 3 * n], got[3 * n :])
    )
    tops = jnp.concatenate(
        [
            jnp.broadcast_to(jnp.max(pair[NK * z : NK * z + NK], axis=0, keepdims=True), (16, 128))
            for z in range(NZ)
        ],
        axis=0,
    )
    p = iota((128, 128), 0)
    best = jnp.full((1, V), LOW, F32)
    for x in range(NX):
        slot = (x * NK + (p // 8) % NK) * 4 + p % 4
        value = jnp.max(jnp.where(iota((128, 128), 1) == slot, tops, LOW), axis=1, keepdims=True)
        table = table_ref[128 * x : 128 * x + 128, :V].astype(F32)
        best = jnp.maximum(best, jnp.max(jnp.where(table > 0.5, value, LOW), axis=0, keepdims=True))
    best_ref[...] = best
    vals = jnp.where((lane >= 32) & (lane < 36), got, 0.0).astype(BF)
    total = jnp.zeros((8, 128), F32)
    pick = iota((8, 128), 0)
    at = iota((8, 128), 1)
    for t in range(2):
        chosen = one_hot(at == 32 + 2 * t + pick)
        rows = dot_nt(chosen, vals).astype(BF)
        total = total + dot(rows, one_hot(lane == src * 2 + t))
    score_ref[...] = total[:2].astype(BF)


def vm():
    return pl.BlockSpec(memory_space=pltpu.VMEM)


def sm():
    return pl.BlockSpec(memory_space=pltpu.SMEM)


def params(mib=28):
    return pltpu.CompilerParams(vmem_limit_bytes=mib * MIB)


def shards(
    vectors,
    centroids,
    postings,
    fill,
    assign,
    split_posts,
    split_members,
    neigh_post,
    neigh_row,
    neigh_split,
    neigh_dest,
):
    place = jnp.stack([lax.axis_index("x"), lax.axis_index("core")]).astype(I32)
    npost, nrow, nsplit, ndest = (
        a.reshape(1, NB) for a in (neigh_post, neigh_row, neigh_split, neigh_dest)
    )
    one = lambda *shape: pl.BlockSpec(shape, lambda i: (0,) * len(shape))
    packed, table = pl.pallas_call(
        pack_kernel,
        out_shape=(
            jax.ShapeDtypeStruct((NC * 8, P8), BF),
            jax.ShapeDtypeStruct((NC * 8, 128), BF),
        ),
        grid=(1,),
        in_specs=[one(V, D), one(POSTS, HEAD, D), one(1, V), one(1, NB), one(1, NB), one(1, NB)],
        out_specs=(one(NC * 8, P8), one(NC * 8, 128)),
        compiler_params=params(60),
        name="pack_rows",
    )(vectors, postings, assign.reshape(1, V), npost, nrow, ndest)
    held, packed = lax.optimization_barrier((centroids, packed))
    mate = lax.ppermute(held, "core", [(0, 1), (1, 0)])
    got = lax.all_to_all(packed.reshape(NC, 8, P8), CENT, 0, 0, tiled=True).reshape(NC * 8, P8)
    share = pl.pallas_call(
        share_kernel,
        out_shape=jax.ShapeDtypeStruct((NC * 4, D), BF),
        in_specs=[vm()],
        out_specs=vm(),
        compiler_params=params(),
        name="share_rows",
    )(got)
    parts = [lax.ppermute(share, "x", [(i, (i + a) % NX) for i in range(NX)]) for a in range(1, NX)]
    spread = pl.pallas_call(
        spread_kernel,
        out_shape=jax.ShapeDtypeStruct((NY, V, W), BF),
        in_specs=[vm(), vm()],
        out_specs=pl.BlockSpec(memory_space=pltpu.HBM),
        scratch_shapes=[pltpu.VMEM((V, W), BF), pltpu.SemaphoreType.DMA((NY,))],
        compiler_params=params(),
        name="spread_rows",
    )(got, share)
    gathered = lax.all_to_all(spread, "y", 0, 0, tiled=True).reshape(NY * V, W)
    moved_rows = pl.pallas_call(
        moved_kernel,
        out_shape=jax.ShapeDtypeStruct((NC * 2, D), BF),
        in_specs=[vm()],
        out_specs=vm(),
        compiler_params=params(),
        name="moved_rows",
    )(got)

    hbm = pl.BlockSpec(memory_space=pl.ANY)

    def cost(count):
        work = 2 * 4096 * 256 * D * count
        return pl.CostEstimate(flops=work, bytes_accessed=2 * 4096 * D, transcendentals=0)

    first = pl.pallas_call(
        first_kernel,
        out_shape=jax.ShapeDtypeStruct((1, 8, NC * 4), F32),
        in_specs=[vm(), hbm, vm()],
        out_specs=vm(),
        scratch_shapes=[pltpu.VMEM((2048, D), BF), pltpu.SemaphoreType.DMA],
        compiler_params=params(),
        cost_estimate=cost(1),
        name="best_of_share",
    )(centroids, mate, share)
    best = pl.pallas_call(
        best_kernel,
        out_shape=jax.ShapeDtypeStruct((NC, 128), F32),
        in_specs=[sm(), vm(), hbm, hbm, hbm, hbm, vm()],
        out_specs=vm(),
        scratch_shapes=[
            pltpu.VMEM((NX - 1, 8, NC * 4), F32),
            pltpu.VMEM((NX - 1, NC * 4, D), BF),
            pltpu.VMEM((2048, D), BF),
            pltpu.SemaphoreType.DMA((NX,)),
        ],
        compiler_params=params(),
        cost_estimate=cost(3),
        name="best_scores",
    )(place, centroids, mate, *parts, first)
    postings_out, new_fill, split_centers, sending = pl.pallas_call(
        append_kernel,
        out_shape=(
            jax.ShapeDtypeStruct((POSTS, ROWS, D), BF),
            jax.ShapeDtypeStruct((POSTS,), I32),
            jax.ShapeDtypeStruct((2, 2, D), F32),
            jax.ShapeDtypeStruct((NC, 128), F32),
        ),
        grid=(1,),
        in_specs=[
            sm(), sm(), one(NY * V, W), one(POSTS, ROWS, D), one(16, D), one(2, ROWS),
            one(1, NB), one(1, NB), one(1, NB), one(1, NB), one(NC, 128),
        ],
        out_specs=(one(POSTS, ROWS, D), sm(), one(2, 2, D), one(NC, 128)),
        compiler_params=params(60),
        name="append_split",
    )(
        fill, split_posts, gathered, postings, centroids, split_members, npost, nrow, nsplit, ndest,
        best,
    )
    back = lax.all_to_all(sending.reshape(NC, 1, 128), CENT, 0, 0, tiled=True).reshape(NC, 128)
    best_score, moved_scores = pl.pallas_call(
        final_kernel,
        out_shape=(jax.ShapeDtypeStruct((1, V), F32), jax.ShapeDtypeStruct((2, 2 * NC), BF)),
        in_specs=[vm(), vm()],
        out_specs=(vm(), vm()),
        compiler_params=params(),
        name="last_step",
    )(back, table)
    return (
        best_score.reshape(V), postings_out, new_fill, split_centers, moved_rows, moved_scores
    )


def solution(mesh):
    fine = Mesh(mesh.devices.reshape(NY, NX, NZ, NK), ("y", "x", "z", "core"))
    both = ("y",) + CENT
    return jax.shard_map(
        shards,
        mesh=fine,
        in_specs=(
            P(both, None),
            P(CENT, None),
            P(CENT, None, None),
            P(CENT),
            P(both),
            P(CENT),
            P(CENT, None),
            P(both),
            P(both),
            P(both),
            P(both),
        ),
        out_specs=(
            P(both),
            P(CENT, None, None),
            P(CENT),
            P(CENT, None, None),
            P(both, None),
            P(None, both),
        ),
        check_vma=False,
    )
```

time: 109 us -> 97.7 us (0.90)
  blocking collectives: 46.9 us -> 28.2 us
  local copies, waits for them, and re-layouts: 8.43 us -> 1.39 us
  Pallas kernels: 16 us -> 22.6 us
  starting transfers between devices: 25.3 us -> 30.7 us
  waiting for transfers between devices: 10.7 us -> 13.5 us
    all_to_all x2 -> x1, blocking collectives: 46.9 us -> 28.2 us  [shards(): lax.all_to_all(packed.reshape(NC, 8, P8), CENT, 0, 0, tiled=True)]
    pallas_call x2 -> x5, Pallas kernels: 2.09 us -> 10.3 us  [the longest x1 3.81 us: shards(): pl.pallas_call(first_kernel, out_shape=jax.ShapeDtypeStruct((1, 8, NC * 4...]
    all_to_all x0 -> x1, waiting for transfers between devices: none -> 8.2 us  [shards(): lax.all_to_all(sending.reshape(NC, 1, 128), CENT, 0, 0, tiled=True)]
    unnamed x34 -> x12, local copies, waits for them, and re-layouts: 8.43 us -> 1.39 us
    all_to_all x1, waiting for transfers between devices: 6.57 us -> 0.01 us  [shards(): gathered = lax.all_to_all(spread, 'y', 0, 0, tiled=True).reshape(NY * V, W)]
    all_to_all x0 -> x1, starting transfers between devices: none -> 5.64 us  [shards(): lax.all_to_all(sending.reshape(NC, 1, 128), CENT, 0, 0, tiled=True)]
    pallas_call x1, Pallas kernels: 9.58 us -> 7.6 us  [shards(): pl.pallas_call(best_kernel, out_shape=jax.ShapeDtypeStruct((NC, 128), F32...]
    ppermute x3, waiting for transfers between devices: 4.16 us -> 5.25 us  [shards(): lax.ppermute(share, 'x', [(i, (i + a) % NX) for i in range(NX)])]
  transfers between devices with their start and end apart: 5 -> 6, of which waited for: 2 -> 2; matrix products, arithmetic and copies ran while one was open for 1% -> 0% of each run, Pallas kernels for 5% -> 15%
where the time goes in v2:
time: 97.7 us; the launch traced here: 97.2 us
  starting transfers between devices  30.7 us (31%)
  blocking collectives  28.2 us (29%)
  Pallas kernels  22.6 us (23%)
  waiting for transfers between devices  13.5 us (14%)
  local copies, waits for them, and re-layouts  1.39 us (1%)
    all_to_all x1, blocking collectives, shards(): lax.all_to_all(packed.reshape(NC, 8, P8), CENT, 0, 0, tiled=True)  28.2 us
    ppermute x3, starting transfers between devices, shards(): lax.ppermute(share, 'x', [(i, (i + a) % NX) for i in range(NX)])  9.43 us
    ppermute x1, starting transfers between devices, shards(): mate = lax.ppermute(held, 'core', [(0, 1), (1, 0)])  8.78 us
    all_to_all x1, waiting for transfers between devices, shards(): lax.all_to_all(sending.reshape(NC, 1, 128), CENT, 0, 0, tiled=True)  8.2 us
    pallas_call x1, Pallas kernels, shards(): pl.pallas_call(best_kernel, out_shape=jax.ShapeDtypeStruct((NC, 128), F32...  7.6 us
    all_to_all x1, starting transfers between devices, shards(): gathered = lax.all_to_all(spread, 'y', 0, 0, tiled=True).reshape(NY * V, W)  6.82 us
    all_to_all x1, starting transfers between devices, shards(): lax.all_to_all(sending.reshape(NC, 1, 128), CENT, 0, 0, tiled=True)  5.64 us
    ppermute x3, waiting for transfers between devices, shards(): lax.ppermute(share, 'x', [(i, (i + a) % NX) for i in range(NX)])  5.25 us
  transfers between devices with their start and end apart: 6, of which 2 were waited for; matrix products, arithmetic and copies ran while one was open for 0% of the time, Pallas kernels for 15%

profile of v2, /device:TPU:1, one launch (start us, length us, event | category | flops | bytes accessed | tf_op | source)
XLA Modules:
  0.0 97.2 jit_solution(16187215346924668440)
XLA Ops:
  0.6 0.0 copy-start
  0.6 3.7 %pack_rows.1 = (bf16[512,640]{1,0:T(8,128)(2,1)}, bf16[512,128]{1,0:T(8,128)(2,1)}) custom-call(bf16[32,768]{1,0:T(8,128)(2,1)} %vec_ref.1, bf16[4,128,768]{2,1,0:T(8,128)(2,1)} %post_ref.1, s32[1,32]{1,0:T(1,128)} %bitcast.27, s32[1,64]{1,0:T(1,128)} %bitcast.21, s32[1,64]{1,0:T(1,128)} %bitcast.23, s32[1,64]{1,0:T(1,128)} %bitcast.25), custom_call_target="tpu_custom_call" | custom-call | tf_op jit(solution)/shard_map/pack_rows/pallas_call | solution.py:339
  4.3 8.8 %collective-permute-start = (bf16[2048,768]{1,0:T(8,128)(2,1)}, bf16[2048,768]{1,0:T(8,128)(2,1)}, u32[]{:S(2)}, u32[]{:S(2)}) collective-permute-start(bf16[2048,768]{1,0:T(8,128)(2,1)} %prior_ref.1), channel_id=1, source_target_pairs={{0,1},{1,0},{2,3},{3,2},{4,5},{5,4},{6,7},{7,6},{8,9},{9,8},{10,11... | collective-permute-start | bytes 9437192 | tf_op jit(solution)/shard_map/ppermute | solution.py:352
  13.1 28.2 %all_to_all.15 = bf16[64,8,640]{2,1,0:T(8,128)(2,1)S(1)} all-to-all(bf16[64,8,640]{2,1,0:T(8,128)(2,1)} %bitcast.19), channel_id=1, replica_groups=mesh['y'=8,'x'=4,'z'=8,'core'=2] {'x','z','core'}, dimensions={0} | all-to-all | bytes 1310720 | tf_op jit(solution)/shard_map/all_to_all | solution.py:353
  41.3 0.0 copy-start.1
  41.3 0.4 share_rows.1.share_ref.v_ref
  41.7 4.6 %collective-permute-start.3 = (bf16[256,768]{1,0:T(8,128)(2,1)S(1)}, bf16[256,768]{1,0:T(8,128)(2,1)}, u32[]{:S(2)}, u32[]{:S(2)}) collective-permute-start(bf16[256,768]{1,0:T(8,128)(2,1)S(1)} %share_rows.1.share_ref.v_ref), channel_id=1, source_target_pairs={{0,48},{16,0},{32,16},{48,32},{1,49},{17,1},{33,17},{49,33},{2,50}... | collective-permute-start | bytes 1179656 | tf_op jit(solution)/shard_map/ppermute | solution.py:362
  46.3 2.3 %collective-permute-start.2 = (bf16[256,768]{1,0:T(8,128)(2,1)S(1)}, bf16[256,768]{1,0:T(8,128)(2,1)}, u32[]{:S(2)}, u32[]{:S(2)}) collective-permute-start(bf16[256,768]{1,0:T(8,128)(2,1)S(1)} %share_rows.1.share_ref.v_ref), channel_id=1, source_target_pairs={{0,32},{16,48},{32,0},{48,16},{1,33},{17,49},{33,1},{49,17},{2,34}... | collective-permute-start | bytes 1179656 | tf_op jit(solution)/shard_map/ppermute | solution.py:362
  48.6 2.6 %collective-permute-start.1 = (bf16[256,768]{1,0:T(8,128)(2,1)S(1)}, bf16[256,768]{1,0:T(8,128)(2,1)}, u32[]{:S(2)}, u32[]{:S(2)}) collective-permute-start(bf16[256,768]{1,0:T(8,128)(2,1)S(1)} %share_rows.1.share_ref.v_ref), channel_id=1, source_target_pairs={{0,16},{16,32},{32,48},{48,0},{1,17},{17,33},{33,49},{49,1},{2,18}... | collective-permute-start | bytes 1179656 | tf_op jit(solution)/shard_map/ppermute | solution.py:362
  51.2 0.0 copy-done.1
  51.2 1.3 %spread_rows.1 = bf16[8,32,896]{2,1,0:T(8,128)(2,1)S(1)} custom-call(bf16[512,640]{1,0:T(8,128)(2,1)S(1)} %bitcast.16, bf16[256,768]{1,0:T(8,128)(2,1)S(1)} %share_rows.1.share_ref.v_ref), custom_call_target="tpu_custom_call" | custom-call | tf_op jit(solution)/shard_map/spread_rows/pallas_call | solution.py:363
  52.6 0.0 copy-start.3
  52.6 0.8 copy-done.3
  53.3 6.8 %all-to-all-start.1 = ((bf16[8,32,896]{2,1,0:T(8,128)(2,1)}), bf16[8,32,896]{2,1,0:T(8,128)(2,1)}, u32[]{:S(2)}, u32[]{:S(2)}) async-start(bf16[8,32,896]{2,1,0:T(8,128)(2,1)} %copy-done.3), calls=%async_computation.1 | async-start | bytes 917504 | tf_op jit(solution)/shard_map/all_to_all | solution.py:372
  60.2 0.1 pad_add_fusion.place_ref
  60.2 0.0 collective-permute-done.mate_ref
  60.2 0.0 copy-done
  60.2 3.8 %best_of_share.1.acc0_ref = f32[1,8,256]{2,1,0:T(8,128)S(1)} custom-call(bf16[2048,768]{1,0:T(8,128)(2,1)S(1)} %copy-done, bf16[2048,768]{1,0:T(8,128)(2,1)} %collective-permute-done.mate_ref, bf16[256,768]{1,0:T(8,128)(2,1)S(1)} %share_rows.1.share_ref.v_ref), custom_call_target="tpu_custom_call" | custom-call | flops 1610612736 | bytes 6291456 | tf_op jit(solution)/shard_map/best_of_share/pallas_call | solution.py:388
  64.0 0.0 collective-permute-done.3.v3_ref
  64.1 0.0 collective-permute-done.2.v2_ref
  64.1 5.2 %collective-permute-done.1.v1_ref = bf16[256,768]{1,0:T(8,128)(2,1)} collective-permute-done((bf16[256,768]{1,0:T(8,128)(2,1)S(1)}, bf16[256,768]{1,0:T(8,128)(2,1)}, u32[]{:S(2)}, u32[]{:S(2)}) %collective-permute-start.1) | collective-permute-done | bytes 393248 | tf_op jit(solution)/shard_map/ppermute | solution.py:362
  69.3 7.6 %best_scores.1.best_ref = f32[64,128]{1,0:T(8,128)S(1)} custom-call(s32[2]{0:T(128)S(1)} %pad_add_fusion.place_ref, bf16[2048,768]{1,0:T(8,128)(2,1)S(1)} %copy-done, bf16[2048,768]{1,0:T(8,128)(2,1)} %collective-permute-done.mate_ref, bf16[256,768]{1,0:T(8,128)(2,1)} %collective-permute-done.1.v1_ref, bf16[256,768]{1,0:T(8,128)(2,1)} %collective-permute-done.2.v2_ref, ...), custom_call_target="tpu_custom_call" | custom-call | flops 4831838208 | bytes 6291456 | tf_op jit(solution)/shard_map/best_scores/pallas_call | solution.py:398
  76.9 0.0 copy-start.5
  76.9 0.6 copy-done.5
  77.5 0.0 all-to-all-done.1
  77.6 3.9 %append_split.1 = (bf16[4,128,768]{2,1,0:T(8,128)(2,1)}, s32[4]{0:T(128)}, f32[2,2,768]{2,1,0:T(2,128)}, f32[64,128]{1,0:T(8,128)}) custom-call(s32[4]{0:T(128)} %fill_ref.1, s32[2]{0:T(128)} %split_ref.1, bf16[256,896]{1,0:T(8,128)(2,1)} %bitcast.6.got_ref, bf16[4,128,768]{2,1,0:T(8,128)(2,1)} %post_ref.1, bf16[2048,768]{1,0:T(8,128)(2,1)} %prior_ref.1, ...), custom_call_target="tpu_custom_call" | custom-call | tf_op jit(solution)/shard_map/append_split/pallas_call | solution.py:413
  81.5 5.6 %all-to-all-start.2 = ((f32[64,1,128]{2,1,0:T(1,128)}), f32[64,1,128]{2,1,0:T(1,128)S(1)}, u32[]{:S(2)}, u32[]{:S(2)}) async-start(f32[64,1,128]{2,1,0:T(1,128)} %bitcast.20), calls=%async_computation.2 | async-start | bytes 65536 | tf_op jit(solution)/shard_map/all_to_all | solution.py:433
  87.1 0.0 copy-done.2
  87.1 1.1 %moved_rows.1 = bf16[128,768]{1,0:T(8,128)(2,1)} custom-call(bf16[512,640]{1,0:T(8,128)(2,1)S(1)} %bitcast.17), custom_call_target="tpu_custom_call" | custom-call | tf_op jit(solution)/shard_map/moved_rows/pallas_call | solution.py:373
  88.2 8.2 %all-to-all-done.2 = f32[64,1,128]{2,1,0:T(1,128)S(1)} async-done(((f32[64,1,128]{2,1,0:T(1,128)}), f32[64,1,128]{2,1,0:T(1,128)S(1)}, u32[]{:S(2)}, u32[]{:S(2)}) %all-to-all-start.2) | async-done | bytes 32800 | tf_op jit(solution)/shard_map/all_to_all | solution.py:433
  96.4 0.0 copy-done.4
  96.4 0.8 last_step.1
  (2 shorter events, 0.0 us)
Async XLA Ops:
  0.6 59.6 %copy-start = (bf16[2048,768]{1,0:T(8,128)(2,1)S(1)}, bf16[2048,768]{1,0:T(8,128)(2,1)}, u32[]{:S(2)}) copy-start(bf16[2048,768]{1,0:T(8,128)(2,1)} %prior_ref.1) | copy-start | bytes 9437188
  4.3 55.9 %collective-permute-start = (bf16[2048,768]{1,0:T(8,128)(2,1)}, bf16[2048,768]{1,0:T(8,128)(2,1)}, u32[]{:S(2)}, u32[]{:S(2)}) collective-permute-start(bf16[2048,768]{1,0:T(8,128)(2,1)} %prior_ref.1), channel_id=1, source_target_pairs={{0,1},{1,0},{2,3},{3,2},{4,5},{5,4},{6,7},{7,6},{8,9},{9,8},{10,11... | collective-permute-start | bytes 9437192 | tf_op jit(solution)/shard_map/ppermute | solution.py:352
  41.3 9.9 %copy-start.1 = (bf16[64,8,640]{2,1,0:T(8,128)(2,1)}, bf16[64,8,640]{2,1,0:T(8,128)(2,1)S(1)}, u32[]{:S(2)}) copy-start(bf16[64,8,640]{2,1,0:T(8,128)(2,1)S(1)} %all_to_all.15) | copy-start | bytes 1966084
  41.7 22.3 %collective-permute-start.3 = (bf16[256,768]{1,0:T(8,128)(2,1)S(1)}, bf16[256,768]{1,0:T(8,128)(2,1)}, u32[]{:S(2)}, u32[]{:S(2)}) collective-permute-start(bf16[256,768]{1,0:T(8,128)(2,1)S(1)} %share_rows.1.share_ref.v_ref), channel_id=1, source_target_pairs={{0,48},{16,0},{32,16},{48,32},{1,49},{17,1},{33,17},{49,33},{2,50}... | collective-permute-start | bytes 1179656 | tf_op jit(solution)/shard_map/ppermute | solution.py:362
  46.3 17.7 %collective-permute-start.2 = (bf16[256,768]{1,0:T(8,128)(2,1)S(1)}, bf16[256,768]{1,0:T(8,128)(2,1)}, u32[]{:S(2)}, u32[]{:S(2)}) collective-permute-start(bf16[256,768]{1,0:T(8,128)(2,1)S(1)} %share_rows.1.share_ref.v_ref), channel_id=1, source_target_pairs={{0,32},{16,48},{32,0},{48,16},{1,33},{17,49},{33,1},{49,17},{2,34}... | collective-permute-start | bytes 1179656 | tf_op jit(solution)/shard_map/ppermute | solution.py:362
  48.6 20.7 %collective-permute-start.1 = (bf16[256,768]{1,0:T(8,128)(2,1)S(1)}, bf16[256,768]{1,0:T(8,128)(2,1)}, u32[]{:S(2)}, u32[]{:S(2)}) collective-permute-start(bf16[256,768]{1,0:T(8,128)(2,1)S(1)} %share_rows.1.share_ref.v_ref), channel_id=1, source_target_pairs={{0,16},{16,32},{32,48},{48,0},{1,17},{17,33},{33,49},{49,1},{2,18}... | collective-permute-start | bytes 1179656 | tf_op jit(solution)/shard_map/ppermute | solution.py:362
  52.6 0.8 copy-start.3
  53.3 24.2 %all-to-all-start.1 = ((bf16[8,32,896]{2,1,0:T(8,128)(2,1)}), bf16[8,32,896]{2,1,0:T(8,128)(2,1)}, u32[]{:S(2)}, u32[]{:S(2)}) async-start(bf16[8,32,896]{2,1,0:T(8,128)(2,1)} %copy-done.3), calls=%async_computation.1 | async-start | bytes 917504 | tf_op jit(solution)/shard_map/all_to_all | solution.py:372
  76.9 0.6 copy-start.5
  77.5 9.6 %copy-start.2 = (bf16[64,8,640]{2,1,0:T(8,128)(2,1)S(1)}, bf16[64,8,640]{2,1,0:T(8,128)(2,1)}, u32[]{:S(2)}) copy-start(bf16[64,8,640]{2,1,0:T(8,128)(2,1)} %copy-done.1) | copy-start | bytes 1966084
  77.5 18.9 %copy-start.4 = (bf16[512,128]{1,0:T(8,128)(2,1)S(1)}, bf16[512,128]{1,0:T(8,128)(2,1)}, u32[]{:S(2)}) copy-start(bf16[512,128]{1,0:T(8,128)(2,1)} %get-tuple-element.20.table_ref) | copy-start | bytes 393220
  81.5 14.9 %all-to-all-start.2 = ((f32[64,1,128]{2,1,0:T(1,128)}), f32[64,1,128]{2,1,0:T(1,128)S(1)}, u32[]{:S(2)}, u32[]{:S(2)}) async-start(f32[64,1,128]{2,1,0:T(1,128)} %bitcast.20), calls=%async_computation.2 | async-start | bytes 65536 | tf_op jit(solution)/shard_map/all_to_all | solution.py:433

commit v3 on v2

--- a/solution.py
+++ b/solution.py
@@ -53,6 +53,14 @@
 
 def dot_nt(a, b):
     return lax.dot_general(a, b, (((1,), (1,)), ((), ())), preferred_element_type=F32)
+
+
+def fetch(pairs, sems):
+    copies = [pltpu.make_async_copy(src, dst, sems.at[i]) for i, (src, dst) in enumerate(pairs)]
+    for copy in copies:
+        copy.start()
+    for copy in copies:
+        copy.wait()
 
 
 def pack_kernel(vec_ref, head_ref, assign_ref, npost_ref, nrow_ref, ndest_ref, out_ref, table_ref):
@@ -153,28 +161,51 @@
         copy.wait()
 
 
-def append_kernel(
-    fill_ref, split_ref, got_ref, post_ref, prior_ref, member_ref, npost_ref, nrow_ref, nsplit_ref,
-    ndest_ref, best_ref, out_ref, count_ref, centers_ref, send_ref,
+def ranks(got, posts):
+    n = NY * V
+    mark = dot_nt(one_hot(iota((8, 128), 1) == 0), got).astype(I32)
+    row = iota((8, n), 0)
+    wanted = jnp.zeros((8, n), I32)
+    for i, q in enumerate(posts):
+        wanted = jnp.where(row == i, q + 1, wanted)
+    match = mark == wanted
+    upper = one_hot(iota((n, n), 0) < iota((n, n), 1))
+    return match, dot(one_hot(match), upper).astype(I32)
+
+
+def appended(match, rank, i, first, got, before):
+    mine = match[i : i + 1]
+    count = jnp.sum(mine.astype(I32))
+    table = one_hot(mine & (iota((ROWS, NY * V), 0) == first + rank[i : i + 1]))
+    line = iota((ROWS, 1), 0)
+    hit = (line >= first) & (line < first + count)
+    return jnp.where(hit, dot(table, got), before), first + count
+
+
+def append_kernel(fill_in, got_in, post_ref, out_ref, count_ref, got_ref, fill_ref, sems):
+    fetch([(fill_in, fill_ref), (got_in, got_ref)], sems)
+    match, rank = ranks(got_ref[:, D:], range(POSTS))
+    for q in range(POSTS):
+        rows, count = appended(
+            match, rank, q, fill_ref[q], got_ref[:, :D], post_ref[q].astype(F32)
+        )
+        out_ref[q] = rows.astype(BF)
+        count_ref[q] = count
+
+
+def split_kernel(
+    fill_in, split_in, got_in, member_in, npost_in, nrow_in, nsplit_in, ndest_in, post_ref, own_ref, best_ref,
+    centers_ref, send_ref,
+    fill_ref, split_ref, got_ref, member_ref, npost_ref, nrow_ref, nsplit_ref, ndest_ref, sems,
 ):
-    n = NY * V
-    mark = dot_nt(one_hot(iota((8, 128), 1) == 0), got_ref[:, D:]).astype(I32)
-    match = mark == iota((8, n), 0) + 1
-    upper = one_hot(iota((n, n), 0) < iota((n, n), 1))
-    rank = dot(one_hot(match), upper).astype(I32)
-    row = iota((ROWS, n), 0)
+    fetch(
+        [
+            (fill_in, fill_ref), (split_in, split_ref), (got_in, got_ref), (member_in, member_ref),
+            (npost_in, npost_ref), (nrow_in, nrow_ref), (nsplit_in, nsplit_ref), (ndest_in, ndest_ref),
+        ],
+        sems,
+    )
     line = iota((ROWS, 1), 0)
-    got = got_ref[:, :D]
-    for q in range(POSTS):
-        mine = match[q : q + 1]
-        count = jnp.sum(mine.astype(I32))
-        first = fill_ref[q]
-        table = one_hot(mine & (row == first + rank[q : q + 1]))
-        written = dot(table, got)
-        hit = (line >= first) & (line < first + count)
-        out_ref[q] = jnp.where(hit, written, post_ref[q].astype(F32)).astype(BF)
-        count_ref[q] = first + count
-
     head = post_ref[:, :HEAD, :].reshape(POSTS * HEAD, D).astype(F32)
     members = member_ref[...].astype(F32)
     eye = iota((ROWS, ROWS), 0) == iota((ROWS, ROWS), 1)
@@ -184,15 +215,16 @@
     nsplit = nsplit_ref[...]
     picks = one_hot(npost_ref[...] * HEAD + nrow_ref[...] == iota((POSTS * HEAD, NB), 0))
     to = iota((NC, NB), 0)
+    own = own_ref[:16, :].astype(F32)
+    posts = [jnp.maximum(split_ref[s], 0) for s in range(2)]
+    match, rank = ranks(got_ref[:, D:], posts)
     sent = jnp.zeros((NC, 128), F32)
     for s in range(2):
-        j = split_ref[s]
-        alive = jnp.where(j >= 0, 1.0, 0.0).astype(F32)
-        q = jnp.maximum(j, 0)
-        x = out_ref[q].astype(F32)
-        own = prior_ref[...].astype(F32)
+        q = posts[s]
+        alive = jnp.where(split_ref[s] >= 0, 1.0, 0.0).astype(F32)
+        x, filled = appended(match, rank, s, fill_ref[q], got_ref[:, :D], post_ref[q].astype(F32))
         prior = jnp.sum(jnp.where(iota(own.shape, 0) == q, own, 0.0), axis=0, keepdims=True)
-        mask = jnp.where(line < count_ref[q], 1.0, 0.0).astype(F32)
+        mask = jnp.where(line < filled, 1.0, 0.0).astype(F32)
         weights = jnp.sum(jnp.where(eye, members[s : s + 1], 0.0), axis=1, keepdims=True)
 
         def update(weights):
@@ -232,37 +264,38 @@
     return best
 
 
-def first_kernel(own_ref, mate_ref, v_ref, acc_ref, buf_ref, sem):
-    copy = pltpu.make_async_copy(mate_ref, buf_ref, sem)
-    copy.start()
-    best = scan_blocks(own_ref, v_ref[...], jnp.full((8, NC * 4), LOW, F32))
-    copy.wait()
-    acc_ref[0] = scan_blocks(buf_ref, v_ref[...], best)
-
-
-def best_kernel(
-    place_ref, own_ref, mate_ref, v1_ref, v2_ref, v3_ref, acc0_ref, out_ref, acc_ref, part_ref, buf_ref, sems
-):
-    copies = [
-        pltpu.make_async_copy(v, part_ref.at[a], sems.at[a])
-        for a, v in enumerate((v1_ref, v2_ref, v3_ref))
-    ] + [pltpu.make_async_copy(mate_ref, buf_ref, sems.at[NX - 1])]
+def first_kernel(own_ref, mate_in, v_ref, v1_in, v2_in, acc_ref, mate_ref, part_ref, sems):
+    pairs = ((v1_in, part_ref.at[0]), (v2_in, part_ref.at[1]), (mate_in, mate_ref))
+    copies = [pltpu.make_async_copy(src, dst, sems.at[i]) for i, (src, dst) in enumerate(pairs)]
     for copy in copies:
         copy.start()
-    for a in range(NX - 1):
-        copies[a].wait()
-        acc_ref[a] = scan_blocks(own_ref, part_ref[a], jnp.full((8, NC * 4), LOW, F32))
-    copies[NX - 1].wait()
-    for a in range(NX - 1):
-        acc_ref[a] = scan_blocks(buf_ref, part_ref[a], acc_ref[a])
+    blank = jnp.full((8, NC * 4), LOW, F32)
+    acc_ref[0] = scan_blocks(own_ref, v_ref[...], blank)
+    copies[0].wait()
+    acc_ref[1] = scan_blocks(own_ref, part_ref[0], blank)
+    copies[1].wait()
+    acc_ref[2] = scan_blocks(own_ref, part_ref[1], blank)
+    copies[2].wait()
+    acc_ref[0] = scan_blocks(mate_ref, v_ref[...], acc_ref[0])
+    acc_ref[1] = scan_blocks(mate_ref, part_ref[0], acc_ref[1])
+    acc_ref[2] = scan_blocks(mate_ref, part_ref[1], acc_ref[2])
+
+
+def best_kernel(
+    place_ref, own_ref, mate_ref, v_in, post_in, acc_ref, out_ref, post_ref, part_ref, sems
+):
+    later = pltpu.make_async_copy(post_in, post_ref, sems.at[1])
+    fetch([(v_in, part_ref)], sems)
+    later.start()
+    best = scan_blocks(own_ref, part_ref[...], jnp.full((8, NC * 4), LOW, F32))
+    accs = [acc_ref[0], acc_ref[1], scan_blocks(mate_ref, part_ref[...], best), acc_ref[2]]
     x, core = place_ref[0], place_ref[1]
     wide = (NC, NC * 4)
     mine = iota(wide, 1) // 4 == iota(wide, 0)
     lane = iota((NC, 128), 1)
     best = jnp.full((NC, 128), LOW, F32)
     for a in range(NX):
-        acc = acc0_ref[0] if a == 0 else acc_ref[a - 1]
-        top = jnp.max(acc, axis=0, keepdims=True)
+        top = jnp.max(accs[a], axis=0, keepdims=True)
         spread = jnp.where(mine, jnp.broadcast_to(top, wide), LOW)
         folded = jnp.maximum(spread[:, :128], spread[:, 128:])
         for shift in (64, 32, 16, 8, 4):
@@ -270,6 +303,7 @@
         group = lax.rem(x + NX - a, NX) * NK + core
         best = jnp.where(lane // 4 == group, folded, best)
     out_ref[...] = best
+    later.wait()
 
 
 def final_kernel(in_ref, table_ref, best_ref, score_ref):
@@ -336,6 +370,7 @@
         a.reshape(1, NB) for a in (neigh_post, neigh_row, neigh_split, neigh_dest)
     )
     one = lambda *shape: pl.BlockSpec(shape, lambda i: (0,) * len(shape))
+    hbm = pl.BlockSpec(memory_space=pl.ANY)
     packed, table = pl.pallas_call(
         pack_kernel,
         out_shape=(
@@ -348,8 +383,6 @@
         compiler_params=params(60),
         name="pack_rows",
     )(vectors, postings, assign.reshape(1, V), npost, nrow, ndest)
-    held, packed = lax.optimization_barrier((centroids, packed))
-    mate = lax.ppermute(held, "core", [(0, 1), (1, 0)])
     got = lax.all_to_all(packed.reshape(NC, 8, P8), CENT, 0, 0, tiled=True).reshape(NC * 8, P8)
     share = pl.pallas_call(
         share_kernel,
@@ -359,7 +392,9 @@
         compiler_params=params(),
         name="share_rows",
     )(got)
-    parts = [lax.ppermute(share, "x", [(i, (i + a) % NX) for i in range(NX)]) for a in range(1, NX)]
+    held, _ = lax.optimization_barrier((centroids, share))
+    mate = lax.ppermute(held, "core", [(0, 1), (1, 0)])
+    parts = {a: lax.ppermute(share, "x", [(i, (i + a) % NX) for i in range(NX)]) for a in (2, 1, 3)}
     spread = pl.pallas_call(
         spread_kernel,
         out_shape=jax.ShapeDtypeStruct((NY, V, W), BF),
@@ -379,57 +414,68 @@
         name="moved_rows",
     )(got)
 
-    hbm = pl.BlockSpec(memory_space=pl.ANY)
-
     def cost(count):
         work = 2 * 4096 * 256 * D * count
         return pl.CostEstimate(flops=work, bytes_accessed=2 * 4096 * D, transcendentals=0)
 
-    first = pl.pallas_call(
+    first, mate = pl.pallas_call(
         first_kernel,
-        out_shape=jax.ShapeDtypeStruct((1, 8, NC * 4), F32),
-        in_specs=[vm(), hbm, vm()],
-        out_specs=vm(),
-        scratch_shapes=[pltpu.VMEM((2048, D), BF), pltpu.SemaphoreType.DMA],
-        compiler_params=params(),
-        cost_estimate=cost(1),
-        name="best_of_share",
-    )(centroids, mate, share)
-    best = pl.pallas_call(
+        out_shape=(
+            jax.ShapeDtypeStruct((NX - 1, 8, NC * 4), F32),
+            jax.ShapeDtypeStruct((2048, D), BF),
+        ),
+        in_specs=[vm(), hbm, vm(), hbm, hbm],
+        out_specs=(vm(), vm()),
+        scratch_shapes=[pltpu.VMEM((2, NC * 4, D), BF), pltpu.SemaphoreType.DMA((3,))],
+        compiler_params=params(),
+        cost_estimate=cost(3),
+        name="best_of_three",
+    )(centroids, mate, share, parts[1], parts[3])
+    best, post_copy = pl.pallas_call(
         best_kernel,
-        out_shape=jax.ShapeDtypeStruct((NC, 128), F32),
-        in_specs=[sm(), vm(), hbm, hbm, hbm, hbm, vm()],
-        out_specs=vm(),
-        scratch_shapes=[
-            pltpu.VMEM((NX - 1, 8, NC * 4), F32),
-            pltpu.VMEM((NX - 1, NC * 4, D), BF),
-            pltpu.VMEM((2048, D), BF),
-            pltpu.SemaphoreType.DMA((NX,)),
-        ],
+        out_shape=(
+            jax.ShapeDtypeStruct((NC, 128), F32),
+            jax.ShapeDtypeStruct((POSTS, ROWS, D), BF),
+        ),
+        in_specs=[sm(), vm(), vm(), hbm, hbm, vm()],
+        out_specs=(vm(), vm()),
+        scratch_shapes=[pltpu.VMEM((NC * 4, D), BF), pltpu.SemaphoreType.DMA((2,))],
         compiler_params=params(),
         cost_estimate=cost(3),
         name="best_scores",
-    )(place, centroids, mate, *parts, first)
-    postings_out, new_fill, split_centers, sending = pl.pallas_call(
+    )(place, centroids, mate, parts[2], postings, first)
+    row = pltpu.VMEM((1, NB), I32)
+    split_centers, sending = pl.pallas_call(
+        split_kernel,
+        out_shape=(
+            jax.ShapeDtypeStruct((2, 2, D), F32),
+            jax.ShapeDtypeStruct((NC, 128), F32),
+        ),
+        in_specs=[hbm] * 8 + [vm()] * 3,
+        out_specs=(vm(), vm()),
+        scratch_shapes=[
+            pltpu.SMEM((POSTS,), I32), pltpu.SMEM((2,), I32), pltpu.VMEM((NY * V, W), BF),
+            pltpu.VMEM((2, ROWS), I32), row, row, row, row, pltpu.SemaphoreType.DMA((8,)),
+        ],
+        compiler_params=params(),
+        name="split_scores",
+    )(
+        fill, split_posts, gathered, split_members, npost, nrow, nsplit, ndest, post_copy, centroids, best
+    )
+    postings_out, new_fill = pl.pallas_call(
         append_kernel,
         out_shape=(
             jax.ShapeDtypeStruct((POSTS, ROWS, D), BF),
             jax.ShapeDtypeStruct((POSTS,), I32),
-            jax.ShapeDtypeStruct((2, 2, D), F32),
-            jax.ShapeDtypeStruct((NC, 128), F32),
-        ),
-        grid=(1,),
-        in_specs=[
-            sm(), sm(), one(NY * V, W), one(POSTS, ROWS, D), one(16, D), one(2, ROWS),
-            one(1, NB), one(1, NB), one(1, NB), one(1, NB), one(NC, 128),
+        ),
+        in_specs=[hbm, hbm, vm()],
+        out_specs=(vm(), sm()),
+        scratch_shapes=[
+            pltpu.VMEM((NY * V, W), BF), pltpu.SMEM((POSTS,), I32), pltpu.SemaphoreType.DMA((2,)),
         ],
-        out_specs=(one(POSTS, ROWS, D), sm(), one(2, 2, D), one(NC, 128)),
-        compiler_params=params(60),
-        name="append_split",
-    )(
-        fill, split_posts, gathered, postings, centroids, split_members, npost, nrow, nsplit, ndest,
-        best,
-    )
+        compiler_params=params(),
+        name="append_rows",
+    )(fill, gathered, post_copy)
     back = lax.all_to_all(sending.reshape(NC, 1, 128), CENT, 0, 0, tiled=True).reshape(NC, 128)
     best_score, moved_scores = pl.pallas_call(
         final_kernel,

time: 97.7 us -> 102 us (1.044)
  blocking collectives: 28.2 us -> 35 us
  waiting for transfers between devices: 13.5 us -> 8.17 us
  Pallas kernels: 22.6 us -> 26.9 us
  local copies, waits for them, and re-layouts: 1.39 us -> 0.05 us
    all_to_all x1, blocking collectives: 28.2 us -> 35 us  [shards(): lax.all_to_all(packed.reshape(NC, 8, P8), CENT, 0, 0, tiled=True)]
    ppermute x1, starting transfers between devices: 8.78 us -> 2.2 us  [shards(): mate = lax.ppermute(held, 'core', [(0, 1), (1, 0)])]
    all_to_all x1, starting transfers between devices: 5.64 us -> 12.1 us  [shards(): lax.all_to_all(sending.reshape(NC, 1, 128), CENT, 0, 0, tiled=True)]
    pallas_call x2 -> x3, Pallas kernels: 11.4 us -> 17.5 us  [the longest x1 8.04 us: shards(): pl.pallas_call(first_kernel, out_shape=(jax.ShapeDtypeStruct((NX - 1, 8,...]
    ppermute x3, waiting for transfers between devices: 5.25 us -> 0.01 us  [shards(): lax.ppermute(share, 'x', [(i, (i + a) % NX) for i in range(NX)])]
    all_to_all x1, waiting for transfers between devices: 8.2 us -> 6.12 us  [shards(): lax.all_to_all(sending.reshape(NC, 1, 128), CENT, 0, 0, tiled=True)]
    all_to_all x1, waiting for transfers between devices: 0.01 us -> 2.04 us  [shards(): gathered = lax.all_to_all(spread, 'y', 0, 0, tiled=True).reshape(NY * V, W)]
    pallas_call x1, Pallas kernels: 3.91 us -> 2.08 us  [shards(): pl.pallas_call(append_kernel, out_shape=(jax.ShapeDtypeStruct((POSTS, ROW...]
  transfers between devices with their start and end apart: 6 -> 6, of which waited for: 2 -> 2; matrix products, arithmetic and copies ran while one was open for 0% -> 0% of each run, Pallas kernels for 15% -> 17%
where the time goes in v3:
time: 102 us
  blocking collectives  35 us (34%)
  starting transfers between devices  30.9 us (30%)
  Pallas kernels  26.9 us (26%)
  waiting for transfers between devices  8.17 us (8%)
    all_to_all x1, blocking collectives, shards(): lax.all_to_all(packed.reshape(NC, 8, P8), CENT, 0, 0, tiled=True)  35 us
    all_to_all x1, starting transfers between devices, shards(): lax.all_to_all(sending.reshape(NC, 1, 128), CENT, 0, 0, tiled=True)  12.1 us
    ppermute x3, starting transfers between devices, shards(): lax.ppermute(share, 'x', [(i, (i + a) % NX) for i in range(NX)])  9.74 us
    pallas_call x1, Pallas kernels, shards(): pl.pallas_call(first_kernel, out_shape=(jax.ShapeDtypeStruct((NX - 1, 8,...  8.04 us
    all_to_all x1, starting transfers between devices, shards(): gathered = lax.all_to_all(spread, 'y', 0, 0, tiled=True).reshape(NY * V, W)  6.84 us
    all_to_all x1, waiting for transfers between devices, shards(): lax.all_to_all(sending.reshape(NC, 1, 128), CENT, 0, 0, tiled=True)  6.12 us
    pallas_call x1, Pallas kernels, shards(): pl.pallas_call(split_kernel, out_shape=(jax.ShapeDtypeStruct((2, 2, D), F...  5.08 us
    pallas_call x1, Pallas kernels, shards(): pl.pallas_call(best_kernel, out_shape=(jax.ShapeDtypeStruct((NC, 128), F3...  4.38 us
  transfers between devices with their start and end apart: 6, of which 2 were waited for; matrix products, arithmetic and copies ran while one was open for 0% of the time, Pallas kernels for 17%

profile of v3, /device:TPU:1, one launch (start us, length us, event | category | flops | bytes accessed | tf_op | source)
XLA Modules:
  0.0 101.9 jit_solution(7779580644760187943)
XLA Ops:
  0.6 3.5 %pack_rows.1 = (bf16[512,640]{1,0:T(8,128)(2,1)}, bf16[512,128]{1,0:T(8,128)(2,1)}) custom-call(bf16[32,768]{1,0:T(8,128)(2,1)} %vec_ref.1, bf16[4,128,768]{2,1,0:T(8,128)(2,1)} %post_in.1, s32[1,32]{1,0:T(1,128)} %bitcast.29, s32[1,64]{1,0:T(1,128)} %bitcast.21, s32[1,64]{1,0:T(1,128)} %bitcast.23, s32[1,64]{1,0:T(1,128)} %bitcast.25), custom_call_target="tpu_custom_call" | custom-call | tf_op jit(solution)/shard_map/pack_rows/pallas_call | solution.py:374
  4.2 35.0 %all_to_all.15 = bf16[64,8,640]{2,1,0:T(8,128)(2,1)S(1)} all-to-all(bf16[64,8,640]{2,1,0:T(8,128)(2,1)} %bitcast.28), channel_id=1, replica_groups=mesh['y'=8,'x'=4,'z'=8,'core'=2] {'x','z','core'}, dimensions={0} | all-to-all | bytes 1310720 | tf_op jit(solution)/shard_map/all_to_all | solution.py:386
  39.1 0.4 share_rows.1.share_ref.v_ref
  39.5 2.2 %collective-permute-start = (bf16[2048,768]{1,0:T(8,128)(2,1)}, bf16[2048,768]{1,0:T(8,128)(2,1)}, u32[]{:S(2)}, u32[]{:S(2)}) collective-permute-start(bf16[2048,768]{1,0:T(8,128)(2,1)} %own_ref.5), channel_id=1, source_target_pairs={{0,1},{1,0},{2,3},{3,2},{4,5},{5,4},{6,7},{7,6},{8,9},{9,8},{10,11... | collective-permute-start | bytes 9437192 | tf_op jit(solution)/shard_map/ppermute | solution.py:396
  41.8 2.9 %collective-permute-start.1 = (bf16[256,768]{1,0:T(8,128)(2,1)S(1)}, bf16[256,768]{1,0:T(8,128)(2,1)S(1)}, u32[]{:S(2)}, u32[]{:S(2)}) collective-permute-start(bf16[256,768]{1,0:T(8,128)(2,1)S(1)} %share_rows.1.share_ref.v_ref), channel_id=1, source_target_pairs={{0,16},{16,32},{32,48},{48,0},{1,17},{17,33},{33,49},{49,1},{2,18}... | collective-permute-start | bytes 1179656 | tf_op jit(solution)/shard_map/ppermute | solution.py:397
  44.6 3.6 %collective-permute-start.2 = (bf16[256,768]{1,0:T(8,128)(2,1)S(1)}, bf16[256,768]{1,0:T(8,128)(2,1)S(1)}, u32[]{:S(2)}, u32[]{:S(2)}) collective-permute-start(bf16[256,768]{1,0:T(8,128)(2,1)S(1)} %share_rows.1.share_ref.v_ref), channel_id=1, source_target_pairs={{0,48},{16,0},{32,16},{48,32},{1,49},{17,1},{33,17},{49,33},{2,50}... | collective-permute-start | bytes 1179656 | tf_op jit(solution)/shard_map/ppermute | solution.py:397
  48.3 0.1 pad_add_fusion.place_ref
  48.3 3.2 %collective-permute-start.3 = (bf16[256,768]{1,0:T(8,128)(2,1)S(1)}, bf16[256,768]{1,0:T(8,128)(2,1)S(1)}, u32[]{:S(2)}, u32[]{:S(2)}) collective-permute-start(bf16[256,768]{1,0:T(8,128)(2,1)S(1)} %share_rows.1.share_ref.v_ref), channel_id=1, source_target_pairs={{0,32},{16,48},{32,0},{48,16},{1,33},{17,49},{33,1},{49,17},{2,34}... | collective-permute-start | bytes 1179656 | tf_op jit(solution)/shard_map/ppermute | solution.py:397
  51.6 1.5 %spread_rows.1 = bf16[8,32,896]{2,1,0:T(8,128)(2,1)} custom-call(bf16[512,640]{1,0:T(8,128)(2,1)S(1)} %bitcast.16, bf16[256,768]{1,0:T(8,128)(2,1)S(1)} %share_rows.1.share_ref.v_ref), custom_call_target="tpu_custom_call" | custom-call | tf_op jit(solution)/shard_map/spread_rows/pallas_call | solution.py:398
  53.1 6.8 %all-to-all-start.1 = ((bf16[8,32,896]{2,1,0:T(8,128)(2,1)}), bf16[8,32,896]{2,1,0:T(8,128)(2,1)S(1)}, u32[]{:S(2)}, u32[]{:S(2)}) async-start(bf16[8,32,896]{2,1,0:T(8,128)(2,1)} %spread_rows.1), calls=%async_computation.1 | async-start | bytes 917504 | tf_op jit(solution)/shard_map/all_to_all | solution.py:407
  60.0 0.0 collective-permute-done.1.v1_in
  60.0 0.0 collective-permute-done.2.v2_in
  60.0 0.0 collective-permute-done.mate_in
  60.0 8.0 %best_of_three.1 = (f32[3,8,256]{2,1,0:T(8,128)S(1)}, bf16[2048,768]{1,0:T(8,128)(2,1)S(1)}) custom-call(bf16[2048,768]{1,0:T(8,128)(2,1)} %own_ref.5, bf16[2048,768]{1,0:T(8,128)(2,1)} %collective-permute-done.mate_in, bf16[256,768]{1,0:T(8,128)(2,1)S(1)} %share_rows.1.share_ref.v_ref, bf16[256,768]{1,0:T(8,128)(2,1)S(1)} %collective-permute-done.1.v1_in, ...), custom_call_target="tpu_custom_call" | custom-call | flops 4831838208 | bytes 6291456 | tf_op jit(solution)/shard_map/best_of_three/pallas_call | solution.py:421
  68.0 0.0 collective-permute-done.3.v_in
  68.0 0.0 copy-done
  68.1 0.0 copy-start.2
  68.1 0.0 copy-start.3
  68.1 0.0 copy-start.4
  68.1 0.0 copy-start.5
  68.1 0.0 copy-start.6
  68.1 0.0 copy-start.7
  68.1 0.0 copy-start.8
  68.1 4.4 %best_scores.1 = (f32[64,128]{1,0:T(8,128)S(1)}, bf16[4,128,768]{2,1,0:T(8,128)(2,1)S(1)}) custom-call(s32[2]{0:T(128)S(1)} %pad_add_fusion.place_ref, bf16[2048,768]{1,0:T(8,128)(2,1)} %own_ref.5, bf16[2048,768]{1,0:T(8,128)(2,1)S(1)} %get-tuple-element.21.mate_ref, bf16[256,768]{1,0:T(8,128)(2,1)S(1)} %collective-permute-done.3.v_in, ...), custom_call_target="tpu_custom_call" | custom-call | flops 4831838208 | bytes 6291456 | tf_op jit(solution)/shard_map/best_scores/pallas_call | solution.py:434
  72.5 2.0 %all-to-all-done.1 = bf16[8,32,896]{2,1,0:T(8,128)(2,1)S(1)} async-done(((bf16[8,32,896]{2,1,0:T(8,128)(2,1)}), bf16[8,32,896]{2,1,0:T(8,128)(2,1)S(1)}, u32[]{:S(2)}, u32[]{:S(2)}) %all-to-all-start.1) | async-done | bytes 458784 | tf_op jit(solution)/shard_map/all_to_all | solution.py:407
  74.6 0.0 copy-done.3
  74.6 5.1 %split_scores.1 = (f32[2,2,768]{2,1,0:T(2,128)}, f32[64,128]{1,0:T(8,128)}) custom-call(s32[4]{0:T(128)S(1)} %copy-done.5, s32[2]{0:T(128)S(1)} %copy-done.7, bf16[256,896]{1,0:T(8,128)(2,1)S(1)} %bitcast.18, s32[2,128]{1,0:T(2,128)S(1)} %copy-done.6, s32[1,64]{1,0:T(1,128)S(1)} %bitcast.22, s32[1,64]{1,0:T(1,128)S(1)} %bitcast.24, s32[1,64]{1,0:T(1,128)S(1)} %bitcast.27, ...), custom_call_target="tpu_custom_call" | custom-call | tf_op jit(solution)/shard_map/split_scores/pallas_call | solution.py:448
  79.7 12.1 %all-to-all-start.2 = ((f32[64,1,128]{2,1,0:T(1,128)}), f32[64,1,128]{2,1,0:T(1,128)S(1)}, u32[]{:S(2)}, u32[]{:S(2)}) async-start(f32[64,1,128]{2,1,0:T(1,128)} %bitcast.11), calls=%async_computation.2 | async-start | bytes 65536 | tf_op jit(solution)/shard_map/all_to_all | solution.py:479
  91.9 1.1 %moved_rows.1 = bf16[128,768]{1,0:T(8,128)(2,1)} custom-call(bf16[512,640]{1,0:T(8,128)(2,1)S(1)} %bitcast.17), custom_call_target="tpu_custom_call" | custom-call | tf_op jit(solution)/shard_map/moved_rows/pallas_call | solution.py:408
  92.9 2.1 %append_rows.1 = (bf16[4,128,768]{2,1,0:T(8,128)(2,1)}, s32[4]{0:T(128)}) custom-call(s32[4]{0:T(128)S(1)} %copy-done.5, bf16[256,896]{1,0:T(8,128)(2,1)S(1)} %bitcast.19, bf16[4,128,768]{2,1,0:T(8,128)(2,1)S(1)} %get-tuple-element.23.post_ref), custom_call_target="tpu_custom_call" | custom-call | tf_op jit(solution)/shard_map/append_rows/pallas_call | solution.py:465
  95.0 6.1 %all-to-all-done.2 = f32[64,1,128]{2,1,0:T(1,128)S(1)} async-done(((f32[64,1,128]{2,1,0:T(1,128)}), f32[64,1,128]{2,1,0:T(1,128)S(1)}, u32[]{:S(2)}, u32[]{:S(2)}) %all-to-all-start.2) | async-done | bytes 32800 | tf_op jit(solution)/shard_map/all_to_all | solution.py:479
  101.1 0.8 last_step.1
  (9 shorter events, 0.0 us)
Async XLA Ops:
  39.5 20.4 %collective-permute-start = (bf16[2048,768]{1,0:T(8,128)(2,1)}, bf16[2048,768]{1,0:T(8,128)(2,1)}, u32[]{:S(2)}, u32[]{:S(2)}) collective-permute-start(bf16[2048,768]{1,0:T(8,128)(2,1)} %own_ref.5), channel_id=1, source_target_pairs={{0,1},{1,0},{2,3},{3,2},{4,5},{5,4},{6,7},{7,6},{8,9},{9,8},{10,11... | collective-permute-start | bytes 9437192 | tf_op jit(solution)/shard_map/ppermute | solution.py:396
  41.8 18.2 %collective-permute-start.1 = (bf16[256,768]{1,0:T(8,128)(2,1)S(1)}, bf16[256,768]{1,0:T(8,128)(2,1)S(1)}, u32[]{:S(2)}, u32[]{:S(2)}) collective-permute-start(bf16[256,768]{1,0:T(8,128)(2,1)S(1)} %share_rows.1.share_ref.v_ref), channel_id=1, source_target_pairs={{0,16},{16,32},{32,48},{48,0},{1,17},{17,33},{33,49},{49,1},{2,18}... | collective-permute-start | bytes 1179656 | tf_op jit(solution)/shard_map/ppermute | solution.py:397
  44.6 15.3 %collective-permute-start.2 = (bf16[256,768]{1,0:T(8,128)(2,1)S(1)}, bf16[256,768]{1,0:T(8,128)(2,1)S(1)}, u32[]{:S(2)}, u32[]{:S(2)}) collective-permute-start(bf16[256,768]{1,0:T(8,128)(2,1)S(1)} %share_rows.1.share_ref.v_ref), channel_id=1, source_target_pairs={{0,48},{16,0},{32,16},{48,32},{1,49},{17,1},{33,17},{49,33},{2,50}... | collective-permute-start | bytes 1179656 | tf_op jit(solution)/shard_map/ppermute | solution.py:397
  48.3 19.7 %collective-permute-start.3 = (bf16[256,768]{1,0:T(8,128)(2,1)S(1)}, bf16[256,768]{1,0:T(8,128)(2,1)S(1)}, u32[]{:S(2)}, u32[]{:S(2)}) collective-permute-start(bf16[256,768]{1,0:T(8,128)(2,1)S(1)} %share_rows.1.share_ref.v_ref), channel_id=1, source_target_pairs={{0,32},{16,48},{32,0},{48,16},{1,33},{17,49},{33,1},{49,17},{2,34}... | collective-permute-start | bytes 1179656 | tf_op jit(solution)/shard_map/ppermute | solution.py:397
  53.1 21.4 %all-to-all-start.1 = ((bf16[8,32,896]{2,1,0:T(8,128)(2,1)}), bf16[8,32,896]{2,1,0:T(8,128)(2,1)S(1)}, u32[]{:S(2)}, u32[]{:S(2)}) async-start(bf16[8,32,896]{2,1,0:T(8,128)(2,1)} %spread_rows.1), calls=%async_computation.1 | async-start | bytes 917504 | tf_op jit(solution)/shard_map/all_to_all | solution.py:407
  60.0 8.1 %copy-start = (bf16[4,128,768]{2,1,0:T(8,128)(2,1)S(1)}, bf16[4,128,768]{2,1,0:T(8,128)(2,1)}, u32[]{:S(2)}) copy-start(bf16[4,128,768]{2,1,0:T(8,128)(2,1)} %post_in.1) | copy-start | bytes 2359300
  68.1 6.5 %copy-start.2 = (s32[64]{0:T(128)S(1)}, s32[64]{0:T(128)}, u32[]{:S(2)}) copy-start(s32[64]{0:T(128)} %param.18) | copy-start | bytes 772
  68.1 6.5 %copy-start.3 = (s32[64]{0:T(128)S(1)}, s32[64]{0:T(128)}, u32[]{:S(2)}) copy-start(s32[64]{0:T(128)} %param.19) | copy-start | bytes 772
  68.1 6.5 %copy-start.4 = (s32[64]{0:T(128)S(1)}, s32[64]{0:T(128)}, u32[]{:S(2)}) copy-start(s32[64]{0:T(128)} %param.21) | copy-start | bytes 772
  68.1 6.5 %copy-start.5 = (s32[4]{0:T(128)S(1)}, s32[4]{0:T(128)}, u32[]{:S(2)}) copy-start(s32[4]{0:T(128)} %fill_in.3) | copy-start | bytes 52
  68.1 6.5 %copy-start.6 = (s32[2,128]{1,0:T(2,128)S(1)}, s32[2,128]{1,0:T(2,128)}, u32[]{:S(2)}) copy-start(s32[2,128]{1,0:T(2,128)} %member_in.1) | copy-start | bytes 3076
  68.1 6.5 %copy-start.7 = (s32[2]{0:T(128)S(1)}, s32[2]{0:T(128)}, u32[]{:S(2)}) copy-start(s32[2]{0:T(128)} %split_in.1) | copy-start | bytes 28
  68.1 6.5 %copy-start.8 = (s32[64]{0:T(128)S(1)}, s32[64]{0:T(128)}, u32[]{:S(2)}) copy-start(s32[64]{0:T(128)} %param.20) | copy-start | bytes 772
  74.6 26.5 %copy-start.1 = (bf16[512,128]{1,0:T(8,128)(2,1)S(1)}, bf16[512,128]{1,0:T(8,128)(2,1)}, u32[]{:S(2)}) copy-start(bf16[512,128]{1,0:T(8,128)(2,1)} %get-tuple-element.26.table_ref) | copy-start | bytes 393220
  79.7 21.4 %all-to-all-start.2 = ((f32[64,1,128]{2,1,0:T(1,128)}), f32[64,1,128]{2,1,0:T(1,128)S(1)}, u32[]{:S(2)}, u32[]{:S(2)}) async-start(f32[64,1,128]{2,1,0:T(1,128)} %bitcast.11), calls=%async_computation.2 | async-start | bytes 65536 | tf_op jit(solution)/shard_map/all_to_all | solution.py:479

commit v4 on v3

--- a/solution.py
+++ b/solution.py
@@ -182,8 +182,7 @@
     return jnp.where(hit, dot(table, got), before), first + count
 
 
-def append_kernel(fill_in, got_in, post_ref, out_ref, count_ref, got_ref, fill_ref, sems):
-    fetch([(fill_in, fill_ref), (got_in, got_ref)], sems)
+def append_kernel(fill_ref, got_ref, post_ref, out_ref, count_ref):
     match, rank = ranks(got_ref[:, D:], range(POSTS))
     for q in range(POSTS):
         rows, count = appended(
@@ -194,17 +193,9 @@
 
 
 def split_kernel(
-    fill_in, split_in, got_in, member_in, npost_in, nrow_in, nsplit_in, ndest_in, post_ref, own_ref, best_ref,
-    centers_ref, send_ref,
-    fill_ref, split_ref, got_ref, member_ref, npost_ref, nrow_ref, nsplit_ref, ndest_ref, sems,
+    fill_ref, split_ref, got_ref, member_ref, npost_ref, nrow_ref, nsplit_ref, ndest_ref, post_ref, own_ref,
+    best_ref, centers_ref, send_ref,
 ):
-    fetch(
-        [
-            (fill_in, fill_ref), (split_in, split_ref), (got_in, got_ref), (member_in, member_ref),
-            (npost_in, npost_ref), (nrow_in, nrow_ref), (nsplit_in, nsplit_ref), (ndest_in, ndest_ref),
-        ],
-        sems,
-    )
     line = iota((ROWS, 1), 0)
     head = post_ref[:, :HEAD, :].reshape(POSTS * HEAD, D).astype(F32)
     members = member_ref[...].astype(F32)
@@ -264,8 +255,8 @@
     return best
 
 
-def first_kernel(own_ref, mate_in, v_ref, v1_in, v2_in, acc_ref, mate_ref, part_ref, sems):
-    pairs = ((v1_in, part_ref.at[0]), (v2_in, part_ref.at[1]), (mate_in, mate_ref))
+def first_kernel(own_ref, mate_in, v_ref, v1_in, v2_in, acc_ref, near_ref, mate_ref, part_ref, sems):
+    pairs = ((v1_in, part_ref.at[0]), (v2_in, part_ref.at[1]), (mate_in, mate_ref), (own_ref, near_ref))
     copies = [pltpu.make_async_copy(src, dst, sems.at[i]) for i, (src, dst) in enumerate(pairs)]
     for copy in copies:
         copy.start()
@@ -279,14 +270,14 @@
     acc_ref[0] = scan_blocks(mate_ref, v_ref[...], acc_ref[0])
     acc_ref[1] = scan_blocks(mate_ref, part_ref[0], acc_ref[1])
     acc_ref[2] = scan_blocks(mate_ref, part_ref[1], acc_ref[2])
+    copies[3].wait()
 
 
 def best_kernel(
-    place_ref, own_ref, mate_ref, v_in, post_in, acc_ref, out_ref, post_ref, part_ref, sems
+    place_ref, own_ref, mate_ref, v_in, acc_ref, post_ref, out_ref, prior_ref, part_ref, sems
 ):
-    later = pltpu.make_async_copy(post_in, post_ref, sems.at[1])
     fetch([(v_in, part_ref)], sems)
-    later.start()
+    prior_ref[...] = own_ref[:16, :]
     best = scan_blocks(own_ref, part_ref[...], jnp.full((8, NC * 4), LOW, F32))
     accs = [acc_ref[0], acc_ref[1], scan_blocks(mate_ref, part_ref[...], best), acc_ref[2]]
     x, core = place_ref[0], place_ref[1]
@@ -303,7 +294,6 @@
         group = lax.rem(x + NX - a, NX) * NK + core
         best = jnp.where(lane // 4 == group, folded, best)
     out_ref[...] = best
-    later.wait()
 
 
 def final_kernel(in_ref, table_ref, best_ref, score_ref):
@@ -418,49 +408,42 @@
         work = 2 * 4096 * 256 * D * count
         return pl.CostEstimate(flops=work, bytes_accessed=2 * 4096 * D, transcendentals=0)
 
-    first, mate = pl.pallas_call(
+    first, near, mate = pl.pallas_call(
         first_kernel,
         out_shape=(
             jax.ShapeDtypeStruct((NX - 1, 8, NC * 4), F32),
             jax.ShapeDtypeStruct((2048, D), BF),
+            jax.ShapeDtypeStruct((2048, D), BF),
         ),
         in_specs=[vm(), hbm, vm(), hbm, hbm],
-        out_specs=(vm(), vm()),
-        scratch_shapes=[pltpu.VMEM((2, NC * 4, D), BF), pltpu.SemaphoreType.DMA((3,))],
+        out_specs=(vm(), vm(), vm()),
+        scratch_shapes=[pltpu.VMEM((2, NC * 4, D), BF), pltpu.SemaphoreType.DMA((4,))],
         compiler_params=params(),
         cost_estimate=cost(3),
         name="best_of_three",
     )(centroids, mate, share, parts[1], parts[3])
-    best, post_copy = pl.pallas_call(
+    best, priors = pl.pallas_call(
         best_kernel,
-        out_shape=(
-            jax.ShapeDtypeStruct((NC, 128), F32),
-            jax.ShapeDtypeStruct((POSTS, ROWS, D), BF),
-        ),
-        in_specs=[sm(), vm(), vm(), hbm, hbm, vm()],
+        out_shape=(jax.ShapeDtypeStruct((NC, 128), F32), jax.ShapeDtypeStruct((16, D), BF)),
+        in_specs=[sm(), vm(), vm(), hbm, vm(), vm()],
         out_specs=(vm(), vm()),
-        scratch_shapes=[pltpu.VMEM((NC * 4, D), BF), pltpu.SemaphoreType.DMA((2,))],
-        compiler_params=params(),
-        cost_estimate=cost(3),
+        scratch_shapes=[pltpu.VMEM((NC * 4, D), BF), pltpu.SemaphoreType.DMA((1,))],
+        compiler_params=params(),
+        cost_estimate=cost(1),
         name="best_scores",
-    )(place, centroids, mate, parts[2], postings, first)
-    row = pltpu.VMEM((1, NB), I32)
+    )(place, near, mate, parts[2], first, postings)
     split_centers, sending = pl.pallas_call(
         split_kernel,
         out_shape=(
             jax.ShapeDtypeStruct((2, 2, D), F32),
             jax.ShapeDtypeStruct((NC, 128), F32),
         ),
-        in_specs=[hbm] * 8 + [vm()] * 3,
+        in_specs=[sm(), sm()] + [vm()] * 9,
         out_specs=(vm(), vm()),
-        scratch_shapes=[
-            pltpu.SMEM((POSTS,), I32), pltpu.SMEM((2,), I32), pltpu.VMEM((NY * V, W), BF),
-            pltpu.VMEM((2, ROWS), I32), row, row, row, row, pltpu.SemaphoreType.DMA((8,)),
-        ],
         compiler_params=params(),
         name="split_scores",
     )(
-        fill, split_posts, gathered, split_members, npost, nrow, nsplit, ndest, post_copy, centroids, best
+        fill, split_posts, gathered, split_members, npost, nrow, nsplit, ndest, postings, priors, best
     )
     postings_out, new_fill = pl.pallas_call(
         append_kernel,
@@ -468,14 +451,11 @@
             jax.ShapeDtypeStruct((POSTS, ROWS, D), BF),
             jax.ShapeDtypeStruct((POSTS,), I32),
         ),
-        in_specs=[hbm, hbm, vm()],
+        in_specs=[sm(), vm(), vm()],
         out_specs=(vm(), sm()),
-        scratch_shapes=[
-            pltpu.VMEM((NY * V, W), BF), pltpu.SMEM((POSTS,), I32), pltpu.SemaphoreType.DMA((2,)),
-        ],
         compiler_params=params(),
         name="append_rows",
-    )(fill, gathered, post_copy)
+    )(fill, gathered, postings)
     back = lax.all_to_all(sending.reshape(NC, 1, 128), CENT, 0, 0, tiled=True).reshape(NC, 128)
     best_score, moved_scores = pl.pallas_call(
         final_kernel,

time: 102 us -> 93.5 us (0.917)
  Pallas kernels: 26.9 us -> 21.7 us
  starting transfers between devices: 30.9 us -> 26 us
  local copies, waits for them, and re-layouts: 0.05 us -> 1.93 us
    all_to_all x1, starting transfers between devices: 12.1 us -> 7.05 us  [shards(): lax.all_to_all(sending.reshape(NC, 1, 128), CENT, 0, 0, tiled=True)]
    all_to_all x1, waiting for transfers between devices: 2.04 us -> 0.01 us  [shards(): gathered = lax.all_to_all(spread, 'y', 0, 0, tiled=True).reshape(NY * V, W)]
    pallas_call x1, Pallas kernels: 5.08 us -> 3.07 us  [shards(): pl.pallas_call(split_kernel, out_shape=(jax.ShapeDtypeStruct((2, 2, D), F...]
    unnamed x18 -> x20, local copies, waits for them, and re-layouts: 0.05 us -> 1.93 us
    pallas_call x1, Pallas kernels: 8.04 us -> 6.3 us  [shards(): pl.pallas_call(first_kernel, out_shape=(jax.ShapeDtypeStruct((NX - 1, 8,...]
    pallas_call x1, Pallas kernels: 4.38 us -> 2.93 us  [shards(): pl.pallas_call(best_kernel, out_shape=(jax.ShapeDtypeStruct((NC, 128), F3...]
    ppermute x3, waiting for transfers between devices: 0.01 us -> 1.45 us  [shards(): lax.ppermute(share, 'x', [(i, (i + a) % NX) for i in range(NX)])]
  transfers between devices with their start and end apart: 6 -> 6, of which waited for: 2 -> 2; matrix products, arithmetic and copies ran while one was open for 0% -> 0% of each run, Pallas kernels for 17% -> 15%
where the time goes in v4:
time: 93.5 us; the launch traced here: 93 us
  blocking collectives  35 us (37%)
  starting transfers between devices  26 us (28%)
  Pallas kernels  21.7 us (23%)
  waiting for transfers between devices  7.59 us (8%)
  local copies, waits for them, and re-layouts  1.93 us (2%)
    all_to_all x1, blocking collectives, shards(): lax.all_to_all(packed.reshape(NC, 8, P8), CENT, 0, 0, tiled=True)  35 us
    ppermute x3, starting transfers between devices, shards(): lax.ppermute(share, 'x', [(i, (i + a) % NX) for i in range(NX)])  9.87 us
    all_to_all x1, starting transfers between devices, shards(): lax.all_to_all(sending.reshape(NC, 1, 128), CENT, 0, 0, tiled=True)  7.05 us
    all_to_all x1, starting transfers between devices, shards(): gathered = lax.all_to_all(spread, 'y', 0, 0, tiled=True).reshape(NY * V, W)  6.84 us
    pallas_call x1, Pallas kernels, shards(): pl.pallas_call(first_kernel, out_shape=(jax.ShapeDtypeStruct((NX - 1, 8,...  6.3 us
    all_to_all x1, waiting for transfers between devices, shards(): lax.all_to_all(sending.reshape(NC, 1, 128), CENT, 0, 0, tiled=True)  6.14 us
    pallas_call x1, Pallas kernels, shards(): pl.pallas_call(pack_kernel, out_shape=(jax.ShapeDtypeStruct((NC * 8, P8),...  3.52 us
    pallas_call x1, Pallas kernels, shards(): pl.pallas_call(split_kernel, out_shape=(jax.ShapeDtypeStruct((2, 2, D), F...  3.07 us
  transfers between devices with their start and end apart: 6, of which 2 were waited for; matrix products, arithmetic and copies ran while one was open for 0% of the time, Pallas kernels for 15%

profile of v4, /device:TPU:1, one launch (start us, length us, event | category | flops | bytes accessed | tf_op | source)
XLA Modules:
  0.0 93.0 jit_solution(3152563265291966493)
XLA Ops:
  0.6 3.5 %pack_rows.1 = (bf16[512,640]{1,0:T(8,128)(2,1)}, bf16[512,128]{1,0:T(8,128)(2,1)}) custom-call(bf16[32,768]{1,0:T(8,128)(2,1)} %vec_ref.1, bf16[4,128,768]{2,1,0:T(8,128)(2,1)} %post_ref.5, s32[1,32]{1,0:T(1,128)} %bitcast.29, s32[1,64]{1,0:T(1,128)} %bitcast.21, s32[1,64]{1,0:T(1,128)} %bitcast.23, s32[1,64]{1,0:T(1,128)} %bitcast.25), custom_call_target="tpu_custom_call" | custom-call | tf_op jit(solution)/shard_map/pack_rows/pallas_call | solution.py:364
  4.2 35.0 %all_to_all.15 = bf16[64,8,640]{2,1,0:T(8,128)(2,1)S(1)} all-to-all(bf16[64,8,640]{2,1,0:T(8,128)(2,1)} %bitcast.28), channel_id=1, replica_groups=mesh['y'=8,'x'=4,'z'=8,'core'=2] {'x','z','core'}, dimensions={0} | all-to-all | bytes 1310720 | tf_op jit(solution)/shard_map/all_to_all | solution.py:376
  39.1 0.4 share_rows.1.share_ref.v_ref
  39.5 2.2 %collective-permute-start = (bf16[2048,768]{1,0:T(8,128)(2,1)}, bf16[2048,768]{1,0:T(8,128)(2,1)}, u32[]{:S(2)}, u32[]{:S(2)}) collective-permute-start(bf16[2048,768]{1,0:T(8,128)(2,1)} %own_ref.1), channel_id=1, source_target_pairs={{0,1},{1,0},{2,3},{3,2},{4,5},{5,4},{6,7},{7,6},{8,9},{9,8},{10,11... | collective-permute-start | bytes 9437192 | tf_op jit(solution)/shard_map/ppermute | solution.py:386
  41.8 2.9 %collective-permute-start.1 = (bf16[256,768]{1,0:T(8,128)(2,1)S(1)}, bf16[256,768]{1,0:T(8,128)(2,1)S(1)}, u32[]{:S(2)}, u32[]{:S(2)}) collective-permute-start(bf16[256,768]{1,0:T(8,128)(2,1)S(1)} %share_rows.1.share_ref.v_ref), channel_id=1, source_target_pairs={{0,16},{16,32},{32,48},{48,0},{1,17},{17,33},{33,49},{49,1},{2,18}... | collective-permute-start | bytes 1179656 | tf_op jit(solution)/shard_map/ppermute | solution.py:387
  44.6 3.6 %collective-permute-start.2 = (bf16[256,768]{1,0:T(8,128)(2,1)S(1)}, bf16[256,768]{1,0:T(8,128)(2,1)S(1)}, u32[]{:S(2)}, u32[]{:S(2)}) collective-permute-start(bf16[256,768]{1,0:T(8,128)(2,1)S(1)} %share_rows.1.share_ref.v_ref), channel_id=1, source_target_pairs={{0,48},{16,0},{32,16},{48,32},{1,49},{17,1},{33,17},{49,33},{2,50}... | collective-permute-start | bytes 1179656 | tf_op jit(solution)/shard_map/ppermute | solution.py:387
  48.3 1.5 %spread_rows.1 = bf16[8,32,896]{2,1,0:T(8,128)(2,1)} custom-call(bf16[512,640]{1,0:T(8,128)(2,1)S(1)} %bitcast.16, bf16[256,768]{1,0:T(8,128)(2,1)S(1)} %share_rows.1.share_ref.v_ref), custom_call_target="tpu_custom_call" | custom-call | tf_op jit(solution)/shard_map/spread_rows/pallas_call | solution.py:388
  49.8 6.8 %all-to-all-start.1 = ((bf16[8,32,896]{2,1,0:T(8,128)(2,1)}), bf16[8,32,896]{2,1,0:T(8,128)(2,1)S(1)}, u32[]{:S(2)}, u32[]{:S(2)}) async-start(bf16[8,32,896]{2,1,0:T(8,128)(2,1)} %spread_rows.1), calls=%async_computation.1 | async-start | bytes 917504 | tf_op jit(solution)/shard_map/all_to_all | solution.py:397
  56.6 0.1 pad_add_fusion.place_ref
  56.7 3.4 %collective-permute-start.3 = (bf16[256,768]{1,0:T(8,128)(2,1)S(1)}, bf16[256,768]{1,0:T(8,128)(2,1)S(1)}, u32[]{:S(2)}, u32[]{:S(2)}) collective-permute-start(bf16[256,768]{1,0:T(8,128)(2,1)S(1)} %share_rows.1.share_ref.v_ref), channel_id=1, source_target_pairs={{0,32},{16,48},{32,0},{48,16},{1,33},{17,49},{33,1},{49,17},{2,34}... | collective-permute-start | bytes 1179656 | tf_op jit(solution)/shard_map/ppermute | solution.py:387
  60.1 0.0 collective-permute-done.1.v1_in
  60.1 0.0 collective-permute-done.2.v2_in
  60.1 0.0 collective-permute-done.mate_in
  60.1 0.0 copy-start.9
  60.1 1.9 %copy-done.9 = bf16[2048,768]{1,0:T(8,128)(2,1)S(1)} copy-done((bf16[2048,768]{1,0:T(8,128)(2,1)S(1)}, bf16[2048,768]{1,0:T(8,128)(2,1)}, u32[]{:S(2)}) %copy-start.9) | copy-done | bytes 3145752
  62.0 6.3 %best_of_three.1 = (f32[3,8,256]{2,1,0:T(8,128)S(1)}, bf16[2048,768]{1,0:T(8,128)(2,1)S(1)}, bf16[2048,768]{1,0:T(8,128)(2,1)S(1)}) custom-call(bf16[2048,768]{1,0:T(8,128)(2,1)S(1)} %copy-done.9, bf16[2048,768]{1,0:T(8,128)(2,1)} %collective-permute-done.mate_in, bf16[256,768]{1,0:T(8,128)(2,1)S(1)} %share_rows.1.share_ref.v_ref, ...), custom_call_target="tpu_custom_call" | custom-call | flops 4831838208 | bytes 6291456 | tf_op jit(solution)/shard_map/best_of_three/pallas_call | solution.py:411
  68.3 1.4 %collective-permute-done.3.v_in = bf16[256,768]{1,0:T(8,128)(2,1)S(1)} collective-permute-done((bf16[256,768]{1,0:T(8,128)(2,1)S(1)}, bf16[256,768]{1,0:T(8,128)(2,1)S(1)}, u32[]{:S(2)}, u32[]{:S(2)}) %collective-permute-start.3) | collective-permute-done | bytes 393248 | tf_op jit(solution)/shard_map/ppermute | solution.py:387
  69.8 0.0 copy-done
  69.8 0.0 copy-start.5
  69.8 0.0 copy-start.6
  69.8 0.0 copy-start.7
  69.8 0.0 copy-start.8
  69.8 2.9 %best_scores.1 = (f32[64,128]{1,0:T(8,128)S(1)}, bf16[16,768]{1,0:T(8,128)(2,1)S(1)}) custom-call(s32[2]{0:T(128)S(1)} %pad_add_fusion.place_ref, bf16[2048,768]{1,0:T(8,128)(2,1)S(1)} %get-tuple-element.22.own_ref, bf16[2048,768]{1,0:T(8,128)(2,1)S(1)} %get-tuple-element.23.mate_ref, bf16[256,768]{1,0:T(8,128)(2,1)S(1)} %collective-permute-done.3.v_in, ...), custom_call_target="tpu_custom_call" | custom-call | flops 1610612736 | bytes 6291456 | tf_op jit(solution)/shard_map/best_scores/pallas_call | solution.py:425
  72.8 0.0 all-to-all-done.1
  72.8 0.0 copy-done.2
  72.8 0.0 copy-done.3
  72.9 3.1 %split_scores.1 = (f32[2,2,768]{2,1,0:T(2,128)}, f32[64,128]{1,0:T(8,128)}) custom-call(s32[4]{0:T(128)S(1)} %copy-done.5, s32[2]{0:T(128)S(1)} %copy-done.7, bf16[256,896]{1,0:T(8,128)(2,1)S(1)} %bitcast.18, s32[2,128]{1,0:T(2,128)S(1)} %copy-done.6, s32[1,64]{1,0:T(1,128)S(1)} %bitcast.22, s32[1,64]{1,0:T(1,128)S(1)} %bitcast.24, s32[1,64]{1,0:T(1,128)S(1)} %bitcast.27, ...), custom_call_target="tpu_custom_call" | custom-call | tf_op jit(solution)/shard_map/split_scores/pallas_call | solution.py:435
  75.9 7.0 %all-to-all-start.2 = ((f32[64,1,128]{2,1,0:T(1,128)}), f32[64,1,128]{2,1,0:T(1,128)S(1)}, u32[]{:S(2)}, u32[]{:S(2)}) async-start(f32[64,1,128]{2,1,0:T(1,128)} %bitcast.11), calls=%async_computation.2 | async-start | bytes 65536 | tf_op jit(solution)/shard_map/all_to_all | solution.py:459
  83.0 1.1 %moved_rows.1 = bf16[128,768]{1,0:T(8,128)(2,1)} custom-call(bf16[512,640]{1,0:T(8,128)(2,1)S(1)} %bitcast.17), custom_call_target="tpu_custom_call" | custom-call | tf_op jit(solution)/shard_map/moved_rows/pallas_call | solution.py:398
  84.0 2.1 %append_rows.1 = (bf16[4,128,768]{2,1,0:T(8,128)(2,1)}, s32[4]{0:T(128)}) custom-call(s32[4]{0:T(128)S(1)} %copy-done.5, bf16[256,896]{1,0:T(8,128)(2,1)S(1)} %bitcast.19, bf16[4,128,768]{2,1,0:T(8,128)(2,1)S(1)} %copy-done), custom_call_target="tpu_custom_call" | custom-call | tf_op jit(solution)/shard_map/append_rows/pallas_call | solution.py:448
  86.1 6.1 %all-to-all-done.2 = f32[64,1,128]{2,1,0:T(1,128)S(1)} async-done(((f32[64,1,128]{2,1,0:T(1,128)}), f32[64,1,128]{2,1,0:T(1,128)S(1)}, u32[]{:S(2)}, u32[]{:S(2)}) %all-to-all-start.2) | async-done | bytes 32800 | tf_op jit(solution)/shard_map/all_to_all | solution.py:459
  92.3 0.8 last_step.1
  (11 shorter events, 0.0 us)
Async XLA Ops:
  39.5 20.6 %collective-permute-start = (bf16[2048,768]{1,0:T(8,128)(2,1)}, bf16[2048,768]{1,0:T(8,128)(2,1)}, u32[]{:S(2)}, u32[]{:S(2)}) collective-permute-start(bf16[2048,768]{1,0:T(8,128)(2,1)} %own_ref.1), channel_id=1, source_target_pairs={{0,1},{1,0},{2,3},{3,2},{4,5},{5,4},{6,7},{7,6},{8,9},{9,8},{10,11... | collective-permute-start | bytes 9437192 | tf_op jit(solution)/shard_map/ppermute | solution.py:386
  41.8 18.3 %collective-permute-start.1 = (bf16[256,768]{1,0:T(8,128)(2,1)S(1)}, bf16[256,768]{1,0:T(8,128)(2,1)S(1)}, u32[]{:S(2)}, u32[]{:S(2)}) collective-permute-start(bf16[256,768]{1,0:T(8,128)(2,1)S(1)} %share_rows.1.share_ref.v_ref), channel_id=1, source_target_pairs={{0,16},{16,32},{32,48},{48,0},{1,17},{17,33},{33,49},{49,1},{2,18}... | collective-permute-start | bytes 1179656 | tf_op jit(solution)/shard_map/ppermute | solution.py:387
  44.6 15.5 %collective-permute-start.2 = (bf16[256,768]{1,0:T(8,128)(2,1)S(1)}, bf16[256,768]{1,0:T(8,128)(2,1)S(1)}, u32[]{:S(2)}, u32[]{:S(2)}) collective-permute-start(bf16[256,768]{1,0:T(8,128)(2,1)S(1)} %share_rows.1.share_ref.v_ref), channel_id=1, source_target_pairs={{0,48},{16,0},{32,16},{48,32},{1,49},{17,1},{33,17},{49,33},{2,50}... | collective-permute-start | bytes 1179656 | tf_op jit(solution)/shard_map/ppermute | solution.py:387
  49.8 23.0 %all-to-all-start.1 = ((bf16[8,32,896]{2,1,0:T(8,128)(2,1)}), bf16[8,32,896]{2,1,0:T(8,128)(2,1)S(1)}, u32[]{:S(2)}, u32[]{:S(2)}) async-start(bf16[8,32,896]{2,1,0:T(8,128)(2,1)} %spread_rows.1), calls=%async_computation.1 | async-start | bytes 917504 | tf_op jit(solution)/shard_map/all_to_all | solution.py:397
  56.7 13.1 %copy-start = (bf16[4,128,768]{2,1,0:T(8,128)(2,1)S(1)}, bf16[4,128,768]{2,1,0:T(8,128)(2,1)}, u32[]{:S(2)}) copy-start(bf16[4,128,768]{2,1,0:T(8,128)(2,1)} %post_ref.5) | copy-start | bytes 2359300
  56.7 13.1 %collective-permute-start.3 = (bf16[256,768]{1,0:T(8,128)(2,1)S(1)}, bf16[256,768]{1,0:T(8,128)(2,1)S(1)}, u32[]{:S(2)}, u32[]{:S(2)}) collective-permute-start(bf16[256,768]{1,0:T(8,128)(2,1)S(1)} %share_rows.1.share_ref.v_ref), channel_id=1, source_target_pairs={{0,32},{16,48},{32,0},{48,16},{1,33},{17,49},{33,1},{49,17},{2,34}... | collective-permute-start | bytes 1179656 | tf_op jit(solution)/shard_map/ppermute | solution.py:387
  60.1 1.9 %copy-start.9 = (bf16[2048,768]{1,0:T(8,128)(2,1)S(1)}, bf16[2048,768]{1,0:T(8,128)(2,1)}, u32[]{:S(2)}) copy-start(bf16[2048,768]{1,0:T(8,128)(2,1)} %own_ref.1) | copy-start | bytes 9437188
  69.8 3.0 %copy-start.2 = (s32[64]{0:T(128)S(1)}, s32[64]{0:T(128)}, u32[]{:S(2)}) copy-start(s32[64]{0:T(128)} %param.18) | copy-start | bytes 772
  69.8 3.0 %copy-start.3 = (s32[64]{0:T(128)S(1)}, s32[64]{0:T(128)}, u32[]{:S(2)}) copy-start(s32[64]{0:T(128)} %param.19) | copy-start | bytes 772
  69.8 3.0 %copy-start.4 = (s32[64]{0:T(128)S(1)}, s32[64]{0:T(128)}, u32[]{:S(2)}) copy-start(s32[64]{0:T(128)} %param.21) | copy-start | bytes 772
  69.8 3.0 %copy-start.5 = (s32[4]{0:T(128)S(1)}, s32[4]{0:T(128)}, u32[]{:S(2)}) copy-start(s32[4]{0:T(128)} %fill_ref.3) | copy-start | bytes 52
  69.8 3.0 %copy-start.6 = (s32[2,128]{1,0:T(2,128)S(1)}, s32[2,128]{1,0:T(2,128)}, u32[]{:S(2)}) copy-start(s32[2,128]{1,0:T(2,128)} %member_ref.1) | copy-start | bytes 3076
  69.8 3.0 %copy-start.7 = (s32[2]{0:T(128)S(1)}, s32[2]{0:T(128)}, u32[]{:S(2)}) copy-start(s32[2]{0:T(128)} %split_ref.1) | copy-start | bytes 28
  69.8 3.0 %copy-start.8 = (s32[64]{0:T(128)S(1)}, s32[64]{0:T(128)}, u32[]{:S(2)}) copy-start(s32[64]{0:T(128)} %param.20) | copy-start | bytes 772
  72.8 19.5 %copy-start.1 = (bf16[512,128]{1,0:T(8,128)(2,1)S(1)}, bf16[512,128]{1,0:T(8,128)(2,1)}, u32[]{:S(2)}) copy-start(bf16[512,128]{1,0:T(8,128)(2,1)} %get-tuple-element.28.table_ref) | copy-start | bytes 393220
  75.9 16.3 %all-to-all-start.2 = ((f32[64,1,128]{2,1,0:T(1,128)}), f32[64,1,128]{2,1,0:T(1,128)S(1)}, u32[]{:S(2)}, u32[]{:S(2)}) async-start(f32[64,1,128]{2,1,0:T(1,128)} %bitcast.11), calls=%async_computation.2 | async-start | bytes 65536 | tf_op jit(solution)/shard_map/all_to_all | solution.py:459

commit v5 on v4

--- a/solution.py
+++ b/solution.py
@@ -246,6 +246,7 @@
 
 
 BLOCK = 1024
+CUTS = 4
 
 
 def scan_blocks(ref, part, best):
@@ -255,22 +256,30 @@
     return best
 
 
-def first_kernel(own_ref, mate_in, v_ref, v1_in, v2_in, acc_ref, near_ref, mate_ref, part_ref, sems):
-    pairs = ((v1_in, part_ref.at[0]), (v2_in, part_ref.at[1]), (mate_in, mate_ref), (own_ref, near_ref))
+def first_kernel(own_in, mate_in, v_ref, v1_in, v2_in, acc_ref, own_ref, mate_ref, part_ref, sems):
+    rows = 2048 // CUTS
+    pieces = [
+        (src.at[pl.ds(rows * i, rows), :], dst.at[pl.ds(rows * i, rows), :])
+        for src, dst in ((own_in, own_ref), (mate_in, mate_ref))
+        for i in range(CUTS)
+    ]
+    pairs = pieces[:1] + [(v1_in, part_ref.at[0]), (v2_in, part_ref.at[1])] + pieces[1:]
     copies = [pltpu.make_async_copy(src, dst, sems.at[i]) for i, (src, dst) in enumerate(pairs)]
     for copy in copies:
         copy.start()
-    blank = jnp.full((8, NC * 4), LOW, F32)
-    acc_ref[0] = scan_blocks(own_ref, v_ref[...], blank)
-    copies[0].wait()
-    acc_ref[1] = scan_blocks(own_ref, part_ref[0], blank)
-    copies[1].wait()
-    acc_ref[2] = scan_blocks(own_ref, part_ref[1], blank)
-    copies[2].wait()
-    acc_ref[0] = scan_blocks(mate_ref, v_ref[...], acc_ref[0])
-    acc_ref[1] = scan_blocks(mate_ref, part_ref[0], acc_ref[1])
-    acc_ref[2] = scan_blocks(mate_ref, part_ref[1], acc_ref[2])
-    copies[3].wait()
+    for copy in copies[:3]:
+        copy.wait()
+    best = [jnp.full((8, NC * 4), LOW, F32)] * 3
+    for c in range(2 * CUTS):
+        if c > 0:
+            copies[2 + c].wait()
+        ref = own_ref if c < CUTS else mate_ref
+        block = ref[rows * (c % CUTS) : rows * (c % CUTS) + rows, :]
+        for a, part in enumerate((v_ref[...], part_ref[0], part_ref[1])):
+            scores = dot_nt(block, part)
+            best[a] = jnp.maximum(best[a], jnp.max(scores.reshape(rows // 8, 8, NC * 4), axis=0))
+    for a in range(3):
+        acc_ref[a] = best[a]
 
 
 def best_kernel(
@@ -373,6 +382,8 @@
         compiler_params=params(60),
         name="pack_rows",
     )(vectors, postings, assign.reshape(1, V), npost, nrow, ndest)
+    held, packed = lax.optimization_barrier((centroids, packed))
+    mate = lax.ppermute(held, "core", [(0, 1), (1, 0)])
     got = lax.all_to_all(packed.reshape(NC, 8, P8), CENT, 0, 0, tiled=True).reshape(NC * 8, P8)
     share = pl.pallas_call(
         share_kernel,
@@ -380,11 +391,10 @@
         in_specs=[vm()],
         out_specs=vm(),
         compiler_params=params(),
+        cost_estimate=pl.CostEstimate(flops=2 * 10**10, bytes_accessed=0, transcendentals=0),
         name="share_rows",
     )(got)
-    held, _ = lax.optimization_barrier((centroids, share))
-    mate = lax.ppermute(held, "core", [(0, 1), (1, 0)])
-    parts = {a: lax.ppermute(share, "x", [(i, (i + a) % NX) for i in range(NX)]) for a in (2, 1, 3)}
+    parts = {a: lax.ppermute(share, "x", [(i, (i + a) % NX) for i in range(NX)]) for a in (1, 3)}
     spread = pl.pallas_call(
         spread_kernel,
         out_shape=jax.ShapeDtypeStruct((NY, V, W), BF),
@@ -392,8 +402,11 @@
         out_specs=pl.BlockSpec(memory_space=pltpu.HBM),
         scratch_shapes=[pltpu.VMEM((V, W), BF), pltpu.SemaphoreType.DMA((NY,))],
         compiler_params=params(),
+        cost_estimate=pl.CostEstimate(flops=2 * 10**10, bytes_accessed=0, transcendentals=0),
         name="spread_rows",
     )(got, share)
+    later, spread = lax.optimization_barrier((share, spread))
+    parts[2] = lax.ppermute(later, "x", [(i, (i + 2) % NX) for i in range(NX)])
     gathered = lax.all_to_all(spread, "y", 0, 0, tiled=True).reshape(NY * V, W)
     moved_rows = pl.pallas_call(
         moved_kernel,
@@ -405,7 +418,7 @@
     )(got)
 
     def cost(count):
-        work = 2 * 4096 * 256 * D * count
+        work = int(2 * 4096 * 256 * D * count)
         return pl.CostEstimate(flops=work, bytes_accessed=2 * 4096 * D, transcendentals=0)
 
     first, near, mate = pl.pallas_call(
@@ -415,10 +428,10 @@
             jax.ShapeDtypeStruct((2048, D), BF),
             jax.ShapeDtypeStruct((2048, D), BF),
         ),
-        in_specs=[vm(), hbm, vm(), hbm, hbm],
+        in_specs=[hbm, hbm, vm(), hbm, hbm],
         out_specs=(vm(), vm(), vm()),
-        scratch_shapes=[pltpu.VMEM((2, NC * 4, D), BF), pltpu.SemaphoreType.DMA((4,))],
-        compiler_params=params(),
+        scratch_shapes=[pltpu.VMEM((2, NC * 4, D), BF), pltpu.SemaphoreType.DMA((2 + 2 * CUTS,))],
+        compiler_params=params(44),
         cost_estimate=cost(3),
         name="best_of_three",
     )(centroids, mate, share, parts[1], parts[3])
@@ -429,7 +442,7 @@
         out_specs=(vm(), vm()),
         scratch_shapes=[pltpu.VMEM((NC * 4, D), BF), pltpu.SemaphoreType.DMA((1,))],
         compiler_params=params(),
-        cost_estimate=cost(1),
+        cost_estimate=cost(2.6),
         name="best_scores",
     )(place, near, mate, parts[2], first, postings)
     split_centers, sending = pl.pallas_call(

time: 93.5 us -> 98 us (1.048)
  blocking collectives: 35 us -> 0 us
  waiting for transfers between devices: 7.59 us -> 27.8 us
  starting transfers between devices: 26 us -> 43.9 us
  Pallas kernels: 21.7 us -> 24.9 us
  local copies, waits for them, and re-layouts: 1.93 us -> 0.05 us
    all_to_all x1 -> x0, blocking collectives: 35 us -> none  [shards(): lax.all_to_all(packed.reshape(NC, 8, P8), CENT, 0, 0, tiled=True)]
    all_to_all x0 -> x1, waiting for transfers between devices: none -> 17.7 us  [shards(): lax.all_to_all(packed.reshape(NC, 8, P8), CENT, 0, 0, tiled=True)]
    all_to_all x0 -> x1, starting transfers between devices: none -> 14.8 us  [shards(): lax.all_to_all(packed.reshape(NC, 8, P8), CENT, 0, 0, tiled=True)]
    all_to_all x1, waiting for transfers between devices: 0.01 us -> 3.96 us  [shards(): gathered = lax.all_to_all(spread, 'y', 0, 0, tiled=True).reshape(NY * V, W)]
    ppermute x0 -> x1, starting transfers between devices: none -> 3.54 us  [shards(): parts[2] = lax.ppermute(later, 'x', [(i, (i + 2) % NX) for i in range(NX)])]
    ppermute x3 -> x2, starting transfers between devices: 9.87 us -> 6.49 us  [shards(): lax.ppermute(share, 'x', [(i, (i + a) % NX) for i in range(NX)])]
    pallas_call x1, Pallas kernels: 6.3 us -> 9.49 us  [shards(): pl.pallas_call(first_kernel, out_shape=(jax.ShapeDtypeStruct((NX - 1, 8,...]
    all_to_all x1, starting transfers between devices: 7.05 us -> 9.82 us  [shards(): lax.all_to_all(sending.reshape(NC, 1, 128), CENT, 0, 0, tiled=True)]
  transfers between devices with their start and end apart: 6 -> 7, of which waited for: 2 -> 3; matrix products, arithmetic and copies ran while one was open for 0% -> 0% of each run, Pallas kernels for 15% -> 18%
where the time goes in v5:
time: 98 us; the launch traced here: 97.5 us
  starting transfers between devices  43.9 us (45%)
  waiting for transfers between devices  27.8 us (28%)
  Pallas kernels  24.9 us (25%)
    all_to_all x1, waiting for transfers between devices, shards(): lax.all_to_all(packed.reshape(NC, 8, P8), CENT, 0, 0, tiled=True)  17.7 us
    all_to_all x1, starting transfers between devices, shards(): lax.all_to_all(packed.reshape(NC, 8, P8), CENT, 0, 0, tiled=True)  14.8 us
    all_to_all x1, starting transfers between devices, shards(): lax.all_to_all(sending.reshape(NC, 1, 128), CENT, 0, 0, tiled=True)  9.82 us
    pallas_call x1, Pallas kernels, shards(): pl.pallas_call(first_kernel, out_shape=(jax.ShapeDtypeStruct((NX - 1, 8,...  9.49 us
    all_to_all x1, starting transfers between devices, shards(): gathered = lax.all_to_all(spread, 'y', 0, 0, tiled=True).reshape(NY * V, W)  6.84 us
    ppermute x2, starting transfers between devices, shards(): lax.ppermute(share, 'x', [(i, (i + a) % NX) for i in range(NX)])  6.49 us
    all_to_all x1, waiting for transfers between devices, shards(): lax.all_to_all(sending.reshape(NC, 1, 128), CENT, 0, 0, tiled=True)  6.14 us
    all_to_all x1, waiting for transfers between devices, shards(): gathered = lax.all_to_all(spread, 'y', 0, 0, tiled=True).reshape(NY * V, W)  3.96 us
  transfers between devices with their start and end apart: 7, of which 3 were waited for; matrix products, arithmetic and copies ran while one was open for 0% of the time, Pallas kernels for 18%

profile of v5, /device:TPU:1, one launch (start us, length us, event | category | flops | bytes accessed | tf_op | source)
XLA Modules:
  0.0 97.5 jit_solution(11918440660454226145)
XLA Ops:
  0.6 3.5 %pack_rows.1 = (bf16[512,640]{1,0:T(8,128)(2,1)}, bf16[512,128]{1,0:T(8,128)(2,1)}) custom-call(bf16[32,768]{1,0:T(8,128)(2,1)} %vec_ref.1, bf16[4,128,768]{2,1,0:T(8,128)(2,1)} %post_ref.5, s32[1,32]{1,0:T(1,128)} %bitcast.29, s32[1,64]{1,0:T(1,128)} %bitcast.21, s32[1,64]{1,0:T(1,128)} %bitcast.23, s32[1,64]{1,0:T(1,128)} %bitcast.25), custom_call_target="tpu_custom_call" | custom-call | tf_op jit(solution)/shard_map/pack_rows/pallas_call | solution.py:373
  4.2 14.8 %all-to-all-start = ((bf16[64,8,640]{2,1,0:T(8,128)(2,1)}), bf16[64,8,640]{2,1,0:T(8,128)(2,1)S(1)}, u32[]{:S(2)}, u32[]{:S(2)}) async-start(bf16[64,8,640]{2,1,0:T(8,128)(2,1)} %bitcast.28), calls=%async_computation | async-start | bytes 1310720 | tf_op jit(solution)/shard_map/all_to_all | solution.py:387
  19.0 2.4 %collective-permute-start = (bf16[2048,768]{1,0:T(8,128)(2,1)}, bf16[2048,768]{1,0:T(8,128)(2,1)}, u32[]{:S(2)}, u32[]{:S(2)}) collective-permute-start(bf16[2048,768]{1,0:T(8,128)(2,1)} %own_in.1), channel_id=1, source_target_pairs={{0,1},{1,0},{2,3},{3,2},{4,5},{5,4},{6,7},{7,6},{8,9},{9,8},{10,11... | collective-permute-start | bytes 9437192 | tf_op jit(solution)/shard_map/ppermute | solution.py:386
  21.4 0.1 pad_add_fusion.place_ref
  21.5 17.7 %all-to-all-done = bf16[64,8,640]{2,1,0:T(8,128)(2,1)S(1)} async-done(((bf16[64,8,640]{2,1,0:T(8,128)(2,1)}), bf16[64,8,640]{2,1,0:T(8,128)(2,1)S(1)}, u32[]{:S(2)}, u32[]{:S(2)}) %all-to-all-start) | async-done | bytes 655392 | tf_op jit(solution)/shard_map/all_to_all | solution.py:387
  39.1 0.4 share_rows.1.share_ref.v_ref
  39.6 3.1 %collective-permute-start.1 = (bf16[256,768]{1,0:T(8,128)(2,1)S(1)}, bf16[256,768]{1,0:T(8,128)(2,1)S(1)}, u32[]{:S(2)}, u32[]{:S(2)}) collective-permute-start(bf16[256,768]{1,0:T(8,128)(2,1)S(1)} %share_rows.1.share_ref.v_ref), channel_id=1, source_target_pairs={{0,16},{16,32},{32,48},{48,0},{1,17},{17,33},{33,49},{49,1},{2,18}... | collective-permute-start | bytes 1179656 | tf_op jit(solution)/shard_map/ppermute | solution.py:397
  42.7 3.4 %collective-permute-start.2 = (bf16[256,768]{1,0:T(8,128)(2,1)S(1)}, bf16[256,768]{1,0:T(8,128)(2,1)S(1)}, u32[]{:S(2)}, u32[]{:S(2)}) collective-permute-start(bf16[256,768]{1,0:T(8,128)(2,1)S(1)} %share_rows.1.share_ref.v_ref), channel_id=1, source_target_pairs={{0,48},{16,0},{32,16},{48,32},{1,49},{17,1},{33,17},{49,33},{2,50}... | collective-permute-start | bytes 1179656 | tf_op jit(solution)/shard_map/ppermute | solution.py:397
  46.1 1.5 %spread_rows.1 = bf16[8,32,896]{2,1,0:T(8,128)(2,1)} custom-call(bf16[512,640]{1,0:T(8,128)(2,1)S(1)} %bitcast.18, bf16[256,768]{1,0:T(8,128)(2,1)S(1)} %share_rows.1.share_ref.v_ref), custom_call_target="tpu_custom_call" | custom-call | flops 20000000000 | tf_op jit(solution)/shard_map/spread_rows/pallas_call | solution.py:398
  47.6 3.5 %collective-permute-start.3 = (bf16[256,768]{1,0:T(8,128)(2,1)S(1)}, bf16[256,768]{1,0:T(8,128)(2,1)S(1)}, u32[]{:S(2)}, u32[]{:S(2)}) collective-permute-start(bf16[256,768]{1,0:T(8,128)(2,1)S(1)} %share_rows.1.share_ref.v_ref), channel_id=1, source_target_pairs={{0,32},{16,48},{32,0},{48,16},{1,33},{17,49},{33,1},{49,17},{2,34}... | collective-permute-start | bytes 1179656 | tf_op jit(solution)/shard_map/ppermute | solution.py:409
  51.1 6.8 %all-to-all-start.1 = ((bf16[8,32,896]{2,1,0:T(8,128)(2,1)}), bf16[8,32,896]{2,1,0:T(8,128)(2,1)S(1)}, u32[]{:S(2)}, u32[]{:S(2)}) async-start(bf16[8,32,896]{2,1,0:T(8,128)(2,1)} %spread_rows.1), calls=%async_computation.1 | async-start | bytes 917504 | tf_op jit(solution)/shard_map/all_to_all | solution.py:410
  58.0 0.0 collective-permute-done.1.v1_in
  58.0 0.0 collective-permute-done.2.v2_in
  58.0 0.0 collective-permute-done.mate_in
  58.0 9.5 %best_of_three.1 = (f32[3,8,256]{2,1,0:T(8,128)S(1)}, bf16[2048,768]{1,0:T(8,128)(2,1)S(1)}, bf16[2048,768]{1,0:T(8,128)(2,1)S(1)}) custom-call(bf16[2048,768]{1,0:T(8,128)(2,1)} %own_in.1, bf16[2048,768]{1,0:T(8,128)(2,1)} %collective-permute-done.mate_in, bf16[256,768]{1,0:T(8,128)(2,1)S(1)} %share_rows.1.share_ref.v_ref, ...), custom_call_target="tpu_custom_call" | custom-call | flops 4831838208 | bytes 6291456 | tf_op jit(solution)/shard_map/best_of_three/pallas_call | solution.py:424
  67.5 0.0 collective-permute-done.3.v_in
  67.5 0.0 copy-start.2
  67.5 0.0 copy-start.3
  67.5 0.0 copy-start.4
  67.6 0.0 copy-start.5
  67.6 0.0 copy-start.6
  67.6 0.0 copy-start.7
  67.6 0.0 copy-start.8
  67.6 2.9 %best_scores.1 = (f32[64,128]{1,0:T(8,128)S(1)}, bf16[16,768]{1,0:T(8,128)(2,1)S(1)}) custom-call(s32[2]{0:T(128)S(1)} %pad_add_fusion.place_ref, bf16[2048,768]{1,0:T(8,128)(2,1)S(1)} %get-tuple-element.27.own_ref, bf16[2048,768]{1,0:T(8,128)(2,1)S(1)} %get-tuple-element.28.mate_ref, bf16[256,768]{1,0:T(8,128)(2,1)S(1)} %collective-permute-done.3.v_in, ...), custom_call_target="tpu_custom_call" | custom-call | flops 4187593216 | bytes 6291456 | tf_op jit(solution)/shard_map/best_scores/pallas_call | solution.py:438
  70.6 4.0 %all-to-all-done.1 = bf16[8,32,896]{2,1,0:T(8,128)(2,1)S(1)} async-done(((bf16[8,32,896]{2,1,0:T(8,128)(2,1)}), bf16[8,32,896]{2,1,0:T(8,128)(2,1)S(1)}, u32[]{:S(2)}, u32[]{:S(2)}) %all-to-all-start.1) | async-done | bytes 458784 | tf_op jit(solution)/shard_map/all_to_all | solution.py:410
  74.5 0.0 copy-done.5
  74.6 3.1 %split_scores.1 = (f32[2,2,768]{2,1,0:T(2,128)}, f32[64,128]{1,0:T(8,128)}) custom-call(s32[4]{0:T(128)S(1)} %copy-done.5, s32[2]{0:T(128)S(1)} %copy-done.7, bf16[256,896]{1,0:T(8,128)(2,1)S(1)} %bitcast.15, s32[2,128]{1,0:T(2,128)S(1)} %copy-done.6, s32[1,64]{1,0:T(1,128)S(1)} %bitcast.22, s32[1,64]{1,0:T(1,128)S(1)} %bitcast.24, s32[1,64]{1,0:T(1,128)S(1)} %bitcast.27, ...), custom_call_target="tpu_custom_call" | custom-call | tf_op jit(solution)/shard_map/split_scores/pallas_call | solution.py:448
  77.7 9.8 %all-to-all-start.2 = ((f32[64,1,128]{2,1,0:T(1,128)}), f32[64,1,128]{2,1,0:T(1,128)S(1)}, u32[]{:S(2)}, u32[]{:S(2)}) async-start(f32[64,1,128]{2,1,0:T(1,128)} %bitcast.11), calls=%async_computation.2 | async-start | bytes 65536 | tf_op jit(solution)/shard_map/all_to_all | solution.py:472
  87.5 1.1 %moved_rows.1 = bf16[128,768]{1,0:T(8,128)(2,1)} custom-call(bf16[512,640]{1,0:T(8,128)(2,1)S(1)} %bitcast.19), custom_call_target="tpu_custom_call" | custom-call | tf_op jit(solution)/shard_map/moved_rows/pallas_call | solution.py:411
  88.6 2.1 %append_rows.1 = (bf16[4,128,768]{2,1,0:T(8,128)(2,1)}, s32[4]{0:T(128)}) custom-call(s32[4]{0:T(128)S(1)} %copy-done.5, bf16[256,896]{1,0:T(8,128)(2,1)S(1)} %bitcast.16, bf16[4,128,768]{2,1,0:T(8,128)(2,1)S(1)} %copy-done), custom_call_target="tpu_custom_call" | custom-call | tf_op jit(solution)/shard_map/append_rows/pallas_call | solution.py:461
  90.6 6.1 %all-to-all-done.2 = f32[64,1,128]{2,1,0:T(1,128)S(1)} async-done(((f32[64,1,128]{2,1,0:T(1,128)}), f32[64,1,128]{2,1,0:T(1,128)S(1)}, u32[]{:S(2)}, u32[]{:S(2)}) %all-to-all-start.2) | async-done | bytes 32800 | tf_op jit(solution)/shard_map/all_to_all | solution.py:472
  96.8 0.8 last_step.1
  (10 shorter events, 0.0 us)
Async XLA Ops:
  4.2 35.0 %all-to-all-start = ((bf16[64,8,640]{2,1,0:T(8,128)(2,1)}), bf16[64,8,640]{2,1,0:T(8,128)(2,1)S(1)}, u32[]{:S(2)}, u32[]{:S(2)}) async-start(bf16[64,8,640]{2,1,0:T(8,128)(2,1)} %bitcast.28), calls=%async_computation | async-start | bytes 1310720 | tf_op jit(solution)/shard_map/all_to_all | solution.py:387
  19.0 39.0 %collective-permute-start = (bf16[2048,768]{1,0:T(8,128)(2,1)}, bf16[2048,768]{1,0:T(8,128)(2,1)}, u32[]{:S(2)}, u32[]{:S(2)}) collective-permute-start(bf16[2048,768]{1,0:T(8,128)(2,1)} %own_in.1), channel_id=1, source_target_pairs={{0,1},{1,0},{2,3},{3,2},{4,5},{5,4},{6,7},{7,6},{8,9},{9,8},{10,11... | collective-permute-start | bytes 9437192 | tf_op jit(solution)/shard_map/ppermute | solution.py:386
  39.6 18.4 %collective-permute-start.1 = (bf16[256,768]{1,0:T(8,128)(2,1)S(1)}, bf16[256,768]{1,0:T(8,128)(2,1)S(1)}, u32[]{:S(2)}, u32[]{:S(2)}) collective-permute-start(bf16[256,768]{1,0:T(8,128)(2,1)S(1)} %share_rows.1.share_ref.v_ref), channel_id=1, source_target_pairs={{0,16},{16,32},{32,48},{48,0},{1,17},{17,33},{33,49},{49,1},{2,18}... | collective-permute-start | bytes 1179656 | tf_op jit(solution)/shard_map/ppermute | solution.py:397
  42.7 15.3 %collective-permute-start.2 = (bf16[256,768]{1,0:T(8,128)(2,1)S(1)}, bf16[256,768]{1,0:T(8,128)(2,1)S(1)}, u32[]{:S(2)}, u32[]{:S(2)}) collective-permute-start(bf16[256,768]{1,0:T(8,128)(2,1)S(1)} %share_rows.1.share_ref.v_ref), channel_id=1, source_target_pairs={{0,48},{16,0},{32,16},{48,32},{1,49},{17,1},{33,17},{49,33},{2,50}... | collective-permute-start | bytes 1179656 | tf_op jit(solution)/shard_map/ppermute | solution.py:397
  47.6 19.9 %collective-permute-start.3 = (bf16[256,768]{1,0:T(8,128)(2,1)S(1)}, bf16[256,768]{1,0:T(8,128)(2,1)S(1)}, u32[]{:S(2)}, u32[]{:S(2)}) collective-permute-start(bf16[256,768]{1,0:T(8,128)(2,1)S(1)} %share_rows.1.share_ref.v_ref), channel_id=1, source_target_pairs={{0,32},{16,48},{32,0},{48,16},{1,33},{17,49},{33,1},{49,17},{2,34}... | collective-permute-start | bytes 1179656 | tf_op jit(solution)/shard_map/ppermute | solution.py:409
  51.1 23.4 %all-to-all-start.1 = ((bf16[8,32,896]{2,1,0:T(8,128)(2,1)}), bf16[8,32,896]{2,1,0:T(8,128)(2,1)S(1)}, u32[]{:S(2)}, u32[]{:S(2)}) async-start(bf16[8,32,896]{2,1,0:T(8,128)(2,1)} %spread_rows.1), calls=%async_computation.1 | async-start | bytes 917504 | tf_op jit(solution)/shard_map/all_to_all | solution.py:410
  58.0 9.5 %copy-start = (bf16[4,128,768]{2,1,0:T(8,128)(2,1)S(1)}, bf16[4,128,768]{2,1,0:T(8,128)(2,1)}, u32[]{:S(2)}) copy-start(bf16[4,128,768]{2,1,0:T(8,128)(2,1)} %post_ref.5) | copy-start | bytes 2359300
  67.5 7.0 %copy-start.2 = (s32[64]{0:T(128)S(1)}, s32[64]{0:T(128)}, u32[]{:S(2)}) copy-start(s32[64]{0:T(128)} %param.18) | copy-start | bytes 772
  67.5 7.0 %copy-start.3 = (s32[64]{0:T(128)S(1)}, s32[64]{0:T(128)}, u32[]{:S(2)}) copy-start(s32[64]{0:T(128)} %param.19) | copy-start | bytes 772
  67.5 7.0 %copy-start.4 = (s32[64]{0:T(128)S(1)}, s32[64]{0:T(128)}, u32[]{:S(2)}) copy-start(s32[64]{0:T(128)} %param.21) | copy-start | bytes 772
  67.6 7.0 %copy-start.5 = (s32[4]{0:T(128)S(1)}, s32[4]{0:T(128)}, u32[]{:S(2)}) copy-start(s32[4]{0:T(128)} %fill_ref.3) | copy-start | bytes 52
  67.6 7.0 %copy-start.6 = (s32[2,128]{1,0:T(2,128)S(1)}, s32[2,128]{1,0:T(2,128)}, u32[]{:S(2)}) copy-start(s32[2,128]{1,0:T(2,128)} %member_ref.1) | copy-start | bytes 3076
  67.6 7.0 %copy-start.7 = (s32[2]{0:T(128)S(1)}, s32[2]{0:T(128)}, u32[]{:S(2)}) copy-start(s32[2]{0:T(128)} %split_ref.1) | copy-start | bytes 28
  67.6 7.0 %copy-start.8 = (s32[64]{0:T(128)S(1)}, s32[64]{0:T(128)}, u32[]{:S(2)}) copy-start(s32[64]{0:T(128)} %param.20) | copy-start | bytes 772
  70.5 26.2 %copy-start.1 = (bf16[512,128]{1,0:T(8,128)(2,1)S(1)}, bf16[512,128]{1,0:T(8,128)(2,1)}, u32[]{:S(2)}) copy-start(bf16[512,128]{1,0:T(8,128)(2,1)} %get-tuple-element.34.table_ref) | copy-start | bytes 393220
  77.7 19.1 %all-to-all-start.2 = ((f32[64,1,128]{2,1,0:T(1,128)}), f32[64,1,128]{2,1,0:T(1,128)S(1)}, u32[]{:S(2)}, u32[]{:S(2)}) async-start(f32[64,1,128]{2,1,0:T(1,128)} %bitcast.11), calls=%async_computation.2 | async-start | bytes 65536 | tf_op jit(solution)/shard_map/all_to_all | solution.py:472

commit v6 on v4

--- a/solution.py
+++ b/solution.py
@@ -373,6 +373,8 @@
         compiler_params=params(60),
         name="pack_rows",
     )(vectors, postings, assign.reshape(1, V), npost, nrow, ndest)
+    held, packed = lax.optimization_barrier((centroids, packed))
+    mate = lax.ppermute(held, "core", [(0, 1), (1, 0)])
     got = lax.all_to_all(packed.reshape(NC, 8, P8), CENT, 0, 0, tiled=True).reshape(NC * 8, P8)
     share = pl.pallas_call(
         share_kernel,
@@ -380,10 +382,9 @@
         in_specs=[vm()],
         out_specs=vm(),
         compiler_params=params(),
+        cost_estimate=pl.CostEstimate(flops=2 * 10**10, bytes_accessed=0, transcendentals=0),
         name="share_rows",
     )(got)
-    held, _ = lax.optimization_barrier((centroids, share))
-    mate = lax.ppermute(held, "core", [(0, 1), (1, 0)])
     parts = {a: lax.ppermute(share, "x", [(i, (i + a) % NX) for i in range(NX)]) for a in (2, 1, 3)}
     spread = pl.pallas_call(
         spread_kernel,
@@ -392,6 +393,7 @@
         out_specs=pl.BlockSpec(memory_space=pltpu.HBM),
         scratch_shapes=[pltpu.VMEM((V, W), BF), pltpu.SemaphoreType.DMA((NY,))],
         compiler_params=params(),
+        cost_estimate=pl.CostEstimate(flops=2 * 10**10, bytes_accessed=0, transcendentals=0),
         name="spread_rows",
     )(got, share)
     gathered = lax.all_to_all(spread, "y", 0, 0, tiled=True).reshape(NY * V, W)

time: 93.5 us -> 91.1 us (0.974)
  blocking collectives: 35 us -> 0 us
  waiting for transfers between devices: 7.59 us -> 25 us
  starting transfers between devices: 26 us -> 41.1 us
    all_to_all x1 -> x0, blocking collectives: 35 us -> none  [shards(): lax.all_to_all(packed.reshape(NC, 8, P8), CENT, 0, 0, tiled=True)]
    all_to_all x0 -> x1, waiting for transfers between devices: none -> 17.8 us  [shards(): lax.all_to_all(packed.reshape(NC, 8, P8), CENT, 0, 0, tiled=True)]
    all_to_all x0 -> x1, starting transfers between devices: none -> 14.8 us  [shards(): lax.all_to_all(packed.reshape(NC, 8, P8), CENT, 0, 0, tiled=True)]
  transfers between devices with their start and end apart: 6 -> 7, of which waited for: 2 -> 3; matrix products, arithmetic and copies ran while one was open for 0% -> 0% of each run, Pallas kernels for 15% -> 16%
where the time goes in v6:
time: 91.1 us; the launch traced here: 90.7 us
  starting transfers between devices  41.1 us (45%)
  waiting for transfers between devices  25 us (27%)
  Pallas kernels  21.7 us (24%)
  local copies, waits for them, and re-layouts  1.93 us (2%)
    all_to_all x1, waiting for transfers between devices, shards(): lax.all_to_all(packed.reshape(NC, 8, P8), CENT, 0, 0, tiled=True)  17.8 us
    all_to_all x1, starting transfers between devices, shards(): lax.all_to_all(packed.reshape(NC, 8, P8), CENT, 0, 0, tiled=True)  14.8 us
    ppermute x3, starting transfers between devices, shards(): lax.ppermute(share, 'x', [(i, (i + a) % NX) for i in range(NX)])  10.1 us
    all_to_all x1, starting transfers between devices, shards(): lax.all_to_all(sending.reshape(NC, 1, 128), CENT, 0, 0, tiled=True)  6.94 us
    all_to_all x1, starting transfers between devices, shards(): gathered = lax.all_to_all(spread, 'y', 0, 0, tiled=True).reshape(NY * V, W)  6.84 us
    pallas_call x1, Pallas kernels, shards(): pl.pallas_call(first_kernel, out_shape=(jax.ShapeDtypeStruct((NX - 1, 8,...  6.3 us
    all_to_all x1, waiting for transfers between devices, shards(): lax.all_to_all(sending.reshape(NC, 1, 128), CENT, 0, 0, tiled=True)  6.14 us
    pallas_call x1, Pallas kernels, shards(): pl.pallas_call(pack_kernel, out_shape=(jax.ShapeDtypeStruct((NC * 8, P8),...  3.52 us
  transfers between devices with their start and end apart: 7, of which 3 were waited for; matrix products, arithmetic and copies ran while one was open for 0% of the time, Pallas kernels for 16%

profile of v6, /device:TPU:1, one launch (start us, length us, event | category | flops | bytes accessed | tf_op | source)
XLA Modules:
  0.0 90.7 jit_solution(14271193426665569806)
XLA Ops:
  0.6 3.5 %pack_rows.1 = (bf16[512,640]{1,0:T(8,128)(2,1)}, bf16[512,128]{1,0:T(8,128)(2,1)}) custom-call(bf16[32,768]{1,0:T(8,128)(2,1)} %vec_ref.1, bf16[4,128,768]{2,1,0:T(8,128)(2,1)} %post_ref.5, s32[1,32]{1,0:T(1,128)} %bitcast.29, s32[1,64]{1,0:T(1,128)} %bitcast.21, s32[1,64]{1,0:T(1,128)} %bitcast.23, s32[1,64]{1,0:T(1,128)} %bitcast.25), custom_call_target="tpu_custom_call" | custom-call | tf_op jit(solution)/shard_map/pack_rows/pallas_call | solution.py:364
  4.2 14.8 %all-to-all-start = ((bf16[64,8,640]{2,1,0:T(8,128)(2,1)}), bf16[64,8,640]{2,1,0:T(8,128)(2,1)S(1)}, u32[]{:S(2)}, u32[]{:S(2)}) async-start(bf16[64,8,640]{2,1,0:T(8,128)(2,1)} %bitcast.28), calls=%async_computation | async-start | bytes 1310720 | tf_op jit(solution)/shard_map/all_to_all | solution.py:378
  19.0 2.4 %collective-permute-start = (bf16[2048,768]{1,0:T(8,128)(2,1)}, bf16[2048,768]{1,0:T(8,128)(2,1)}, u32[]{:S(2)}, u32[]{:S(2)}) collective-permute-start(bf16[2048,768]{1,0:T(8,128)(2,1)} %own_ref.1), channel_id=1, source_target_pairs={{0,1},{1,0},{2,3},{3,2},{4,5},{5,4},{6,7},{7,6},{8,9},{9,8},{10,11... | collective-permute-start | bytes 9437192 | tf_op jit(solution)/shard_map/ppermute | solution.py:377
  21.4 17.8 %all-to-all-done = bf16[64,8,640]{2,1,0:T(8,128)(2,1)S(1)} async-done(((bf16[64,8,640]{2,1,0:T(8,128)(2,1)}), bf16[64,8,640]{2,1,0:T(8,128)(2,1)S(1)}, u32[]{:S(2)}, u32[]{:S(2)}) %all-to-all-start) | async-done | bytes 655392 | tf_op jit(solution)/shard_map/all_to_all | solution.py:378
  39.1 0.4 share_rows.1.share_ref.v_ref
  39.6 3.1 %collective-permute-start.1 = (bf16[256,768]{1,0:T(8,128)(2,1)S(1)}, bf16[256,768]{1,0:T(8,128)(2,1)S(1)}, u32[]{:S(2)}, u32[]{:S(2)}) collective-permute-start(bf16[256,768]{1,0:T(8,128)(2,1)S(1)} %share_rows.1.share_ref.v_ref), channel_id=1, source_target_pairs={{0,16},{16,32},{32,48},{48,0},{1,17},{17,33},{33,49},{49,1},{2,18}... | collective-permute-start | bytes 1179656 | tf_op jit(solution)/shard_map/ppermute | solution.py:388
  42.7 3.4 %collective-permute-start.2 = (bf16[256,768]{1,0:T(8,128)(2,1)S(1)}, bf16[256,768]{1,0:T(8,128)(2,1)S(1)}, u32[]{:S(2)}, u32[]{:S(2)}) collective-permute-start(bf16[256,768]{1,0:T(8,128)(2,1)S(1)} %share_rows.1.share_ref.v_ref), channel_id=1, source_target_pairs={{0,48},{16,0},{32,16},{48,32},{1,49},{17,1},{33,17},{49,33},{2,50}... | collective-permute-start | bytes 1179656 | tf_op jit(solution)/shard_map/ppermute | solution.py:388
  46.1 1.5 %spread_rows.1 = bf16[8,32,896]{2,1,0:T(8,128)(2,1)} custom-call(bf16[512,640]{1,0:T(8,128)(2,1)S(1)} %bitcast.18, bf16[256,768]{1,0:T(8,128)(2,1)S(1)} %share_rows.1.share_ref.v_ref), custom_call_target="tpu_custom_call" | custom-call | flops 20000000000 | tf_op jit(solution)/shard_map/spread_rows/pallas_call | solution.py:389
  47.6 6.8 %all-to-all-start.1 = ((bf16[8,32,896]{2,1,0:T(8,128)(2,1)}), bf16[8,32,896]{2,1,0:T(8,128)(2,1)S(1)}, u32[]{:S(2)}, u32[]{:S(2)}) async-start(bf16[8,32,896]{2,1,0:T(8,128)(2,1)} %spread_rows.1), calls=%async_computation.1 | async-start | bytes 917504 | tf_op jit(solution)/shard_map/all_to_all | solution.py:399
  54.4 0.1 pad_add_fusion.place_ref
  54.5 3.7 %collective-permute-start.3 = (bf16[256,768]{1,0:T(8,128)(2,1)S(1)}, bf16[256,768]{1,0:T(8,128)(2,1)S(1)}, u32[]{:S(2)}, u32[]{:S(2)}) collective-permute-start(bf16[256,768]{1,0:T(8,128)(2,1)S(1)} %share_rows.1.share_ref.v_ref), channel_id=1, source_target_pairs={{0,32},{16,48},{32,0},{48,16},{1,33},{17,49},{33,1},{49,17},{2,34}... | collective-permute-start | bytes 1179656 | tf_op jit(solution)/shard_map/ppermute | solution.py:388
  58.2 0.0 collective-permute-done.1.v1_in
  58.2 0.0 collective-permute-done.2.v2_in
  58.2 0.0 collective-permute-done.mate_in
  58.2 0.0 copy-start.9
  58.2 1.9 %copy-done.9 = bf16[2048,768]{1,0:T(8,128)(2,1)S(1)} copy-done((bf16[2048,768]{1,0:T(8,128)(2,1)S(1)}, bf16[2048,768]{1,0:T(8,128)(2,1)}, u32[]{:S(2)}) %copy-start.9) | copy-done | bytes 3145752
  60.1 6.3 %best_of_three.1 = (f32[3,8,256]{2,1,0:T(8,128)S(1)}, bf16[2048,768]{1,0:T(8,128)(2,1)S(1)}, bf16[2048,768]{1,0:T(8,128)(2,1)S(1)}) custom-call(bf16[2048,768]{1,0:T(8,128)(2,1)S(1)} %copy-done.9, bf16[2048,768]{1,0:T(8,128)(2,1)} %collective-permute-done.mate_in, bf16[256,768]{1,0:T(8,128)(2,1)S(1)} %share_rows.1.share_ref.v_ref, ...), custom_call_target="tpu_custom_call" | custom-call | flops 4831838208 | bytes 6291456 | tf_op jit(solution)/shard_map/best_of_three/pallas_call | solution.py:413
  66.4 1.1 %collective-permute-done.3.v_in = bf16[256,768]{1,0:T(8,128)(2,1)S(1)} collective-permute-done((bf16[256,768]{1,0:T(8,128)(2,1)S(1)}, bf16[256,768]{1,0:T(8,128)(2,1)S(1)}, u32[]{:S(2)}, u32[]{:S(2)}) %collective-permute-start.3) | collective-permute-done | bytes 393248 | tf_op jit(solution)/shard_map/ppermute | solution.py:388
  67.5 0.0 copy-start.5
  67.5 0.0 copy-start.6
  67.5 0.0 copy-start.7
  67.5 0.0 copy-start.8
  67.6 2.9 %best_scores.1 = (f32[64,128]{1,0:T(8,128)S(1)}, bf16[16,768]{1,0:T(8,128)(2,1)S(1)}) custom-call(s32[2]{0:T(128)S(1)} %pad_add_fusion.place_ref, bf16[2048,768]{1,0:T(8,128)(2,1)S(1)} %get-tuple-element.24.own_ref, bf16[2048,768]{1,0:T(8,128)(2,1)S(1)} %get-tuple-element.25.mate_ref, bf16[256,768]{1,0:T(8,128)(2,1)S(1)} %collective-permute-done.3.v_in, ...), custom_call_target="tpu_custom_call" | custom-call | flops 1610612736 | bytes 6291456 | tf_op jit(solution)/shard_map/best_scores/pallas_call | solution.py:427
  70.5 0.0 all-to-all-done.1
  70.5 0.0 copy-done.2
  70.5 0.0 copy-done.3
  70.6 3.1 %split_scores.1 = (f32[2,2,768]{2,1,0:T(2,128)}, f32[64,128]{1,0:T(8,128)}) custom-call(s32[4]{0:T(128)S(1)} %copy-done.5, s32[2]{0:T(128)S(1)} %copy-done.7, bf16[256,896]{1,0:T(8,128)(2,1)S(1)} %bitcast.15, s32[2,128]{1,0:T(2,128)S(1)} %copy-done.6, s32[1,64]{1,0:T(1,128)S(1)} %bitcast.22, s32[1,64]{1,0:T(1,128)S(1)} %bitcast.24, s32[1,64]{1,0:T(1,128)S(1)} %bitcast.27, ...), custom_call_target="tpu_custom_call" | custom-call | tf_op jit(solution)/shard_map/split_scores/pallas_call | solution.py:437
  73.7 6.9 %all-to-all-start.2 = ((f32[64,1,128]{2,1,0:T(1,128)}), f32[64,1,128]{2,1,0:T(1,128)S(1)}, u32[]{:S(2)}, u32[]{:S(2)}) async-start(f32[64,1,128]{2,1,0:T(1,128)} %bitcast.11), calls=%async_computation.2 | async-start | bytes 65536 | tf_op jit(solution)/shard_map/all_to_all | solution.py:461
  80.6 1.1 %moved_rows.1 = bf16[128,768]{1,0:T(8,128)(2,1)} custom-call(bf16[512,640]{1,0:T(8,128)(2,1)S(1)} %bitcast.19), custom_call_target="tpu_custom_call" | custom-call | tf_op jit(solution)/shard_map/moved_rows/pallas_call | solution.py:400
  81.7 2.1 %append_rows.1 = (bf16[4,128,768]{2,1,0:T(8,128)(2,1)}, s32[4]{0:T(128)}) custom-call(s32[4]{0:T(128)S(1)} %copy-done.5, bf16[256,896]{1,0:T(8,128)(2,1)S(1)} %bitcast.16, bf16[4,128,768]{2,1,0:T(8,128)(2,1)S(1)} %copy-done), custom_call_target="tpu_custom_call" | custom-call | tf_op jit(solution)/shard_map/append_rows/pallas_call | solution.py:450
  83.8 6.1 %all-to-all-done.2 = f32[64,1,128]{2,1,0:T(1,128)S(1)} async-done(((f32[64,1,128]{2,1,0:T(1,128)}), f32[64,1,128]{2,1,0:T(1,128)S(1)}, u32[]{:S(2)}, u32[]{:S(2)}) %all-to-all-start.2) | async-done | bytes 32800 | tf_op jit(solution)/shard_map/all_to_all | solution.py:461
  89.9 0.8 last_step.1
  (12 shorter events, 0.0 us)
Async XLA Ops:
  4.2 35.0 %all-to-all-start = ((bf16[64,8,640]{2,1,0:T(8,128)(2,1)}), bf16[64,8,640]{2,1,0:T(8,128)(2,1)S(1)}, u32[]{:S(2)}, u32[]{:S(2)}) async-start(bf16[64,8,640]{2,1,0:T(8,128)(2,1)} %bitcast.28), calls=%async_computation | async-start | bytes 1310720 | tf_op jit(solution)/shard_map/all_to_all | solution.py:378
  19.0 39.2 %collective-permute-start = (bf16[2048,768]{1,0:T(8,128)(2,1)}, bf16[2048,768]{1,0:T(8,128)(2,1)}, u32[]{:S(2)}, u32[]{:S(2)}) collective-permute-start(bf16[2048,768]{1,0:T(8,128)(2,1)} %own_ref.1), channel_id=1, source_target_pairs={{0,1},{1,0},{2,3},{3,2},{4,5},{5,4},{6,7},{7,6},{8,9},{9,8},{10,11... | collective-permute-start | bytes 9437192 | tf_op jit(solution)/shard_map/ppermute | solution.py:377
  39.6 18.6 %collective-permute-start.1 = (bf16[256,768]{1,0:T(8,128)(2,1)S(1)}, bf16[256,768]{1,0:T(8,128)(2,1)S(1)}, u32[]{:S(2)}, u32[]{:S(2)}) collective-permute-start(bf16[256,768]{1,0:T(8,128)(2,1)S(1)} %share_rows.1.share_ref.v_ref), channel_id=1, source_target_pairs={{0,16},{16,32},{32,48},{48,0},{1,17},{17,33},{33,49},{49,1},{2,18}... | collective-permute-start | bytes 1179656 | tf_op jit(solution)/shard_map/ppermute | solution.py:388
  42.7 15.5 %collective-permute-start.2 = (bf16[256,768]{1,0:T(8,128)(2,1)S(1)}, bf16[256,768]{1,0:T(8,128)(2,1)S(1)}, u32[]{:S(2)}, u32[]{:S(2)}) collective-permute-start(bf16[256,768]{1,0:T(8,128)(2,1)S(1)} %share_rows.1.share_ref.v_ref), channel_id=1, source_target_pairs={{0,48},{16,0},{32,16},{48,32},{1,49},{17,1},{33,17},{49,33},{2,50}... | collective-permute-start | bytes 1179656 | tf_op jit(solution)/shard_map/ppermute | solution.py:388
  47.6 22.9 %all-to-all-start.1 = ((bf16[8,32,896]{2,1,0:T(8,128)(2,1)}), bf16[8,32,896]{2,1,0:T(8,128)(2,1)S(1)}, u32[]{:S(2)}, u32[]{:S(2)}) async-start(bf16[8,32,896]{2,1,0:T(8,128)(2,1)} %spread_rows.1), calls=%async_computation.1 | async-start | bytes 917504 | tf_op jit(solution)/shard_map/all_to_all | solution.py:399
  54.5 13.0 %copy-start = (bf16[4,128,768]{2,1,0:T(8,128)(2,1)S(1)}, bf16[4,128,768]{2,1,0:T(8,128)(2,1)}, u32[]{:S(2)}) copy-start(bf16[4,128,768]{2,1,0:T(8,128)(2,1)} %post_ref.5) | copy-start | bytes 2359300
  54.5 13.0 %collective-permute-start.3 = (bf16[256,768]{1,0:T(8,128)(2,1)S(1)}, bf16[256,768]{1,0:T(8,128)(2,1)S(1)}, u32[]{:S(2)}, u32[]{:S(2)}) collective-permute-start(bf16[256,768]{1,0:T(8,128)(2,1)S(1)} %share_rows.1.share_ref.v_ref), channel_id=1, source_target_pairs={{0,32},{16,48},{32,0},{48,16},{1,33},{17,49},{33,1},{49,17},{2,34}... | collective-permute-start | bytes 1179656 | tf_op jit(solution)/shard_map/ppermute | solution.py:388
  58.2 1.9 %copy-start.9 = (bf16[2048,768]{1,0:T(8,128)(2,1)S(1)}, bf16[2048,768]{1,0:T(8,128)(2,1)}, u32[]{:S(2)}) copy-start(bf16[2048,768]{1,0:T(8,128)(2,1)} %own_ref.1) | copy-start | bytes 9437188
  67.5 3.0 %copy-start.2 = (s32[64]{0:T(128)S(1)}, s32[64]{0:T(128)}, u32[]{:S(2)}) copy-start(s32[64]{0:T(128)} %param.18) | copy-start | bytes 772
  67.5 3.0 %copy-start.3 = (s32[64]{0:T(128)S(1)}, s32[64]{0:T(128)}, u32[]{:S(2)}) copy-start(s32[64]{0:T(128)} %param.19) | copy-start | bytes 772
  67.5 3.0 %copy-start.4 = (s32[64]{0:T(128)S(1)}, s32[64]{0:T(128)}, u32[]{:S(2)}) copy-start(s32[64]{0:T(128)} %param.21) | copy-start | bytes 772
  67.5 3.0 %copy-start.5 = (s32[4]{0:T(128)S(1)}, s32[4]{0:T(128)}, u32[]{:S(2)}) copy-start(s32[4]{0:T(128)} %fill_ref.3) | copy-start | bytes 52
  67.5 3.0 %copy-start.6 = (s32[2,128]{1,0:T(2,128)S(1)}, s32[2,128]{1,0:T(2,128)}, u32[]{:S(2)}) copy-start(s32[2,128]{1,0:T(2,128)} %member_ref.1) | copy-start | bytes 3076
  67.5 3.0 %copy-start.7 = (s32[2]{0:T(128)S(1)}, s32[2]{0:T(128)}, u32[]{:S(2)}) copy-start(s32[2]{0:T(128)} %split_ref.1) | copy-start | bytes 28
  67.5 3.0 %copy-start.8 = (s32[64]{0:T(128)S(1)}, s32[64]{0:T(128)}, u32[]{:S(2)}) copy-start(s32[64]{0:T(128)} %param.20) | copy-start | bytes 772
  70.5 19.4 %copy-start.1 = (bf16[512,128]{1,0:T(8,128)(2,1)S(1)}, bf16[512,128]{1,0:T(8,128)(2,1)}, u32[]{:S(2)}) copy-start(bf16[512,128]{1,0:T(8,128)(2,1)} %get-tuple-element.30.table_ref) | copy-start | bytes 393220
  73.7 16.2 %all-to-all-start.2 = ((f32[64,1,128]{2,1,0:T(1,128)}), f32[64,1,128]{2,1,0:T(1,128)S(1)}, u32[]{:S(2)}, u32[]{:S(2)}) async-start(f32[64,1,128]{2,1,0:T(1,128)} %bitcast.11), calls=%async_computation.2 | async-start | bytes 65536 | tf_op jit(solution)/shard_map/all_to_all | solution.py:461

commit v7 on v6

--- a/solution.py
+++ b/solution.py
@@ -63,7 +63,19 @@
         copy.wait()
 
 
-def pack_kernel(vec_ref, head_ref, assign_ref, npost_ref, nrow_ref, ndest_ref, out_ref, table_ref):
+def pack_kernel(
+    vec_in, post_in, assign_in, npost_in, nrow_in, ndest_in, out_hbm, table_ref,
+    vec_ref, head_ref, assign_ref, npost_ref, nrow_ref, ndest_ref, out_ref, sems,
+):
+    pairs = (
+        (assign_in, assign_ref), (vec_in, vec_ref), (ndest_in, ndest_ref), (npost_in, npost_ref),
+        (nrow_in, nrow_ref), (post_in.at[:, :HEAD, :], head_ref),
+        (out_ref.at[:, :HALF], out_hbm.at[:, :HALF]), (out_ref.at[:, HALF:], out_hbm.at[:, HALF:]),
+    )
+    copies = [pltpu.make_async_copy(src, dst, sems.at[i]) for i, (src, dst) in enumerate(pairs)]
+    for copy in copies[:6]:
+        copy.start()
+    copies[0].wait()
     n = NC * 8
     assign = assign_ref[...]
     dest = assign // POSTS
@@ -93,10 +105,13 @@
     low_half = iota((n, V), 0) % 8 < 4
     table = one_hot(share & low_half)
     table_ref[:, :V] = table
+    copies[1].wait()
     out_ref[:, :HALF] = (
         dot(table, vec_ref[:, :HALF]) + dot(one_hot(share & ~low_half), vec_ref[:, HALF:])
     ).astype(BF)
-
+    copies[6].start()
+    for copy in copies[2:6]:
+        copy.wait()
     ndest = ndest_ref[...]
     nplace = earlier_equal(ndest)
     picks = one_hot(npost_ref[...] * HEAD + nrow_ref[...] == iota((POSTS * HEAD, NB), 0))
@@ -114,6 +129,9 @@
         if t == 0:
             tile = tile + dot(sixth, mark)
         out_ref[:, HALF + 128 * t : HALF + 128 * t + 128] = tile.astype(BF)
+    copies[7].start()
+    copies[6].wait()
+    copies[7].wait()
 
 
 def share_kernel(in_ref, share_ref):
@@ -255,7 +273,25 @@
     return best
 
 
-def first_kernel(own_ref, mate_in, v_ref, v1_in, v2_in, acc_ref, near_ref, mate_ref, part_ref, sems):
+def returned(place_ref, accs, best):
+    x, core = place_ref[0], place_ref[1]
+    wide = (NC, NC * 4)
+    mine = iota(wide, 1) // 4 == iota(wide, 0)
+    lane = iota((NC, 128), 1)
+    for a, acc in accs:
+        top = jnp.max(acc, axis=0, keepdims=True)
+        spread = jnp.where(mine, jnp.broadcast_to(top, wide), LOW)
+        folded = jnp.maximum(spread[:, :128], spread[:, 128:])
+        for shift in (64, 32, 16, 8, 4):
+            folded = jnp.maximum(folded, pltpu.roll(folded, shift, 1))
+        group = lax.rem(x + NX - a, NX) * NK + core
+        best = jnp.where(lane // 4 == group, folded, best)
+    return best
+
+
+def first_kernel(
+    place_ref, own_ref, mate_in, v_ref, v1_in, v2_in, best_ref, near_ref, mate_ref, acc_ref, part_ref, sems
+):
     pairs = ((v1_in, part_ref.at[0]), (v2_in, part_ref.at[1]), (mate_in, mate_ref), (own_ref, near_ref))
     copies = [pltpu.make_async_copy(src, dst, sems.at[i]) for i, (src, dst) in enumerate(pairs)]
     for copy in copies:
@@ -270,30 +306,19 @@
     acc_ref[0] = scan_blocks(mate_ref, v_ref[...], acc_ref[0])
     acc_ref[1] = scan_blocks(mate_ref, part_ref[0], acc_ref[1])
     acc_ref[2] = scan_blocks(mate_ref, part_ref[1], acc_ref[2])
+    blank = jnp.full((NC, 128), LOW, F32)
+    best_ref[...] = returned(place_ref, ((0, acc_ref[0]), (1, acc_ref[1]), (3, acc_ref[2])), blank)
     copies[3].wait()
 
 
 def best_kernel(
-    place_ref, own_ref, mate_ref, v_in, acc_ref, post_ref, out_ref, prior_ref, part_ref, sems
+    place_ref, own_ref, mate_ref, v_in, some_ref, post_ref, out_ref, prior_ref, part_ref, sems
 ):
     fetch([(v_in, part_ref)], sems)
     prior_ref[...] = own_ref[:16, :]
     best = scan_blocks(own_ref, part_ref[...], jnp.full((8, NC * 4), LOW, F32))
-    accs = [acc_ref[0], acc_ref[1], scan_blocks(mate_ref, part_ref[...], best), acc_ref[2]]
-    x, core = place_ref[0], place_ref[1]
-    wide = (NC, NC * 4)
-    mine = iota(wide, 1) // 4 == iota(wide, 0)
-    lane = iota((NC, 128), 1)
-    best = jnp.full((NC, 128), LOW, F32)
-    for a in range(NX):
-        top = jnp.max(accs[a], axis=0, keepdims=True)
-        spread = jnp.where(mine, jnp.broadcast_to(top, wide), LOW)
-        folded = jnp.maximum(spread[:, :128], spread[:, 128:])
-        for shift in (64, 32, 16, 8, 4):
-            folded = jnp.maximum(folded, pltpu.roll(folded, shift, 1))
-        group = lax.rem(x + NX - a, NX) * NK + core
-        best = jnp.where(lane // 4 == group, folded, best)
-    out_ref[...] = best
+    best = scan_blocks(mate_ref, part_ref[...], best)
+    out_ref[...] = returned(place_ref, ((2, best),), some_ref[...])
 
 
 def final_kernel(in_ref, table_ref, best_ref, score_ref):
@@ -367,9 +392,13 @@
             jax.ShapeDtypeStruct((NC * 8, P8), BF),
             jax.ShapeDtypeStruct((NC * 8, 128), BF),
         ),
-        grid=(1,),
-        in_specs=[one(V, D), one(POSTS, HEAD, D), one(1, V), one(1, NB), one(1, NB), one(1, NB)],
-        out_specs=(one(NC * 8, P8), one(NC * 8, 128)),
+        in_specs=[hbm] * 6,
+        out_specs=(hbm, vm()),
+        scratch_shapes=[
+            pltpu.VMEM((V, D), BF), pltpu.VMEM((POSTS, HEAD, D), BF), pltpu.VMEM((1, V), I32),
+            pltpu.VMEM((1, NB), I32), pltpu.VMEM((1, NB), I32), pltpu.VMEM((1, NB), I32),
+            pltpu.VMEM((NC * 8, P8), BF), pltpu.SemaphoreType.DMA((8,)),
+        ],
         compiler_params=params(60),
         name="pack_rows",
     )(vectors, postings, assign.reshape(1, V), npost, nrow, ndest)
@@ -413,17 +442,21 @@
     first, near, mate = pl.pallas_call(
         first_kernel,
         out_shape=(
-            jax.ShapeDtypeStruct((NX - 1, 8, NC * 4), F32),
+            jax.ShapeDtypeStruct((NC, 128), F32),
             jax.ShapeDtypeStruct((2048, D), BF),
             jax.ShapeDtypeStruct((2048, D), BF),
         ),
-        in_specs=[vm(), hbm, vm(), hbm, hbm],
+        in_specs=[sm(), vm(), hbm, vm(), hbm, hbm],
         out_specs=(vm(), vm(), vm()),
-        scratch_shapes=[pltpu.VMEM((2, NC * 4, D), BF), pltpu.SemaphoreType.DMA((4,))],
+        scratch_shapes=[
+            pltpu.VMEM((NX - 1, 8, NC * 4), F32),
+            pltpu.VMEM((2, NC * 4, D), BF),
+            pltpu.SemaphoreType.DMA((4,)),
+        ],
         compiler_params=params(),
         cost_estimate=cost(3),
         name="best_of_three",
-    )(centroids, mate, share, parts[1], parts[3])
+    )(place, centroids, mate, share, parts[1], parts[3])
     best, priors = pl.pallas_call(
         best_kernel,
         out_shape=(jax.ShapeDtypeStruct((NC, 128), F32), jax.ShapeDtypeStruct((16, D), BF)),

time: 91.1 us -> 92.3 us (1.013)
  Pallas kernels: 21.7 us -> 23.2 us
  transfers between devices with their start and end apart: 7 -> 7, of which waited for: 3 -> 3; matrix products, arithmetic and copies ran while one was open for 0% -> 0% of each run, Pallas kernels for 16% -> 17%
where the time goes in v7:
time: 92.3 us; the launch traced here: 91.8 us
  starting transfers between devices  41.6 us (45%)
  waiting for transfers between devices  24.1 us (26%)
  Pallas kernels  23.2 us (25%)
  local copies, waits for them, and re-layouts  1.93 us (2%)
    all_to_all x1, waiting for transfers between devices, shards(): lax.all_to_all(packed.reshape(NC, 8, P8), CENT, 0, 0, tiled=True)  17.8 us
    all_to_all x1, starting transfers between devices, shards(): lax.all_to_all(packed.reshape(NC, 8, P8), CENT, 0, 0, tiled=True)  14.9 us
    ppermute x3, starting transfers between devices, shards(): lax.ppermute(share, 'x', [(i, (i + a) % NX) for i in range(NX)])  10.1 us
    all_to_all x1, starting transfers between devices, shards(): lax.all_to_all(sending.reshape(NC, 1, 128), CENT, 0, 0, tiled=True)  7.4 us
    pallas_call x1, Pallas kernels, shards(): pl.pallas_call(first_kernel, out_shape=(jax.ShapeDtypeStruct((NC, 128), F...  7.2 us
    all_to_all x1, starting transfers between devices, shards(): gathered = lax.all_to_all(spread, 'y', 0, 0, tiled=True).reshape(NY * V, W)  6.83 us
    all_to_all x1, waiting for transfers between devices, shards(): lax.all_to_all(sending.reshape(NC, 1, 128), CENT, 0, 0, tiled=True)  6.13 us
    pallas_call x1, Pallas kernels, shards(): pl.pallas_call(pack_kernel, out_shape=(jax.ShapeDtypeStruct((NC * 8, P8),...  4.19 us
  transfers between devices with their start and end apart: 7, of which 3 were waited for; matrix products, arithmetic and copies ran while one was open for 0% of the time, Pallas kernels for 17%

profile of v7, /device:TPU:1, one launch (start us, length us, event | category | flops | bytes accessed | tf_op | source)
XLA Modules:
  0.0 91.8 jit_solution(17980845103034600802)
XLA Ops:
  0.6 4.2 %pack_rows.1 = (bf16[512,640]{1,0:T(8,128)(2,1)}, bf16[512,128]{1,0:T(8,128)(2,1)}) custom-call(bf16[32,768]{1,0:T(8,128)(2,1)} %vec_in.1, bf16[4,128,768]{2,1,0:T(8,128)(2,1)} %post_ref.5, s32[1,32]{1,0:T(1,128)} %bitcast.29, s32[1,64]{1,0:T(1,128)} %bitcast.21, s32[1,64]{1,0:T(1,128)} %bitcast.23, s32[1,64]{1,0:T(1,128)} %bitcast.25), custom_call_target="tpu_custom_call" | custom-call | tf_op jit(solution)/shard_map/pack_rows/pallas_call | solution.py:389
  4.8 14.9 %all-to-all-start = ((bf16[64,8,640]{2,1,0:T(8,128)(2,1)}), bf16[64,8,640]{2,1,0:T(8,128)(2,1)S(1)}, u32[]{:S(2)}, u32[]{:S(2)}) async-start(bf16[64,8,640]{2,1,0:T(8,128)(2,1)} %bitcast.28), calls=%async_computation | async-start | bytes 1310720 | tf_op jit(solution)/shard_map/all_to_all | solution.py:407
  19.7 2.4 %collective-permute-start = (bf16[2048,768]{1,0:T(8,128)(2,1)}, bf16[2048,768]{1,0:T(8,128)(2,1)}, u32[]{:S(2)}, u32[]{:S(2)}) collective-permute-start(bf16[2048,768]{1,0:T(8,128)(2,1)} %own_ref.1), channel_id=1, source_target_pairs={{0,1},{1,0},{2,3},{3,2},{4,5},{5,4},{6,7},{7,6},{8,9},{9,8},{10,11... | collective-permute-start | bytes 9437192 | tf_op jit(solution)/shard_map/ppermute | solution.py:406
  22.1 17.8 %all-to-all-done = bf16[64,8,640]{2,1,0:T(8,128)(2,1)S(1)} async-done(((bf16[64,8,640]{2,1,0:T(8,128)(2,1)}), bf16[64,8,640]{2,1,0:T(8,128)(2,1)S(1)}, u32[]{:S(2)}, u32[]{:S(2)}) %all-to-all-start) | async-done | bytes 655392 | tf_op jit(solution)/shard_map/all_to_all | solution.py:407
  39.8 0.4 share_rows.1.share_ref.v_ref
  40.2 3.1 %collective-permute-start.1 = (bf16[256,768]{1,0:T(8,128)(2,1)S(1)}, bf16[256,768]{1,0:T(8,128)(2,1)S(1)}, u32[]{:S(2)}, u32[]{:S(2)}) collective-permute-start(bf16[256,768]{1,0:T(8,128)(2,1)S(1)} %share_rows.1.share_ref.v_ref), channel_id=1, source_target_pairs={{0,16},{16,32},{32,48},{48,0},{1,17},{17,33},{33,49},{49,1},{2,18}... | collective-permute-start | bytes 1179656 | tf_op jit(solution)/shard_map/ppermute | solution.py:417
  43.4 3.4 %collective-permute-start.2 = (bf16[256,768]{1,0:T(8,128)(2,1)S(1)}, bf16[256,768]{1,0:T(8,128)(2,1)S(1)}, u32[]{:S(2)}, u32[]{:S(2)}) collective-permute-start(bf16[256,768]{1,0:T(8,128)(2,1)S(1)} %share_rows.1.share_ref.v_ref), channel_id=1, source_target_pairs={{0,48},{16,0},{32,16},{48,32},{1,49},{17,1},{33,17},{49,33},{2,50}... | collective-permute-start | bytes 1179656 | tf_op jit(solution)/shard_map/ppermute | solution.py:417
  46.8 1.5 %spread_rows.1 = bf16[8,32,896]{2,1,0:T(8,128)(2,1)} custom-call(bf16[512,640]{1,0:T(8,128)(2,1)S(1)} %bitcast.18, bf16[256,768]{1,0:T(8,128)(2,1)S(1)} %share_rows.1.share_ref.v_ref), custom_call_target="tpu_custom_call" | custom-call | flops 20000000000 | tf_op jit(solution)/shard_map/spread_rows/pallas_call | solution.py:418
  48.3 6.8 %all-to-all-start.1 = ((bf16[8,32,896]{2,1,0:T(8,128)(2,1)}), bf16[8,32,896]{2,1,0:T(8,128)(2,1)S(1)}, u32[]{:S(2)}, u32[]{:S(2)}) async-start(bf16[8,32,896]{2,1,0:T(8,128)(2,1)} %spread_rows.1), calls=%async_computation.1 | async-start | bytes 917504 | tf_op jit(solution)/shard_map/all_to_all | solution.py:428
  55.1 0.1 pad_add_fusion.place_ref
  55.2 3.7 %collective-permute-start.3 = (bf16[256,768]{1,0:T(8,128)(2,1)S(1)}, bf16[256,768]{1,0:T(8,128)(2,1)S(1)}, u32[]{:S(2)}, u32[]{:S(2)}) collective-permute-start(bf16[256,768]{1,0:T(8,128)(2,1)S(1)} %share_rows.1.share_ref.v_ref), channel_id=1, source_target_pairs={{0,32},{16,48},{32,0},{48,16},{1,33},{17,49},{33,1},{49,17},{2,34}... | collective-permute-start | bytes 1179656 | tf_op jit(solution)/shard_map/ppermute | solution.py:417
  58.8 0.0 collective-permute-done.1.v1_in
  58.9 0.0 collective-permute-done.2.v2_in
  58.9 0.0 collective-permute-done.mate_in
  58.9 0.0 copy-start.9
  58.9 1.9 %copy-done.9 = bf16[2048,768]{1,0:T(8,128)(2,1)S(1)} copy-done((bf16[2048,768]{1,0:T(8,128)(2,1)S(1)}, bf16[2048,768]{1,0:T(8,128)(2,1)}, u32[]{:S(2)}) %copy-start.9) | copy-done | bytes 3145752
  60.8 7.2 %best_of_three.1 = (f32[64,128]{1,0:T(8,128)S(1)}, bf16[2048,768]{1,0:T(8,128)(2,1)S(1)}, bf16[2048,768]{1,0:T(8,128)(2,1)S(1)}) custom-call(s32[2]{0:T(128)S(1)} %pad_add_fusion.place_ref, bf16[2048,768]{1,0:T(8,128)(2,1)S(1)} %copy-done.9, bf16[2048,768]{1,0:T(8,128)(2,1)} %collective-permute-done.mate_in, bf16[256,768]{1,0:T(8,128)(2,1)S(1)} %share_rows.1.share_ref.v_ref, ...), custom_call_target="tpu_custom_call" | custom-call | flops 4831838208 | bytes 6291456 | tf_op jit(solution)/shard_map/best_of_three/pallas_call | solution.py:442
  68.0 0.2 collective-permute-done.3.v_in
  68.2 0.0 copy-start.5
  68.2 0.0 copy-start.6
  68.2 0.0 copy-start.7
  68.2 0.0 copy-start.8
  68.2 2.9 %best_scores.1 = (f32[64,128]{1,0:T(8,128)S(1)}, bf16[16,768]{1,0:T(8,128)(2,1)S(1)}) custom-call(s32[2]{0:T(128)S(1)} %pad_add_fusion.place_ref, bf16[2048,768]{1,0:T(8,128)(2,1)S(1)} %get-tuple-element.24.own_ref, bf16[2048,768]{1,0:T(8,128)(2,1)S(1)} %get-tuple-element.25.mate_ref, bf16[256,768]{1,0:T(8,128)(2,1)S(1)} %collective-permute-done.3.v_in, ...), custom_call_target="tpu_custom_call" | custom-call | flops 1610612736 | bytes 6291456 | tf_op jit(solution)/shard_map/best_scores/pallas_call | solution.py:460
  71.2 0.0 all-to-all-done.1
  71.2 0.0 copy-done.2
  71.2 0.0 copy-done.3
  71.3 3.1 %split_scores.1 = (f32[2,2,768]{2,1,0:T(2,128)}, f32[64,128]{1,0:T(8,128)}) custom-call(s32[4]{0:T(128)S(1)} %copy-done.5, s32[2]{0:T(128)S(1)} %copy-done.7, bf16[256,896]{1,0:T(8,128)(2,1)S(1)} %bitcast.15, s32[2,128]{1,0:T(2,128)S(1)} %copy-done.6, s32[1,64]{1,0:T(1,128)S(1)} %bitcast.22, s32[1,64]{1,0:T(1,128)S(1)} %bitcast.24, s32[1,64]{1,0:T(1,128)S(1)} %bitcast.27, ...), custom_call_target="tpu_custom_call" | custom-call | tf_op jit(solution)/shard_map/split_scores/pallas_call | solution.py:470
  74.3 7.4 %all-to-all-start.2 = ((f32[64,1,128]{2,1,0:T(1,128)}), f32[64,1,128]{2,1,0:T(1,128)S(1)}, u32[]{:S(2)}, u32[]{:S(2)}) async-start(f32[64,1,128]{2,1,0:T(1,128)} %bitcast.11), calls=%async_computation.2 | async-start | bytes 65536 | tf_op jit(solution)/shard_map/all_to_all | solution.py:494
  81.7 1.1 %moved_rows.1 = bf16[128,768]{1,0:T(8,128)(2,1)} custom-call(bf16[512,640]{1,0:T(8,128)(2,1)S(1)} %bitcast.19), custom_call_target="tpu_custom_call" | custom-call | tf_op jit(solution)/shard_map/moved_rows/pallas_call | solution.py:429
  82.8 2.1 %append_rows.1 = (bf16[4,128,768]{2,1,0:T(8,128)(2,1)}, s32[4]{0:T(128)}) custom-call(s32[4]{0:T(128)S(1)} %copy-done.5, bf16[256,896]{1,0:T(8,128)(2,1)S(1)} %bitcast.16, bf16[4,128,768]{2,1,0:T(8,128)(2,1)S(1)} %copy-done), custom_call_target="tpu_custom_call" | custom-call | tf_op jit(solution)/shard_map/append_rows/pallas_call | solution.py:483
  84.9 6.1 %all-to-all-done.2 = f32[64,1,128]{2,1,0:T(1,128)S(1)} async-done(((f32[64,1,128]{2,1,0:T(1,128)}), f32[64,1,128]{2,1,0:T(1,128)S(1)}, u32[]{:S(2)}, u32[]{:S(2)}) %all-to-all-start.2) | async-done | bytes 32800 | tf_op jit(solution)/shard_map/all_to_all | solution.py:494
  91.0 0.8 last_step.1
  (12 shorter events, 0.0 us)
Async XLA Ops:
  4.8 35.0 %all-to-all-start = ((bf16[64,8,640]{2,1,0:T(8,128)(2,1)}), bf16[64,8,640]{2,1,0:T(8,128)(2,1)S(1)}, u32[]{:S(2)}, u32[]{:S(2)}) async-start(bf16[64,8,640]{2,1,0:T(8,128)(2,1)} %bitcast.28), calls=%async_computation | async-start | bytes 1310720 | tf_op jit(solution)/shard_map/all_to_all | solution.py:407
  19.7 39.2 %collective-permute-start = (bf16[2048,768]{1,0:T(8,128)(2,1)}, bf16[2048,768]{1,0:T(8,128)(2,1)}, u32[]{:S(2)}, u32[]{:S(2)}) collective-permute-start(bf16[2048,768]{1,0:T(8,128)(2,1)} %own_ref.1), channel_id=1, source_target_pairs={{0,1},{1,0},{2,3},{3,2},{4,5},{5,4},{6,7},{7,6},{8,9},{9,8},{10,11... | collective-permute-start | bytes 9437192 | tf_op jit(solution)/shard_map/ppermute | solution.py:406
  40.2 18.6 %collective-permute-start.1 = (bf16[256,768]{1,0:T(8,128)(2,1)S(1)}, bf16[256,768]{1,0:T(8,128)(2,1)S(1)}, u32[]{:S(2)}, u32[]{:S(2)}) collective-permute-start(bf16[256,768]{1,0:T(8,128)(2,1)S(1)} %share_rows.1.share_ref.v_ref), channel_id=1, source_target_pairs={{0,16},{16,32},{32,48},{48,0},{1,17},{17,33},{33,49},{49,1},{2,18}... | collective-permute-start | bytes 1179656 | tf_op jit(solution)/shard_map/ppermute | solution.py:417
  43.4 15.5 %collective-permute-start.2 = (bf16[256,768]{1,0:T(8,128)(2,1)S(1)}, bf16[256,768]{1,0:T(8,128)(2,1)S(1)}, u32[]{:S(2)}, u32[]{:S(2)}) collective-permute-start(bf16[256,768]{1,0:T(8,128)(2,1)S(1)} %share_rows.1.share_ref.v_ref), channel_id=1, source_target_pairs={{0,48},{16,0},{32,16},{48,32},{1,49},{17,1},{33,17},{49,33},{2,50}... | collective-permute-start | bytes 1179656 | tf_op jit(solution)/shard_map/ppermute | solution.py:417
  48.3 22.9 %all-to-all-start.1 = ((bf16[8,32,896]{2,1,0:T(8,128)(2,1)}), bf16[8,32,896]{2,1,0:T(8,128)(2,1)S(1)}, u32[]{:S(2)}, u32[]{:S(2)}) async-start(bf16[8,32,896]{2,1,0:T(8,128)(2,1)} %spread_rows.1), calls=%async_computation.1 | async-start | bytes 917504 | tf_op jit(solution)/shard_map/all_to_all | solution.py:428
  55.2 13.0 %copy-start = (bf16[4,128,768]{2,1,0:T(8,128)(2,1)S(1)}, bf16[4,128,768]{2,1,0:T(8,128)(2,1)}, u32[]{:S(2)}) copy-start(bf16[4,128,768]{2,1,0:T(8,128)(2,1)} %post_ref.5) | copy-start | bytes 2359300
  55.2 13.0 %collective-permute-start.3 = (bf16[256,768]{1,0:T(8,128)(2,1)S(1)}, bf16[256,768]{1,0:T(8,128)(2,1)S(1)}, u32[]{:S(2)}, u32[]{:S(2)}) collective-permute-start(bf16[256,768]{1,0:T(8,128)(2,1)S(1)} %share_rows.1.share_ref.v_ref), channel_id=1, source_target_pairs={{0,32},{16,48},{32,0},{48,16},{1,33},{17,49},{33,1},{49,17},{2,34}... | collective-permute-start | bytes 1179656 | tf_op jit(solution)/shard_map/ppermute | solution.py:417
  58.9 1.9 %copy-start.9 = (bf16[2048,768]{1,0:T(8,128)(2,1)S(1)}, bf16[2048,768]{1,0:T(8,128)(2,1)}, u32[]{:S(2)}) copy-start(bf16[2048,768]{1,0:T(8,128)(2,1)} %own_ref.1) | copy-start | bytes 9437188
  68.2 3.0 %copy-start.2 = (s32[64]{0:T(128)S(1)}, s32[64]{0:T(128)}, u32[]{:S(2)}) copy-start(s32[64]{0:T(128)} %param.18) | copy-start | bytes 772
  68.2 3.0 %copy-start.3 = (s32[64]{0:T(128)S(1)}, s32[64]{0:T(128)}, u32[]{:S(2)}) copy-start(s32[64]{0:T(128)} %param.19) | copy-start | bytes 772
  68.2 3.0 %copy-start.4 = (s32[64]{0:T(128)S(1)}, s32[64]{0:T(128)}, u32[]{:S(2)}) copy-start(s32[64]{0:T(128)} %param.21) | copy-start | bytes 772
  68.2 3.0 %copy-start.5 = (s32[4]{0:T(128)S(1)}, s32[4]{0:T(128)}, u32[]{:S(2)}) copy-start(s32[4]{0:T(128)} %fill_ref.3) | copy-start | bytes 52
  68.2 3.0 %copy-start.6 = (s32[2,128]{1,0:T(2,128)S(1)}, s32[2,128]{1,0:T(2,128)}, u32[]{:S(2)}) copy-start(s32[2,128]{1,0:T(2,128)} %member_ref.1) | copy-start | bytes 3076
  68.2 3.0 %copy-start.7 = (s32[2]{0:T(128)S(1)}, s32[2]{0:T(128)}, u32[]{:S(2)}) copy-start(s32[2]{0:T(128)} %split_ref.1) | copy-start | bytes 28
  68.2 3.0 %copy-start.8 = (s32[64]{0:T(128)S(1)}, s32[64]{0:T(128)}, u32[]{:S(2)}) copy-start(s32[64]{0:T(128)} %param.20) | copy-start | bytes 772
  71.2 19.9 %copy-start.1 = (bf16[512,128]{1,0:T(8,128)(2,1)S(1)}, bf16[512,128]{1,0:T(8,128)(2,1)}, u32[]{:S(2)}) copy-start(bf16[512,128]{1,0:T(8,128)(2,1)} %get-tuple-element.30.table_ref) | copy-start | bytes 393220
  74.3 16.7 %all-to-all-start.2 = ((f32[64,1,128]{2,1,0:T(1,128)}), f32[64,1,128]{2,1,0:T(1,128)S(1)}, u32[]{:S(2)}, u32[]{:S(2)}) async-start(f32[64,1,128]{2,1,0:T(1,128)} %bitcast.11), calls=%async_computation.2 | async-start | bytes 65536 | tf_op jit(solution)/shard_map/all_to_all | solution.py:494

commit v8 on v6

--- a/solution.py
+++ b/solution.py
@@ -66,31 +66,31 @@
 def pack_kernel(vec_ref, head_ref, assign_ref, npost_ref, nrow_ref, ndest_ref, out_ref, table_ref):
     n = NC * 8
     assign = assign_ref[...]
-    dest = assign // POSTS
-    zdest = (dest // NK) % NZ
+    dest = assign >> 2
+    zdest = (dest >> 1) & 7
     place = earlier_equal(dest)
 
     ones = jnp.ones((V, 128), BF)
 
     def routed(count, per):
         p = iota((count, V), 0)
-        to, t = p // per, p % 4
-        return (dest == to) & (place == t), (zdest != (to // NK) % NZ)
+        to, t = p >> (3 if per == 8 else 2), p & 3
+        return (dest == to) & (place == t), (zdest != ((to >> 1) & 7))
 
     named, other = routed(n, 8)
     small, _ = routed(NC * 4, 4)
     free = (1.0 - dot(one_hot(small), ones)).astype(BF)
     p, c = iota((n, NC * 4), 0), iota((n, NC * 4), 1)
-    pd, cd = p // 8, c // 4
-    slot = ((pd // (NZ * NK)) * NK + pd % NK) * 4 + p % 4
-    cslot = ((cd // (NZ * NK)) * NK + cd % NK) * 4 + c % 4
-    before = one_hot(((pd // NK) % NZ == (cd // NK) % NZ) & (cslot < slot))
+    pd, cd = p >> 3, c >> 2
+    slot = ((pd >> 4) * NK + (pd & 1)) * 4 + (p & 3)
+    cslot = ((cd >> 4) * NK + (cd & 1)) * 4 + (c & 3)
+    before = one_hot((((pd >> 1) & 7) == ((cd >> 1) & 7)) & (cslot < slot))
     free_rank = dot(before, free)[:, :V]
     upper = one_hot(iota((V, V), 0) < iota((V, V), 1))
     rest_rank = dot(one_hot(other), upper)
     taken = dot(one_hot(named), ones)[:, :V]
     share = named | (other & (taken < 0.5) & (free_rank == rest_rank))
-    low_half = iota((n, V), 0) % 8 < 4
+    low_half = (iota((n, V), 0) & 7) < 4
     table = one_hot(share & low_half)
     table_ref[:, :V] = table
     out_ref[:, :HALF] = (
@@ -102,10 +102,10 @@
     picks = one_hot(npost_ref[...] * HEAD + nrow_ref[...] == iota((POSTS * HEAD, NB), 0))
     head = head_ref[...].reshape(POSTS * HEAD, D)
     p, c = iota((n, 6 * NC), 0), iota((n, 6 * NC), 1)
-    spread = one_hot((p // 8 == c % NC) & (p % 8 == c // NC))
-    post = as_column(assign) % POSTS + 1
+    spread = one_hot(((p >> 3) == (c & 63)) & ((p & 7) == (c >> 6)))
+    post = (as_column(assign) & 3) + 1
     mark = jnp.where(iota((V, 128), 1) == as_column(place), post, 0).astype(F32).astype(BF)
-    sixth = one_hot((iota((n, V), 0) // 8 == dest) & (iota((n, V), 0) % 8 == 6))
+    sixth = one_hot(((iota((n, V), 0) >> 3) == dest) & ((iota((n, V), 0) & 7) == 6))
     for t in range(2):
         chosen = one_hot((ndest == iota((NC, NB), 0)) & (nplace == t))
         rows = dot(dot_nt(chosen, picks).astype(BF), head).astype(BF)
@@ -119,7 +119,7 @@
 def share_kernel(in_ref, share_ref):
     n = NC * 8
     p, i = iota((NC * 4, n), 1), iota((NC * 4, n), 0)
-    first = (i // 4) * 8 + i % 4
+    first = (i >> 2) * 8 + (i & 3)
     rows = in_ref[:, :HALF]
     share_ref[:, :HALF] = dot(one_hot(p == first), rows).astype(BF)
     share_ref[:, HALF:] = dot(one_hot(p == first + 4), rows).astype(BF)
@@ -129,9 +129,9 @@
     n = NC * 8
     tiles = in_ref[:, HALF:]
     p, i = iota((NC * 2, n), 1), iota((NC * 2, n), 0)
-    odd = iota((NC * 2, 128), 0) % 2 == 1
+    odd = (iota((NC * 2, 128), 0) & 1) == 1
     for k in range(6):
-        both = dot(one_hot(p == (i // 2) * 8 + k), tiles)
+        both = dot(one_hot(p == (i >> 1) * 8 + k), tiles)
         moved_ref[:, 128 * k : 128 * k + 128] = jnp.where(odd, both[:, 128:], both[:, :128]).astype(BF)
 
 
@@ -144,13 +144,13 @@
     valid = one_hot(first > 0.5)
     rank = dot(valid, upper).astype(BF)
     m = NC * 4
-    widen = one_hot(iota((NC, m), 0) == iota((NC, m), 1) // 4)
+    widen = one_hot(iota((NC, m), 0) == iota((NC, m), 1) >> 2)
     valid, rank = dot(valid, widen)[:1], dot(rank, widen)[:1].astype(I32)
-    t = iota((V, m), 1) % 4
+    t = iota((V, m), 1) & 3
     hit = one_hot((valid > 0.5) & (t < 2) & (2 * rank + t == iota((V, m), 0)))
-    tall = one_hot(iota((m, NC), 1) == iota((m, NC), 0) // 4)
+    tall = one_hot(iota((m, NC), 1) == iota((m, NC), 0) >> 2)
     lane = iota((m, 128), 1)
-    mine = jnp.where(lane == iota((m, 128), 0) % 4, dot(tall, marks), 0.0)
+    mine = jnp.where(lane == (iota((m, 128), 0) & 3), dot(tall, marks), 0.0)
     post = jnp.sum(mine, axis=1, keepdims=True)
     buf_ref[:, :D] = dot(hit, share_ref[...]).astype(BF)
     buf_ref[:, D:] = dot(hit, jnp.where(lane == 0, post, 0.0).astype(BF)).astype(BF)
@@ -282,7 +282,7 @@
     accs = [acc_ref[0], acc_ref[1], scan_blocks(mate_ref, part_ref[...], best), acc_ref[2]]
     x, core = place_ref[0], place_ref[1]
     wide = (NC, NC * 4)
-    mine = iota(wide, 1) // 4 == iota(wide, 0)
+    mine = (iota(wide, 1) >> 2) == iota(wide, 0)
     lane = iota((NC, 128), 1)
     best = jnp.full((NC, 128), LOW, F32)
     for a in range(NX):
@@ -292,7 +292,7 @@
         for shift in (64, 32, 16, 8, 4):
             folded = jnp.maximum(folded, pltpu.roll(folded, shift, 1))
         group = lax.rem(x + NX - a, NX) * NK + core
-        best = jnp.where(lane // 4 == group, folded, best)
+        best = jnp.where((lane >> 2) == group, folded, best)
     out_ref[...] = best
 
 
@@ -314,7 +314,7 @@
     p = iota((128, 128), 0)
     best = jnp.full((1, V), LOW, F32)
     for x in range(NX):
-        slot = (x * NK + (p // 8) % NK) * 4 + p % 4
+        slot = (x * NK + ((p >> 3) & 1)) * 4 + (p & 3)
         value = jnp.max(jnp.where(iota((128, 128), 1) == slot, tops, LOW), axis=1, keepdims=True)
         table = table_ref[128 * x : 128 * x + 128, :V].astype(F32)
         best = jnp.maximum(best, jnp.max(jnp.where(table > 0.5, value, LOW), axis=0, keepdims=True))

time: 91.1 us -> 91.1 us (level)
  no operation moved by 1% of the time
where the time goes in v8:
time: 91.1 us; the launch traced here: 90.6 us
  starting transfers between devices  41.1 us (45%)
  waiting for transfers between devices  25 us (27%)
  Pallas kernels  21.6 us (24%)
  local copies, waits for them, and re-layouts  1.93 us (2%)
    all_to_all x1, waiting for transfers between devices, shards(): lax.all_to_all(packed.reshape(NC, 8, P8), CENT, 0, 0, tiled=True)  17.8 us
    all_to_all x1, starting transfers between devices, shards(): lax.all_to_all(packed.reshape(NC, 8, P8), CENT, 0, 0, tiled=True)  14.8 us
    ppermute x3, starting transfers between devices, shards(): lax.ppermute(share, 'x', [(i, (i + a) % NX) for i in range(NX)])  10.2 us
    all_to_all x1, starting transfers between devices, shards(): lax.all_to_all(sending.reshape(NC, 1, 128), CENT, 0, 0, tiled=True)  6.96 us
    all_to_all x1, starting transfers between devices, shards(): gathered = lax.all_to_all(spread, 'y', 0, 0, tiled=True).reshape(NY * V, W)  6.82 us
    pallas_call x1, Pallas kernels, shards(): pl.pallas_call(first_kernel, out_shape=(jax.ShapeDtypeStruct((NX - 1, 8,...  6.3 us
    all_to_all x1, waiting for transfers between devices, shards(): lax.all_to_all(sending.reshape(NC, 1, 128), CENT, 0, 0, tiled=True)  6.13 us
    pallas_call x1, Pallas kernels, shards(): pl.pallas_call(pack_kernel, out_shape=(jax.ShapeDtypeStruct((NC * 8, P8),...  3.49 us
  transfers between devices with their start and end apart: 7, of which 3 were waited for; matrix products, arithmetic and copies ran while one was open for 0% of the time, Pallas kernels for 16%

profile of v8, /device:TPU:1, one launch (start us, length us, event | category | flops | bytes accessed | tf_op | source)
XLA Modules:
  0.0 90.6 jit_solution(4132049385081057130)
XLA Ops:
  0.6 3.5 %pack_rows.1 = (bf16[512,640]{1,0:T(8,128)(2,1)}, bf16[512,128]{1,0:T(8,128)(2,1)}) custom-call(bf16[32,768]{1,0:T(8,128)(2,1)} %vec_ref.1, bf16[4,128,768]{2,1,0:T(8,128)(2,1)} %post_ref.5, s32[1,32]{1,0:T(1,128)} %bitcast.29, s32[1,64]{1,0:T(1,128)} %bitcast.21, s32[1,64]{1,0:T(1,128)} %bitcast.23, s32[1,64]{1,0:T(1,128)} %bitcast.25), custom_call_target="tpu_custom_call" | custom-call | tf_op jit(solution)/shard_map/pack_rows/pallas_call | solution.py:364
  4.1 14.8 %all-to-all-start = ((bf16[64,8,640]{2,1,0:T(8,128)(2,1)}), bf16[64,8,640]{2,1,0:T(8,128)(2,1)S(1)}, u32[]{:S(2)}, u32[]{:S(2)}) async-start(bf16[64,8,640]{2,1,0:T(8,128)(2,1)} %bitcast.28), calls=%async_computation | async-start | bytes 1310720 | tf_op jit(solution)/shard_map/all_to_all | solution.py:378
  19.0 2.4 %collective-permute-start = (bf16[2048,768]{1,0:T(8,128)(2,1)}, bf16[2048,768]{1,0:T(8,128)(2,1)}, u32[]{:S(2)}, u32[]{:S(2)}) collective-permute-start(bf16[2048,768]{1,0:T(8,128)(2,1)} %own_ref.1), channel_id=1, source_target_pairs={{0,1},{1,0},{2,3},{3,2},{4,5},{5,4},{6,7},{7,6},{8,9},{9,8},{10,11... | collective-permute-start | bytes 9437192 | tf_op jit(solution)/shard_map/ppermute | solution.py:377
  21.3 17.8 %all-to-all-done = bf16[64,8,640]{2,1,0:T(8,128)(2,1)S(1)} async-done(((bf16[64,8,640]{2,1,0:T(8,128)(2,1)}), bf16[64,8,640]{2,1,0:T(8,128)(2,1)S(1)}, u32[]{:S(2)}, u32[]{:S(2)}) %all-to-all-start) | async-done | bytes 655392 | tf_op jit(solution)/shard_map/all_to_all | solution.py:378
  39.1 0.4 share_rows.1.share_ref.v_ref
  39.5 3.1 %collective-permute-start.1 = (bf16[256,768]{1,0:T(8,128)(2,1)S(1)}, bf16[256,768]{1,0:T(8,128)(2,1)S(1)}, u32[]{:S(2)}, u32[]{:S(2)}) collective-permute-start(bf16[256,768]{1,0:T(8,128)(2,1)S(1)} %share_rows.1.share_ref.v_ref), channel_id=1, source_target_pairs={{0,16},{16,32},{32,48},{48,0},{1,17},{17,33},{33,49},{49,1},{2,18}... | collective-permute-start | bytes 1179656 | tf_op jit(solution)/shard_map/ppermute | solution.py:388
  42.7 3.4 %collective-permute-start.2 = (bf16[256,768]{1,0:T(8,128)(2,1)S(1)}, bf16[256,768]{1,0:T(8,128)(2,1)S(1)}, u32[]{:S(2)}, u32[]{:S(2)}) collective-permute-start(bf16[256,768]{1,0:T(8,128)(2,1)S(1)} %share_rows.1.share_ref.v_ref), channel_id=1, source_target_pairs={{0,48},{16,0},{32,16},{48,32},{1,49},{17,1},{33,17},{49,33},{2,50}... | collective-permute-start | bytes 1179656 | tf_op jit(solution)/shard_map/ppermute | solution.py:388
  46.0 1.5 %spread_rows.1 = bf16[8,32,896]{2,1,0:T(8,128)(2,1)} custom-call(bf16[512,640]{1,0:T(8,128)(2,1)S(1)} %bitcast.18, bf16[256,768]{1,0:T(8,128)(2,1)S(1)} %share_rows.1.share_ref.v_ref), custom_call_target="tpu_custom_call" | custom-call | flops 20000000000 | tf_op jit(solution)/shard_map/spread_rows/pallas_call | solution.py:389
  47.6 6.8 %all-to-all-start.1 = ((bf16[8,32,896]{2,1,0:T(8,128)(2,1)}), bf16[8,32,896]{2,1,0:T(8,128)(2,1)S(1)}, u32[]{:S(2)}, u32[]{:S(2)}) async-start(bf16[8,32,896]{2,1,0:T(8,128)(2,1)} %spread_rows.1), calls=%async_computation.1 | async-start | bytes 917504 | tf_op jit(solution)/shard_map/all_to_all | solution.py:399
  54.4 0.1 pad_add_fusion.place_ref
  54.5 3.7 %collective-permute-start.3 = (bf16[256,768]{1,0:T(8,128)(2,1)S(1)}, bf16[256,768]{1,0:T(8,128)(2,1)S(1)}, u32[]{:S(2)}, u32[]{:S(2)}) collective-permute-start(bf16[256,768]{1,0:T(8,128)(2,1)S(1)} %share_rows.1.share_ref.v_ref), channel_id=1, source_target_pairs={{0,32},{16,48},{32,0},{48,16},{1,33},{17,49},{33,1},{49,17},{2,34}... | collective-permute-start | bytes 1179656 | tf_op jit(solution)/shard_map/ppermute | solution.py:388
  58.1 0.0 collective-permute-done.1.v1_in
  58.1 0.0 collective-permute-done.2.v2_in
  58.1 0.0 collective-permute-done.mate_in
  58.2 0.0 copy-start.9
  58.2 1.9 %copy-done.9 = bf16[2048,768]{1,0:T(8,128)(2,1)S(1)} copy-done((bf16[2048,768]{1,0:T(8,128)(2,1)S(1)}, bf16[2048,768]{1,0:T(8,128)(2,1)}, u32[]{:S(2)}) %copy-start.9) | copy-done | bytes 3145752
  60.0 6.3 %best_of_three.1 = (f32[3,8,256]{2,1,0:T(8,128)S(1)}, bf16[2048,768]{1,0:T(8,128)(2,1)S(1)}, bf16[2048,768]{1,0:T(8,128)(2,1)S(1)}) custom-call(bf16[2048,768]{1,0:T(8,128)(2,1)S(1)} %copy-done.9, bf16[2048,768]{1,0:T(8,128)(2,1)} %collective-permute-done.mate_in, bf16[256,768]{1,0:T(8,128)(2,1)S(1)} %share_rows.1.share_ref.v_ref, ...), custom_call_target="tpu_custom_call" | custom-call | flops 4831838208 | bytes 6291456 | tf_op jit(solution)/shard_map/best_of_three/pallas_call | solution.py:413
  66.4 1.1 %collective-permute-done.3.v_in = bf16[256,768]{1,0:T(8,128)(2,1)S(1)} collective-permute-done((bf16[256,768]{1,0:T(8,128)(2,1)S(1)}, bf16[256,768]{1,0:T(8,128)(2,1)S(1)}, u32[]{:S(2)}, u32[]{:S(2)}) %collective-permute-start.3) | collective-permute-done | bytes 393248 | tf_op jit(solution)/shard_map/ppermute | solution.py:388
  67.5 0.0 copy-start.5
  67.5 0.0 copy-start.6
  67.5 0.0 copy-start.7
  67.5 0.0 copy-start.8
  67.5 2.9 %best_scores.1 = (f32[64,128]{1,0:T(8,128)S(1)}, bf16[16,768]{1,0:T(8,128)(2,1)S(1)}) custom-call(s32[2]{0:T(128)S(1)} %pad_add_fusion.place_ref, bf16[2048,768]{1,0:T(8,128)(2,1)S(1)} %get-tuple-element.24.own_ref, bf16[2048,768]{1,0:T(8,128)(2,1)S(1)} %get-tuple-element.25.mate_ref, bf16[256,768]{1,0:T(8,128)(2,1)S(1)} %collective-permute-done.3.v_in, ...), custom_call_target="tpu_custom_call" | custom-call | flops 1610612736 | bytes 6291456 | tf_op jit(solution)/shard_map/best_scores/pallas_call | solution.py:427
  70.5 0.0 all-to-all-done.1
  70.5 0.0 copy-done.2
  70.5 0.0 copy-done.3
  70.5 3.1 %split_scores.1 = (f32[2,2,768]{2,1,0:T(2,128)}, f32[64,128]{1,0:T(8,128)}) custom-call(s32[4]{0:T(128)S(1)} %copy-done.5, s32[2]{0:T(128)S(1)} %copy-done.7, bf16[256,896]{1,0:T(8,128)(2,1)S(1)} %bitcast.15, s32[2,128]{1,0:T(2,128)S(1)} %copy-done.6, s32[1,64]{1,0:T(1,128)S(1)} %bitcast.22, s32[1,64]{1,0:T(1,128)S(1)} %bitcast.24, s32[1,64]{1,0:T(1,128)S(1)} %bitcast.27, ...), custom_call_target="tpu_custom_call" | custom-call | tf_op jit(solution)/shard_map/split_scores/pallas_call | solution.py:437
  73.6 7.0 %all-to-all-start.2 = ((f32[64,1,128]{2,1,0:T(1,128)}), f32[64,1,128]{2,1,0:T(1,128)S(1)}, u32[]{:S(2)}, u32[]{:S(2)}) async-start(f32[64,1,128]{2,1,0:T(1,128)} %bitcast.11), calls=%async_computation.2 | async-start | bytes 65536 | tf_op jit(solution)/shard_map/all_to_all | solution.py:461
  80.6 1.1 %moved_rows.1 = bf16[128,768]{1,0:T(8,128)(2,1)} custom-call(bf16[512,640]{1,0:T(8,128)(2,1)S(1)} %bitcast.19), custom_call_target="tpu_custom_call" | custom-call | tf_op jit(solution)/shard_map/moved_rows/pallas_call | solution.py:400
  81.7 2.1 %append_rows.1 = (bf16[4,128,768]{2,1,0:T(8,128)(2,1)}, s32[4]{0:T(128)}) custom-call(s32[4]{0:T(128)S(1)} %copy-done.5, bf16[256,896]{1,0:T(8,128)(2,1)S(1)} %bitcast.16, bf16[4,128,768]{2,1,0:T(8,128)(2,1)S(1)} %copy-done), custom_call_target="tpu_custom_call" | custom-call | tf_op jit(solution)/shard_map/append_rows/pallas_call | solution.py:450
  83.7 6.1 %all-to-all-done.2 = f32[64,1,128]{2,1,0:T(1,128)S(1)} async-done(((f32[64,1,128]{2,1,0:T(1,128)}), f32[64,1,128]{2,1,0:T(1,128)S(1)}, u32[]{:S(2)}, u32[]{:S(2)}) %all-to-all-start.2) | async-done | bytes 32800 | tf_op jit(solution)/shard_map/all_to_all | solution.py:461
  89.9 0.8 last_step.1
  (12 shorter events, 0.0 us)
Async XLA Ops:
  4.1 35.0 %all-to-all-start = ((bf16[64,8,640]{2,1,0:T(8,128)(2,1)}), bf16[64,8,640]{2,1,0:T(8,128)(2,1)S(1)}, u32[]{:S(2)}, u32[]{:S(2)}) async-start(bf16[64,8,640]{2,1,0:T(8,128)(2,1)} %bitcast.28), calls=%async_computation | async-start | bytes 1310720 | tf_op jit(solution)/shard_map/all_to_all | solution.py:378
  19.0 39.2 %collective-permute-start = (bf16[2048,768]{1,0:T(8,128)(2,1)}, bf16[2048,768]{1,0:T(8,128)(2,1)}, u32[]{:S(2)}, u32[]{:S(2)}) collective-permute-start(bf16[2048,768]{1,0:T(8,128)(2,1)} %own_ref.1), channel_id=1, source_target_pairs={{0,1},{1,0},{2,3},{3,2},{4,5},{5,4},{6,7},{7,6},{8,9},{9,8},{10,11... | collective-permute-start | bytes 9437192 | tf_op jit(solution)/shard_map/ppermute | solution.py:377
  39.5 18.6 %collective-permute-start.1 = (bf16[256,768]{1,0:T(8,128)(2,1)S(1)}, bf16[256,768]{1,0:T(8,128)(2,1)S(1)}, u32[]{:S(2)}, u32[]{:S(2)}) collective-permute-start(bf16[256,768]{1,0:T(8,128)(2,1)S(1)} %share_rows.1.share_ref.v_ref), channel_id=1, source_target_pairs={{0,16},{16,32},{32,48},{48,0},{1,17},{17,33},{33,49},{49,1},{2,18}... | collective-permute-start | bytes 1179656 | tf_op jit(solution)/shard_map/ppermute | solution.py:388
  42.7 15.5 %collective-permute-start.2 = (bf16[256,768]{1,0:T(8,128)(2,1)S(1)}, bf16[256,768]{1,0:T(8,128)(2,1)S(1)}, u32[]{:S(2)}, u32[]{:S(2)}) collective-permute-start(bf16[256,768]{1,0:T(8,128)(2,1)S(1)} %share_rows.1.share_ref.v_ref), channel_id=1, source_target_pairs={{0,48},{16,0},{32,16},{48,32},{1,49},{17,1},{33,17},{49,33},{2,50}... | collective-permute-start | bytes 1179656 | tf_op jit(solution)/shard_map/ppermute | solution.py:388
  47.6 22.9 %all-to-all-start.1 = ((bf16[8,32,896]{2,1,0:T(8,128)(2,1)}), bf16[8,32,896]{2,1,0:T(8,128)(2,1)S(1)}, u32[]{:S(2)}, u32[]{:S(2)}) async-start(bf16[8,32,896]{2,1,0:T(8,128)(2,1)} %spread_rows.1), calls=%async_computation.1 | async-start | bytes 917504 | tf_op jit(solution)/shard_map/all_to_all | solution.py:399
  54.5 13.0 %copy-start = (bf16[4,128,768]{2,1,0:T(8,128)(2,1)S(1)}, bf16[4,128,768]{2,1,0:T(8,128)(2,1)}, u32[]{:S(2)}) copy-start(bf16[4,128,768]{2,1,0:T(8,128)(2,1)} %post_ref.5) | copy-start | bytes 2359300
  54.5 13.0 %collective-permute-start.3 = (bf16[256,768]{1,0:T(8,128)(2,1)S(1)}, bf16[256,768]{1,0:T(8,128)(2,1)S(1)}, u32[]{:S(2)}, u32[]{:S(2)}) collective-permute-start(bf16[256,768]{1,0:T(8,128)(2,1)S(1)} %share_rows.1.share_ref.v_ref), channel_id=1, source_target_pairs={{0,32},{16,48},{32,0},{48,16},{1,33},{17,49},{33,1},{49,17},{2,34}... | collective-permute-start | bytes 1179656 | tf_op jit(solution)/shard_map/ppermute | solution.py:388
  58.2 1.9 %copy-start.9 = (bf16[2048,768]{1,0:T(8,128)(2,1)S(1)}, bf16[2048,768]{1,0:T(8,128)(2,1)}, u32[]{:S(2)}) copy-start(bf16[2048,768]{1,0:T(8,128)(2,1)} %own_ref.1) | copy-start | bytes 9437188
  67.4 3.0 %copy-start.2 = (s32[64]{0:T(128)S(1)}, s32[64]{0:T(128)}, u32[]{:S(2)}) copy-start(s32[64]{0:T(128)} %param.18) | copy-start | bytes 772
  67.5 3.0 %copy-start.3 = (s32[64]{0:T(128)S(1)}, s32[64]{0:T(128)}, u32[]{:S(2)}) copy-start(s32[64]{0:T(128)} %param.19) | copy-start | bytes 772
  67.5 3.0 %copy-start.4 = (s32[64]{0:T(128)S(1)}, s32[64]{0:T(128)}, u32[]{:S(2)}) copy-start(s32[64]{0:T(128)} %param.21) | copy-start | bytes 772
  67.5 3.0 %copy-start.5 = (s32[4]{0:T(128)S(1)}, s32[4]{0:T(128)}, u32[]{:S(2)}) copy-start(s32[4]{0:T(128)} %fill_ref.3) | copy-start | bytes 52
  67.5 3.0 %copy-start.6 = (s32[2,128]{1,0:T(2,128)S(1)}, s32[2,128]{1,0:T(2,128)}, u32[]{:S(2)}) copy-start(s32[2,128]{1,0:T(2,128)} %member_ref.1) | copy-start | bytes 3076
  67.5 3.0 %copy-start.7 = (s32[2]{0:T(128)S(1)}, s32[2]{0:T(128)}, u32[]{:S(2)}) copy-start(s32[2]{0:T(128)} %split_ref.1) | copy-start | bytes 28
  67.5 3.0 %copy-start.8 = (s32[64]{0:T(128)S(1)}, s32[64]{0:T(128)}, u32[]{:S(2)}) copy-start(s32[64]{0:T(128)} %param.20) | copy-start | bytes 772
  70.4 19.4 %copy-start.1 = (bf16[512,128]{1,0:T(8,128)(2,1)S(1)}, bf16[512,128]{1,0:T(8,128)(2,1)}, u32[]{:S(2)}) copy-start(bf16[512,128]{1,0:T(8,128)(2,1)} %get-tuple-element.30.table_ref) | copy-start | bytes 393220
  73.6 16.3 %all-to-all-start.2 = ((f32[64,1,128]{2,1,0:T(1,128)}), f32[64,1,128]{2,1,0:T(1,128)S(1)}, u32[]{:S(2)}, u32[]{:S(2)}) async-start(f32[64,1,128]{2,1,0:T(1,128)} %bitcast.11), calls=%async_computation.2 | async-start | bytes 65536 | tf_op jit(solution)/shard_map/all_to_all | solution.py:461

commit v9 on v8

--- a/solution.py
+++ b/solution.py
@@ -106,14 +106,16 @@
     post = (as_column(assign) & 3) + 1
     mark = jnp.where(iota((V, 128), 1) == as_column(place), post, 0).astype(F32).astype(BF)
     sixth = one_hot(((iota((n, V), 0) >> 3) == dest) & ((iota((n, V), 0) & 7) == 6))
-    for t in range(2):
-        chosen = one_hot((ndest == iota((NC, NB), 0)) & (nplace == t))
-        rows = dot(dot_nt(chosen, picks).astype(BF), head).astype(BF)
-        stack = jnp.concatenate([rows[:, 128 * k : 128 * k + 128] for k in range(6)], axis=0)
-        tile = dot(spread, stack)
-        if t == 0:
-            tile = tile + dot(sixth, mark)
-        out_ref[:, HALF + 128 * t : HALF + 128 * t + 128] = tile.astype(BF)
+    i = iota((2 * NC, NB), 0)
+    chosen = one_hot((ndest == (i & (NC - 1))) & (nplace == (i >> 6)))
+    rows = dot(dot_nt(chosen, picks).astype(BF), head).astype(BF)
+    stacks = [
+        jnp.concatenate([rows[NC * t : NC * t + NC, 128 * k : 128 * k + 128] for k in range(6)], axis=0)
+        for t in range(2)
+    ]
+    tiles = dot(spread, jnp.concatenate(stacks, axis=1))
+    out_ref[:, HALF : HALF + 128] = (tiles[:, :128] + dot(sixth, mark)).astype(BF)
+    out_ref[:, HALF + 128 :] = tiles[:, 128:].astype(BF)
 
 
 def share_kernel(in_ref, share_ref):

time: 91.1 us -> 90.7 us (level)
  no operation moved by 1% of the time
where the time goes in v9:
time: 90.7 us; the launch traced here: 90.2 us
  starting transfers between devices  41.1 us (45%)
  waiting for transfers between devices  25 us (28%)
  Pallas kernels  21.2 us (23%)
  local copies, waits for them, and re-layouts  1.93 us (2%)
    all_to_all x1, waiting for transfers between devices, shards(): lax.all_to_all(packed.reshape(NC, 8, P8), CENT, 0, 0, tiled=True)  17.8 us
    all_to_all x1, starting transfers between devices, shards(): lax.all_to_all(packed.reshape(NC, 8, P8), CENT, 0, 0, tiled=True)  14.8 us
    ppermute x3, starting transfers between devices, shards(): lax.ppermute(share, 'x', [(i, (i + a) % NX) for i in range(NX)])  10.2 us
    all_to_all x1, starting transfers between devices, shards(): lax.all_to_all(sending.reshape(NC, 1, 128), CENT, 0, 0, tiled=True)  6.95 us
    all_to_all x1, starting transfers between devices, shards(): gathered = lax.all_to_all(spread, 'y', 0, 0, tiled=True).reshape(NY * V, W)  6.83 us
    pallas_call x1, Pallas kernels, shards(): pl.pallas_call(first_kernel, out_shape=(jax.ShapeDtypeStruct((NX - 1, 8,...  6.28 us
    all_to_all x1, waiting for transfers between devices, shards(): lax.all_to_all(sending.reshape(NC, 1, 128), CENT, 0, 0, tiled=True)  6.13 us
    pallas_call x1, Pallas kernels, shards(): pl.pallas_call(pack_kernel, out_shape=(jax.ShapeDtypeStruct((NC * 8, P8),...  3.1 us
  transfers between devices with their start and end apart: 7, of which 3 were waited for; matrix products, arithmetic and copies ran while one was open for 0% of the time, Pallas kernels for 16%

profile of v9, /device:TPU:1, one launch (start us, length us, event | category | flops | bytes accessed | tf_op | source)
XLA Modules:
  0.0 90.2 jit_solution(1132115742935037179)
XLA Ops:
  0.6 3.1 %pack_rows.1 = (bf16[512,640]{1,0:T(8,128)(2,1)}, bf16[512,128]{1,0:T(8,128)(2,1)}) custom-call(bf16[32,768]{1,0:T(8,128)(2,1)} %vec_ref.1, bf16[4,128,768]{2,1,0:T(8,128)(2,1)} %post_ref.5, s32[1,32]{1,0:T(1,128)} %bitcast.29, s32[1,64]{1,0:T(1,128)} %bitcast.21, s32[1,64]{1,0:T(1,128)} %bitcast.23, s32[1,64]{1,0:T(1,128)} %bitcast.25), custom_call_target="tpu_custom_call" | custom-call | tf_op jit(solution)/shard_map/pack_rows/pallas_call | solution.py:366
  3.7 14.8 %all-to-all-start = ((bf16[64,8,640]{2,1,0:T(8,128)(2,1)}), bf16[64,8,640]{2,1,0:T(8,128)(2,1)S(1)}, u32[]{:S(2)}, u32[]{:S(2)}) async-start(bf16[64,8,640]{2,1,0:T(8,128)(2,1)} %bitcast.28), calls=%async_computation | async-start | bytes 1310720 | tf_op jit(solution)/shard_map/all_to_all | solution.py:380
  18.6 2.4 %collective-permute-start = (bf16[2048,768]{1,0:T(8,128)(2,1)}, bf16[2048,768]{1,0:T(8,128)(2,1)}, u32[]{:S(2)}, u32[]{:S(2)}) collective-permute-start(bf16[2048,768]{1,0:T(8,128)(2,1)} %own_ref.1), channel_id=1, source_target_pairs={{0,1},{1,0},{2,3},{3,2},{4,5},{5,4},{6,7},{7,6},{8,9},{9,8},{10,11... | collective-permute-start | bytes 9437192 | tf_op jit(solution)/shard_map/ppermute | solution.py:379
  20.9 17.8 %all-to-all-done = bf16[64,8,640]{2,1,0:T(8,128)(2,1)S(1)} async-done(((bf16[64,8,640]{2,1,0:T(8,128)(2,1)}), bf16[64,8,640]{2,1,0:T(8,128)(2,1)S(1)}, u32[]{:S(2)}, u32[]{:S(2)}) %all-to-all-start) | async-done | bytes 655392 | tf_op jit(solution)/shard_map/all_to_all | solution.py:380
  38.7 0.4 share_rows.1.share_ref.v_ref
  39.1 3.1 %collective-permute-start.1 = (bf16[256,768]{1,0:T(8,128)(2,1)S(1)}, bf16[256,768]{1,0:T(8,128)(2,1)S(1)}, u32[]{:S(2)}, u32[]{:S(2)}) collective-permute-start(bf16[256,768]{1,0:T(8,128)(2,1)S(1)} %share_rows.1.share_ref.v_ref), channel_id=1, source_target_pairs={{0,16},{16,32},{32,48},{48,0},{1,17},{17,33},{33,49},{49,1},{2,18}... | collective-permute-start | bytes 1179656 | tf_op jit(solution)/shard_map/ppermute | solution.py:390
  42.3 3.4 %collective-permute-start.2 = (bf16[256,768]{1,0:T(8,128)(2,1)S(1)}, bf16[256,768]{1,0:T(8,128)(2,1)S(1)}, u32[]{:S(2)}, u32[]{:S(2)}) collective-permute-start(bf16[256,768]{1,0:T(8,128)(2,1)S(1)} %share_rows.1.share_ref.v_ref), channel_id=1, source_target_pairs={{0,48},{16,0},{32,16},{48,32},{1,49},{17,1},{33,17},{49,33},{2,50}... | collective-permute-start | bytes 1179656 | tf_op jit(solution)/shard_map/ppermute | solution.py:390
  45.6 1.5 %spread_rows.1 = bf16[8,32,896]{2,1,0:T(8,128)(2,1)} custom-call(bf16[512,640]{1,0:T(8,128)(2,1)S(1)} %bitcast.18, bf16[256,768]{1,0:T(8,128)(2,1)S(1)} %share_rows.1.share_ref.v_ref), custom_call_target="tpu_custom_call" | custom-call | flops 20000000000 | tf_op jit(solution)/shard_map/spread_rows/pallas_call | solution.py:391
  47.1 6.8 %all-to-all-start.1 = ((bf16[8,32,896]{2,1,0:T(8,128)(2,1)}), bf16[8,32,896]{2,1,0:T(8,128)(2,1)S(1)}, u32[]{:S(2)}, u32[]{:S(2)}) async-start(bf16[8,32,896]{2,1,0:T(8,128)(2,1)} %spread_rows.1), calls=%async_computation.1 | async-start | bytes 917504 | tf_op jit(solution)/shard_map/all_to_all | solution.py:401
  54.0 0.1 pad_add_fusion.place_ref
  54.1 3.7 %collective-permute-start.3 = (bf16[256,768]{1,0:T(8,128)(2,1)S(1)}, bf16[256,768]{1,0:T(8,128)(2,1)S(1)}, u32[]{:S(2)}, u32[]{:S(2)}) collective-permute-start(bf16[256,768]{1,0:T(8,128)(2,1)S(1)} %share_rows.1.share_ref.v_ref), channel_id=1, source_target_pairs={{0,32},{16,48},{32,0},{48,16},{1,33},{17,49},{33,1},{49,17},{2,34}... | collective-permute-start | bytes 1179656 | tf_op jit(solution)/shard_map/ppermute | solution.py:390
  57.7 0.0 collective-permute-done.1.v1_in
  57.7 0.0 collective-permute-done.2.v2_in
  57.7 0.0 collective-permute-done.mate_in
  57.8 0.0 copy-start.9
  57.8 1.9 %copy-done.9 = bf16[2048,768]{1,0:T(8,128)(2,1)S(1)} copy-done((bf16[2048,768]{1,0:T(8,128)(2,1)S(1)}, bf16[2048,768]{1,0:T(8,128)(2,1)}, u32[]{:S(2)}) %copy-start.9) | copy-done | bytes 3145752
  59.6 6.3 %best_of_three.1 = (f32[3,8,256]{2,1,0:T(8,128)S(1)}, bf16[2048,768]{1,0:T(8,128)(2,1)S(1)}, bf16[2048,768]{1,0:T(8,128)(2,1)S(1)}) custom-call(bf16[2048,768]{1,0:T(8,128)(2,1)S(1)} %copy-done.9, bf16[2048,768]{1,0:T(8,128)(2,1)} %collective-permute-done.mate_in, bf16[256,768]{1,0:T(8,128)(2,1)S(1)} %share_rows.1.share_ref.v_ref, ...), custom_call_target="tpu_custom_call" | custom-call | flops 4831838208 | bytes 6291456 | tf_op jit(solution)/shard_map/best_of_three/pallas_call | solution.py:415
  65.9 1.1 %collective-permute-done.3.v_in = bf16[256,768]{1,0:T(8,128)(2,1)S(1)} collective-permute-done((bf16[256,768]{1,0:T(8,128)(2,1)S(1)}, bf16[256,768]{1,0:T(8,128)(2,1)S(1)}, u32[]{:S(2)}, u32[]{:S(2)}) %collective-permute-start.3) | collective-permute-done | bytes 393248 | tf_op jit(solution)/shard_map/ppermute | solution.py:390
  67.0 0.0 copy-done
  67.1 0.0 copy-start.5
  67.1 0.0 copy-start.6
  67.1 0.0 copy-start.7
  67.1 0.0 copy-start.8
  67.1 2.9 %best_scores.1 = (f32[64,128]{1,0:T(8,128)S(1)}, bf16[16,768]{1,0:T(8,128)(2,1)S(1)}) custom-call(s32[2]{0:T(128)S(1)} %pad_add_fusion.place_ref, bf16[2048,768]{1,0:T(8,128)(2,1)S(1)} %get-tuple-element.24.own_ref, bf16[2048,768]{1,0:T(8,128)(2,1)S(1)} %get-tuple-element.25.mate_ref, bf16[256,768]{1,0:T(8,128)(2,1)S(1)} %collective-permute-done.3.v_in, ...), custom_call_target="tpu_custom_call" | custom-call | flops 1610612736 | bytes 6291456 | tf_op jit(solution)/shard_map/best_scores/pallas_call | solution.py:429
  70.0 0.0 copy-start.1
  70.1 0.0 all-to-all-done.1
  70.1 3.1 %split_scores.1 = (f32[2,2,768]{2,1,0:T(2,128)}, f32[64,128]{1,0:T(8,128)}) custom-call(s32[4]{0:T(128)S(1)} %copy-done.5, s32[2]{0:T(128)S(1)} %copy-done.7, bf16[256,896]{1,0:T(8,128)(2,1)S(1)} %bitcast.15, s32[2,128]{1,0:T(2,128)S(1)} %copy-done.6, s32[1,64]{1,0:T(1,128)S(1)} %bitcast.22, s32[1,64]{1,0:T(1,128)S(1)} %bitcast.24, s32[1,64]{1,0:T(1,128)S(1)} %bitcast.27, ...), custom_call_target="tpu_custom_call" | custom-call | tf_op jit(solution)/shard_map/split_scores/pallas_call | solution.py:439
  73.2 7.0 %all-to-all-start.2 = ((f32[64,1,128]{2,1,0:T(1,128)}), f32[64,1,128]{2,1,0:T(1,128)S(1)}, u32[]{:S(2)}, u32[]{:S(2)}) async-start(f32[64,1,128]{2,1,0:T(1,128)} %bitcast.11), calls=%async_computation.2 | async-start | bytes 65536 | tf_op jit(solution)/shard_map/all_to_all | solution.py:463
  80.2 1.1 %moved_rows.1 = bf16[128,768]{1,0:T(8,128)(2,1)} custom-call(bf16[512,640]{1,0:T(8,128)(2,1)S(1)} %bitcast.19), custom_call_target="tpu_custom_call" | custom-call | tf_op jit(solution)/shard_map/moved_rows/pallas_call | solution.py:402
  81.2 2.1 %append_rows.1 = (bf16[4,128,768]{2,1,0:T(8,128)(2,1)}, s32[4]{0:T(128)}) custom-call(s32[4]{0:T(128)S(1)} %copy-done.5, bf16[256,896]{1,0:T(8,128)(2,1)S(1)} %bitcast.16, bf16[4,128,768]{2,1,0:T(8,128)(2,1)S(1)} %copy-done), custom_call_target="tpu_custom_call" | custom-call | tf_op jit(solution)/shard_map/append_rows/pallas_call | solution.py:452
  83.3 6.1 %all-to-all-done.2 = f32[64,1,128]{2,1,0:T(1,128)S(1)} async-done(((f32[64,1,128]{2,1,0:T(1,128)}), f32[64,1,128]{2,1,0:T(1,128)S(1)}, u32[]{:S(2)}, u32[]{:S(2)}) %all-to-all-start.2) | async-done | bytes 32800 | tf_op jit(solution)/shard_map/all_to_all | solution.py:463
  89.5 0.8 last_step.1
  (12 shorter events, 0.0 us)
Async XLA Ops:
  3.7 35.0 %all-to-all-start = ((bf16[64,8,640]{2,1,0:T(8,128)(2,1)}), bf16[64,8,640]{2,1,0:T(8,128)(2,1)S(1)}, u32[]{:S(2)}, u32[]{:S(2)}) async-start(bf16[64,8,640]{2,1,0:T(8,128)(2,1)} %bitcast.28), calls=%async_computation | async-start | bytes 1310720 | tf_op jit(solution)/shard_map/all_to_all | solution.py:380
  18.6 39.2 %collective-permute-start = (bf16[2048,768]{1,0:T(8,128)(2,1)}, bf16[2048,768]{1,0:T(8,128)(2,1)}, u32[]{:S(2)}, u32[]{:S(2)}) collective-permute-start(bf16[2048,768]{1,0:T(8,128)(2,1)} %own_ref.1), channel_id=1, source_target_pairs={{0,1},{1,0},{2,3},{3,2},{4,5},{5,4},{6,7},{7,6},{8,9},{9,8},{10,11... | collective-permute-start | bytes 9437192 | tf_op jit(solution)/shard_map/ppermute | solution.py:379
  39.1 18.6 %collective-permute-start.1 = (bf16[256,768]{1,0:T(8,128)(2,1)S(1)}, bf16[256,768]{1,0:T(8,128)(2,1)S(1)}, u32[]{:S(2)}, u32[]{:S(2)}) collective-permute-start(bf16[256,768]{1,0:T(8,128)(2,1)S(1)} %share_rows.1.share_ref.v_ref), channel_id=1, source_target_pairs={{0,16},{16,32},{32,48},{48,0},{1,17},{17,33},{33,49},{49,1},{2,18}... | collective-permute-start | bytes 1179656 | tf_op jit(solution)/shard_map/ppermute | solution.py:390
  42.3 15.5 %collective-permute-start.2 = (bf16[256,768]{1,0:T(8,128)(2,1)S(1)}, bf16[256,768]{1,0:T(8,128)(2,1)S(1)}, u32[]{:S(2)}, u32[]{:S(2)}) collective-permute-start(bf16[256,768]{1,0:T(8,128)(2,1)S(1)} %share_rows.1.share_ref.v_ref), channel_id=1, source_target_pairs={{0,48},{16,0},{32,16},{48,32},{1,49},{17,1},{33,17},{49,33},{2,50}... | collective-permute-start | bytes 1179656 | tf_op jit(solution)/shard_map/ppermute | solution.py:390
  47.1 22.9 %all-to-all-start.1 = ((bf16[8,32,896]{2,1,0:T(8,128)(2,1)}), bf16[8,32,896]{2,1,0:T(8,128)(2,1)S(1)}, u32[]{:S(2)}, u32[]{:S(2)}) async-start(bf16[8,32,896]{2,1,0:T(8,128)(2,1)} %spread_rows.1), calls=%async_computation.1 | async-start | bytes 917504 | tf_op jit(solution)/shard_map/all_to_all | solution.py:401
  54.0 13.0 %copy-start = (bf16[4,128,768]{2,1,0:T(8,128)(2,1)S(1)}, bf16[4,128,768]{2,1,0:T(8,128)(2,1)}, u32[]{:S(2)}) copy-start(bf16[4,128,768]{2,1,0:T(8,128)(2,1)} %post_ref.5) | copy-start | bytes 2359300
  54.1 13.0 %collective-permute-start.3 = (bf16[256,768]{1,0:T(8,128)(2,1)S(1)}, bf16[256,768]{1,0:T(8,128)(2,1)S(1)}, u32[]{:S(2)}, u32[]{:S(2)}) collective-permute-start(bf16[256,768]{1,0:T(8,128)(2,1)S(1)} %share_rows.1.share_ref.v_ref), channel_id=1, source_target_pairs={{0,32},{16,48},{32,0},{48,16},{1,33},{17,49},{33,1},{49,17},{2,34}... | collective-permute-start | bytes 1179656 | tf_op jit(solution)/shard_map/ppermute | solution.py:390
  57.8 1.9 %copy-start.9 = (bf16[2048,768]{1,0:T(8,128)(2,1)S(1)}, bf16[2048,768]{1,0:T(8,128)(2,1)}, u32[]{:S(2)}) copy-start(bf16[2048,768]{1,0:T(8,128)(2,1)} %own_ref.1) | copy-start | bytes 9437188
  67.0 3.0 %copy-start.2 = (s32[64]{0:T(128)S(1)}, s32[64]{0:T(128)}, u32[]{:S(2)}) copy-start(s32[64]{0:T(128)} %param.18) | copy-start | bytes 772
  67.0 3.0 %copy-start.3 = (s32[64]{0:T(128)S(1)}, s32[64]{0:T(128)}, u32[]{:S(2)}) copy-start(s32[64]{0:T(128)} %param.19) | copy-start | bytes 772
  67.0 3.0 %copy-start.4 = (s32[64]{0:T(128)S(1)}, s32[64]{0:T(128)}, u32[]{:S(2)}) copy-start(s32[64]{0:T(128)} %param.21) | copy-start | bytes 772
  67.1 3.0 %copy-start.5 = (s32[4]{0:T(128)S(1)}, s32[4]{0:T(128)}, u32[]{:S(2)}) copy-start(s32[4]{0:T(128)} %fill_ref.3) | copy-start | bytes 52
  67.1 3.0 %copy-start.6 = (s32[2,128]{1,0:T(2,128)S(1)}, s32[2,128]{1,0:T(2,128)}, u32[]{:S(2)}) copy-start(s32[2,128]{1,0:T(2,128)} %member_ref.1) | copy-start | bytes 3076
  67.1 3.0 %copy-start.7 = (s32[2]{0:T(128)S(1)}, s32[2]{0:T(128)}, u32[]{:S(2)}) copy-start(s32[2]{0:T(128)} %split_ref.1) | copy-start | bytes 28
  67.1 3.0 %copy-start.8 = (s32[64]{0:T(128)S(1)}, s32[64]{0:T(128)}, u32[]{:S(2)}) copy-start(s32[64]{0:T(128)} %param.20) | copy-start | bytes 772
  70.0 19.4 %copy-start.1 = (bf16[512,128]{1,0:T(8,128)(2,1)S(1)}, bf16[512,128]{1,0:T(8,128)(2,1)}, u32[]{:S(2)}) copy-start(bf16[512,128]{1,0:T(8,128)(2,1)} %get-tuple-element.30.table_ref) | copy-start | bytes 393220
  73.2 16.2 %all-to-all-start.2 = ((f32[64,1,128]{2,1,0:T(1,128)}), f32[64,1,128]{2,1,0:T(1,128)S(1)}, u32[]{:S(2)}, u32[]{:S(2)}) async-start(f32[64,1,128]{2,1,0:T(1,128)} %bitcast.11), calls=%async_computation.2 | async-start | bytes 65536 | tf_op jit(solution)/shard_map/all_to_all | solution.py:463
